TPU v7x, 32 devices: a whole 2x2x4 slice. The times are simulated.
32 devices in a mesh: groups: 2 (over y), dp: 4 (over x, core), tensor: 4 (over z).
Axes of the slice: x: 2, y: 2, z: 4, core: 2. Of those that a mesh axis runs over, the one named last changes fastest.
Arguments:
- activations: bfloat16 [8192, 8192], P(('groups', 'dp'), 'tensor'), parts along dimension 0, may hold values from -6 to 6
- output_gradient: bfloat16 [8192, 1024], P(('groups', 'dp'), 'tensor'), parts along dimension 0, may hold values from -6 to 6
- value_weight: bfloat16 [8192, 1024], P('tensor'), may hold values from -0.0625 to 0.0625
- adapter_down_factors: float32 [8, 8192, 128], P(('groups', 'dp'), 'tensor'), parts along dimension 0, may hold values from -0.0625 to 0.0625
- adapter_up_factors: float32 [8, 128, 1024], P(('groups', 'dp'), 'tensor'), parts along dimension 0, may hold values from -0.5 to 0.5
- down_first_moment: float32 [8, 8192, 128], P(('groups', 'dp'), 'tensor'), parts along dimension 0, may hold values from -0.12 to 0.12
- down_second_moment: float32 [8, 8192, 128], P(('groups', 'dp'), 'tensor'), parts along dimension 0, may hold values from 1e-05 to 0.001
- up_first_moment: float32 [8, 128, 1024], P(('groups', 'dp'), 'tensor'), parts along dimension 0, may hold values from -0.12 to 0.12
- up_second_moment: float32 [8, 128, 1024], P(('groups', 'dp'), 'tensor'), parts along dimension 0, may hold values from 1e-05 to 0.001
- block_tenant: int32 [128], P(('groups', 'dp')), parts along dimension 0, may hold values from 0 to 3
- block_live_tokens: int32 [128], P(('groups', 'dp')), parts along dimension 0, may hold values from 1 to 64, as said below
- tenant_storage_slot: int32 [8], P('groups'), parts along dimension 0, may hold values from 0 to 3, each once
- tenant_adapter_rank: int32 [8], P('groups'), parts along dimension 0, may hold values from 8 to 128
Outputs:
- grad_acts: bfloat16 [8192, 8192], P(('groups', 'dp'), 'tensor'), parts along dimension 0
- updated_down_factors: float32 [8, 8192, 128], P(('groups', 'dp'), 'tensor'), parts along dimension 0
- updated_down_first: float32 [8, 8192, 128], P(('groups', 'dp'), 'tensor'), parts along dimension 0
- updated_down_second: float32 [8, 8192, 128], P(('groups', 'dp'), 'tensor'), parts along dimension 0
- updated_up_factors: float32 [8, 128, 1024], P(('groups', 'dp'), 'tensor'), parts along dimension 0
- updated_up_first: float32 [8, 128, 1024], P(('groups', 'dp'), 'tensor'), parts along dimension 0
- updated_up_second: float32 [8, 128, 1024], P(('groups', 'dp'), 'tensor'), parts along dimension 0
There are 2 independent parts, one for each index of `groups`. A program takes and returns all parts, laid end to end along the dimension named above; an argument that names none is the same for every part. Nothing has to cross between parts.
Inputs may be any that keep to these rules, and one draw needn't show every extreme that they name: `block_live_tokens`: among the 16 blocks of each index of dp at least one is live in all 64 slots.
All inputs are finite; a program needn't handle non-finite values.
Results may differ from a plain program's by a relative error of at most 0.012.
Values may be sent and summed in bfloat16 or wider, within the bound.
No kernel may reach another device: no remote copies, remote signals or barrier semaphores. Data moves between devices by JAX's collectives and lax.ppermute only.
A program may use at most 128 MiB of HBM per device.

v0:
```python
import jax
import jax.numpy as jnp
from jax import lax
from jax.sharding import PartitionSpec as P

highest = lax.Precision.HIGHEST
adapter_alpha_scale = 16.0
beta_one = 0.9
beta_two = 0.999
adam_eps = 1e-08
learn_rate = 0.001
adam_step = 10


def moment_update_rule(param, first, second, grad):
    new_first = beta_one * first + (1.0 - beta_one) * grad
    new_second = beta_two * second + (1.0 - beta_two) * grad * grad
    fixed_first = new_first / (1.0 - beta_one**adam_step)
    fixed_second = new_second / (1.0 - beta_two**adam_step)
    return (
        param - learn_rate * fixed_first / (jnp.sqrt(fixed_second) + adam_eps),
        new_first,
        new_second,
    )


def shards(
    activations,
    output_gradient,
    value_weight,
    adapter_down_factors,
    adapter_up_factors,
    down_first_moment,
    down_second_moment,
    up_first_moment,
    up_second_moment,
    block_tenant,
    block_live_tokens,
    tenant_storage_slot,
    tenant_adapter_rank,
):
    tok_rows, width_part = activations.shape
    blk_dev = block_tenant.shape[0]
    blk_len = tok_rows // blk_dev
    tenants = tenant_storage_slot.shape[0]
    tenants_per_device = adapter_down_factors.shape[0]
    largest_adapter_rank = adapter_down_factors.shape[2]
    rank_portion = adapter_up_factors.shape[1]
    value_output_width = adapter_up_factors.shape[2]
    tensor_pos = lax.axis_index("tensor")
    replica_pos = lax.axis_index("dp")
    tenant_ids = jnp.arange(tenants, dtype=jnp.int32)
    matches = block_tenant[:, None] == tenant_ids[None, :]
    slot_of = jnp.sum(jnp.where(matches, tenant_storage_slot[None, :], 0), axis=1)
    block_rank_lookup = jnp.sum(jnp.where(matches, tenant_adapter_rank[None, :], 0), axis=1)
    tenant_scales = adapter_alpha_scale / block_rank_lookup.astype(jnp.float32)
    col_live = (
        jnp.arange(largest_adapter_rank, dtype=jnp.int32)[None, :] < block_rank_lookup[:, None]
    )
    own_ranks = tensor_pos * rank_portion + jnp.arange(rank_portion, dtype=jnp.int32)
    rank_rows_live = own_ranks[None, :] < block_rank_lookup[:, None]
    token_live = jnp.arange(blk_len, dtype=jnp.int32)[None, :] < block_live_tokens[:, None]
    slot_match = slot_of[:, None] == tenant_ids[None, :]
    down_factor_half = adapter_down_factors.astype(jnp.bfloat16)
    up_factor_half = adapter_up_factors.astype(jnp.bfloat16)
    zero_half = jnp.zeros((), jnp.bfloat16)
    every_a, every_b = (
        lax.all_gather(down_factor_half, "dp", axis=0, tiled=True),
        lax.all_gather(up_factor_half, "dp", axis=0, tiled=True),
    )
    chosen = slot_match.astype(jnp.bfloat16)
    picked_a = jnp.einsum(
        "bt,tdr->bdr", chosen, every_a, preferred_element_type=jnp.float32
    ).astype(jnp.bfloat16)
    picked_b = jnp.einsum(
        "bt,trk->brk", chosen, every_b, preferred_element_type=jnp.float32
    ).astype(jnp.bfloat16)
    used_a = jnp.where(col_live[:, None, :], picked_a, zero_half)
    used_b = jnp.where(rank_rows_live[:, :, None], picked_b, zero_half)
    cot_full = lax.all_gather(output_gradient, "tensor", axis=1, tiled=True)
    cotangent = jnp.where(
        token_live[:, :, None], cot_full.reshape(blk_dev, blk_len, value_output_width), zero_half
    )
    x_blocks = activations.reshape(blk_dev, blk_len, width_part)
    hidden_part = jnp.einsum(
        "bpd,bdr->bpr", x_blocks, used_a, preferred_element_type=jnp.float32
    ).reshape(tok_rows, largest_adapter_rank)
    hidden_own = (
        lax.psum_scatter(
            hidden_part.astype(jnp.bfloat16), "tensor", scatter_dimension=1, tiled=True
        )
        .astype(jnp.float32)
        .reshape(blk_dev, blk_len, rank_portion)
    )
    upward = jnp.einsum("bpk,brk->bpr", cotangent, used_b, preferred_element_type=jnp.float32)
    scaled_u = (
        (upward * tenant_scales[:, None, None]).astype(jnp.bfloat16).reshape(tok_rows, rank_portion)
    )
    scaled_h = (hidden_own * tenant_scales[:, None, None]).astype(jnp.bfloat16)
    full_u = lax.all_gather(scaled_u, "tensor", axis=1, tiled=True).reshape(
        blk_dev, blk_len, largest_adapter_rank
    )
    base = lax.dot_general(
        cotangent.reshape(tok_rows, value_output_width),
        value_weight,
        (((1,), (1,)), ((), ())),
        preferred_element_type=jnp.float32,
    )
    adapter = jnp.einsum(
        "bpr,bdr->bpd", full_u, used_a, preferred_element_type=jnp.float32
    ).reshape(tok_rows, width_part)
    grad_acts = (base + adapter).astype(jnp.bfloat16)
    local_counts = jnp.sum(jnp.where(matches, block_live_tokens[:, None], 0), axis=0).astype(
        jnp.float32
    )
    all_counts = lax.psum(local_counts, "dp")
    block_a = jnp.einsum("bpd,bpr->bdr", x_blocks, full_u, preferred_element_type=jnp.float32)
    block_b = jnp.einsum("bpr,bpk->brk", scaled_h, cotangent, preferred_element_type=jnp.float32)
    hit_float = slot_match.astype(jnp.float32)
    part_b = jnp.einsum("bt,brk->trk", hit_float, block_b, precision=highest)
    part_a = jnp.einsum("bt,bdr->tdr", hit_float, block_a, precision=highest)
    sum_a, sum_b = (
        lax.psum_scatter(part_a.astype(jnp.bfloat16), "dp", scatter_dimension=0, tiled=True).astype(
            jnp.float32
        ),
        lax.psum_scatter(part_b.astype(jnp.bfloat16), "dp", scatter_dimension=0, tiled=True).astype(
            jnp.float32
        ),
    )
    own_slots = replica_pos * tenants_per_device + jnp.arange(tenants_per_device, dtype=jnp.int32)
    count_own = jnp.sum(
        jnp.where(
            tenant_storage_slot[None, :] == own_slots[:, None],
            all_counts[None, :],
            jnp.float32(0.0),
        ),
        axis=1,
    )
    denom = jnp.maximum(count_own, 1.0)
    down_factor_gradient = sum_a / denom[:, None, None]
    up_factor_gradient = sum_b / denom[:, None, None]
    updated_down_factors, updated_down_first, updated_down_second = moment_update_rule(
        adapter_down_factors, down_first_moment, down_second_moment, down_factor_gradient
    )
    updated_up_factors, updated_up_first, updated_up_second = moment_update_rule(
        adapter_up_factors, up_first_moment, up_second_moment, up_factor_gradient
    )
    return (
        grad_acts,
        updated_down_factors,
        updated_down_first,
        updated_down_second,
        updated_up_factors,
        updated_up_first,
        updated_up_second,
    )


def solution(mesh):
    placed = (
        P(("groups", "dp"), "tensor"),
        P(("groups", "dp"), "tensor"),
        P("tensor", None),
        P(("groups", "dp"), "tensor", None),
        P(("groups", "dp"), "tensor", None),
        P(("groups", "dp"), "tensor", None),
        P(("groups", "dp"), "tensor", None),
        P(("groups", "dp"), "tensor", None),
        P(("groups", "dp"), "tensor", None),
        P(("groups", "dp")),
        P(("groups", "dp")),
        P("groups"),
        P("groups"),
    )
    return jax.shard_map(
        shards,
        mesh=mesh,
        in_specs=placed,
        out_specs=(
            P(("groups", "dp"), "tensor"),
            P(("groups", "dp"), "tensor", None),
            P(("groups", "dp"), "tensor", None),
            P(("groups", "dp"), "tensor", None),
            P(("groups", "dp"), "tensor", None),
            P(("groups", "dp"), "tensor", None),
            P(("groups", "dp"), "tensor", None),
        ),
        check_vma=False,
    )
```

profile of v0, /device:TPU:0, one launch (start us, length us, event | category | flops | bytes accessed | tf_op | source)
XLA Modules:
  0.0 232.7 jit_solution(16383564067284143929)
XLA Ops:
  7.2 0.7 all-gather.3.cloned.1.call-update
  7.9 0.9 convert_element_type.55
  8.9 7.2 %all_gather.13 = bf16[4,32,1024]{2,1,0:T(8,128)(2,1)S(1)} all-gather(bf16[1,32,1024]{2,1,0:T(8,128)(2,1)S(1)} %convert_element_type.55), channel_id=1, replica_groups=mesh['groups'=2,'dp'=4,'tensor'=4] {'dp'}, dimensions={0}, use_global_device_ids=true | all-gather | bytes 327680 | tf_op jit(solution)/shard_map/all_gather | solution.py:69
  16.1 0.9 select_reduce_fusion
  17.0 0.7 iota_compare_fusion.1
  17.8 0.5 fusion.12
  18.3 41.9 %all-gather.3.cloned.1.call-done = bf16[1024,1024]{1,0:T(8,128)(2,1)} async-done(((bf16[1024,256]{1,0:T(8,128)(2,1)}), bf16[1024,1024]{1,0:T(8,128)(2,1)}) %all-gather.3.cloned.1.call-update) | async-done | bytes 2097168 | tf_op jit(solution)/shard_map/all_gather | solution.py:80
  60.2 2.5 %fusion.20 = bf16[16,64,32]{1,2,0:T(8,128)(2,1)S(1)} fusion(bf16[16,64,1024]{2,1,0:T(8,128)(2,1)} %bitcast.32, pred[16,64]{1,0:T(8,128)(4,1)S(1)} %iota_compare_fusion.1, bf16[16,32,1024]{2,0,1:T(8,128)(2,1)S(1)} %fusion.12, f32[16]{0:T(128)S(1)} %convert_divide_fusion.2), kind=kOutput, calls=%fused_computation.23 | convolution fusion | flops 68222976 | bytes 3212352 | tf_op jit(solution)/shard_map/bpk,brk->bpr/dot_general | solution.py:95
  63.0 14.3 %all_gather.14 = bf16[1024,128]{0,1:T(8,128)(2,1)S(1)} all-gather(bf16[1024,32]{0,1:T(8,128)(2,1)S(1)} %reshape.132), channel_id=1, replica_groups=mesh['groups'=2,'dp'=4,'tensor'=4] {'tensor'}, dimensions={1}, use_global_device_ids=true | all-gather | bytes 327680 | tf_op jit(solution)/shard_map/all_gather | solution.py:100
  77.5 10.3 %convolution_bitcast_fusion = f32[16,2048,128]{1,2,0:T(8,128)} fusion(bf16[16,64,128]{2,1,0:T(8,128)(2,1)S(1)} %bitcast.30, bf16[16,64,2048]{2,1,0:T(8,128)(2,1)} %bitcast.28), kind=kOutput, calls=%fused_computation.7 | convolution fusion | flops 536870912 | bytes 21233664 | tf_op jit(solution)/shard_map/bpd,bpr->bdr/dot_general | solution.py:117
  87.7 17.7 %copy.81 = f32[16,2048,128]{2,0,1:T(8,128)} copy(f32[16,2048,128]{1,2,0:T(8,128)} %convolution_bitcast_fusion) | data formatting | bytes 33554432 | tf_op jit(solution)/shard_map/bpd,bpr->bdr/dot_general | solution.py:117
  105.4 10.1 %convolution_convert_fusion = bf16[4,2048,128]{2,0,1:T(4,128)(2,1)S(1)} fusion(f32[16,2048,128]{2,0,1:T(8,128)} %copy.81, s32[16]{0:T(128)S(1)} %get-tuple-element.22), kind=kOutput, calls=%fused_computation.14 | convolution fusion | flops 202375232 | bytes 18874432 | tf_op jit(solution)/shard_map/bt,bdr->tdr/dot_general | solution.py:121
  115.6 1.6 copy.82
  117.2 5.8 %psum.7 = f32[4]{0:T(128)S(1)} all-reduce(f32[4]{0:T(128)S(1)} %convert_element_type.64), channel_id=1, replica_groups=mesh['groups'=2,'dp'=4,'tensor'=4] {'dp'}, use_global_device_ids=true, to_apply=%region_4.5 | all-reduce | flops 4 | bytes 32 | tf_op jit(solution)/shard_map/psum | solution.py:116
  123.0 0.6 fusion.32
  124.3 21.2 %reduce-scatter.4.cloned.1.call-done = bf16[1,2048,128]{2,1,0:T(8,128)(2,1)} async-done(((bf16[4,2048,128]{2,1,0:T(8,128)(2,1)}), bf16[1,2048,128]{2,1,0:T(8,128)(2,1)}) %reduce-scatter.4.cloned.1.call-update) | async-done | bytes 524304 | tf_op jit(solution)/shard_map/reduce_scatter | solution.py:123
  145.5 3.3 %divide_subtract_fusion = (f32[1,2048,128]{2,1,0:T(8,128)}, f32[1,2048,128]{2,1,0:T(8,128)}, f32[1,2048,128]{2,1,0:T(8,128)}, bf16[1,2048,128]{2,1,0:T(8,128)(2,1)}) fusion(f32[1,2048,128]{2,1,0:T(8,128)S(1)} %copy-done.3, f32[]{:T(128)S(6)} %max.4, bf16[1,2048,128]{2,1,0:T(8,128)(2,1)} %reduce-scatter.4.cloned.1.call-done, ...), kind=kLoop, calls=%fused_computation.26 | loop fusion | flops 3932160 | bytes 7340036 | tf_op jit(solution)/shard_map/sub | solution.py:21
  148.8 0.2 reduce-scatter.6.cloned.1.call-start
  149.2 22.4 %all-gather.5.cloned.1.call-done = bf16[4,2048,128]{2,1,0:T(8,128)(2,1)} async-done(((bf16[1,2048,128]{2,1,0:T(8,128)(2,1)}), bf16[4,2048,128]{2,1,0:T(8,128)(2,1)}) %all-gather.5.cloned.1.call-update) | async-done | bytes 2097168 | tf_op jit(solution)/shard_map/all_gather | solution.py:68
  171.6 4.5 %convert_select_fusion = bf16[16,2048,128]{2,0,1:T(8,128)(2,1)S(1)} fusion(pred[16,128]{1,0:T(8,128)(4,1)S(1)} %iota_compare_fusion, bf16[4,2048,128]{2,1,0:T(8,128)(2,1)} %all-gather.5.cloned.1.call-done, s32[16]{0:T(128)S(1)} %get-tuple-element.22), kind=kOutput, calls=%fused_computation.2 | convolution fusion | flops 41943104 | bytes 10487872 | tf_op jit(solution)/shard_map/bt,tdr->bdr/dot_general | solution.py:72
  176.1 5.0 %fusion.13 = bf16[16,128,64]{1,2,0:T(8,128)(2,1)S(1)} fusion(bf16[16,64,2048]{2,1,0:T(8,128)(2,1)S(1)} %bitcast.29, bf16[16,2048,128]{2,0,1:T(8,128)(2,1)S(1)} %convert_select_fusion), kind=kOutput, calls=%fused_computation.20 | convolution fusion | flops 537001984 | bytes 12845056 | tf_op jit(solution)/shard_map/bpd,bdr->bpr/dot_general | solution.py:85
  181.1 0.9 copy.84
  181.9 0.3 reduce-scatter.8.cloned.1.call-start
  182.2 11.9 %fusion.3 = f32[16,64,2048]{2,1,0:T(8,128)} fusion(bf16[16,64,128]{2,1,0:T(8,128)(2,1)S(1)} %bitcast.31, bf16[16,2048,128]{2,0,1:T(8,128)(2,1)} %copy-done.1), kind=kOutput, calls=%fused_computation.5 | convolution fusion | flops 536870912 | bytes 17039360 | tf_op jit(solution)/shard_map/bpr,bdr->bpd/dot_general | solution.py:109
  194.1 7.6 %reduce-scatter.6.cloned.1.call-done = bf16[1024,32]{0,1:T(8,128)(2,1)} async-done(((bf16[1024,128]{0,1:T(8,128)(2,1)}), bf16[1024,32]{0,1:T(8,128)(2,1)}) %reduce-scatter.6.cloned.1.call-update) | async-done | bytes 65552 | tf_op jit(solution)/shard_map/reduce_scatter | solution.py:89
  201.8 1.0 reshape.139
  202.7 0.5 fusion.10
  203.3 2.0 fusion.16
  205.2 0.8 copy.87
  206.1 9.9 %fusion = bf16[1024,2048]{1,0:T(8,128)(2,1)} fusion(f32[16,64,2048]{2,1,0:T(8,128)} %fusion.3, bf16[2048,1024]{1,0:T(8,128)(2,1)} %param.15, bf16[1024,1024]{1,0:T(8,128)(2,1)S(1)} %copy-done.2, pred[1024]{0:T(1024)(128)(4,1)S(1)} %lt.58), kind=kOutput, calls=%fused_computation.1 | convolution fusion | flops 4300210176 | bytes 18875392 | tf_op jit(solution)/shard_map/dot_general | solution.py:103
  216.0 8.5 %reduce-scatter.8.cloned.1.call-done = bf16[1,32,1024]{2,1,0:T(8,128)(2,1)} async-done(((bf16[4,32,1024]{2,1,0:T(8,128)(2,1)}), bf16[1,32,1024]{2,1,0:T(8,128)(2,1)}) %reduce-scatter.8.cloned.1.call-update) | async-done | bytes 65552 | tf_op jit(solution)/shard_map/reduce_scatter | solution.py:126
  224.5 1.6 divide_subtract_fusion.1
  (36 shorter events, 0.9 us)
Async XLA Ops:
  7.2 53.1 %all-gather.3.cloned.1.call-start = ((), (), s32[]{:S(2)}) async-start(), calls=%async_computation.3 | async-start | bytes 2621440 | tf_op jit(solution)/shard_map/all_gather | solution.py:80
  7.9 137.6 %reduce-scatter.4.cloned.1.call-start = ((), (), s32[]{:S(2)}) async-start(), calls=%async_computation.5 | async-start | bytes 2621440 | tf_op jit(solution)/shard_map/reduce_scatter | solution.py:123
  115.5 7.5 %copy-start.9 = (s32[4]{0:T(128)S(1)}, s32[4]{0:T(128)}, u32[]{:S(2)}) copy-start(s32[4]{0:T(128)} %param.24) | copy-start | bytes 52
  115.5 30.0 %copy-start.3 = (f32[1,2048,128]{2,1,0:T(8,128)S(1)}, f32[1,2048,128]{2,1,0:T(8,128)}, u32[]{:S(2)}) copy-start(f32[1,2048,128]{2,1,0:T(8,128)} %param.16) | copy-start | bytes 3145732
  115.5 29.9 %copy-start.4 = (f32[1,2048,128]{2,1,0:T(8,128)S(1)}, f32[1,2048,128]{2,1,0:T(8,128)}, u32[]{:S(2)}) copy-start(f32[1,2048,128]{2,1,0:T(8,128)} %param.18) | copy-start | bytes 3145732
  115.6 29.9 %copy-start.5 = (f32[1,2048,128]{2,1,0:T(8,128)S(1)}, f32[1,2048,128]{2,1,0:T(8,128)}, u32[]{:S(2)}) copy-start(f32[1,2048,128]{2,1,0:T(8,128)} %param.19) | copy-start | bytes 3145732
  117.2 54.4 %all-gather.5.cloned.1.call-start = ((), (), s32[]{:S(2)}) async-start(), calls=%async_computation.4 | async-start | bytes 2621440 | tf_op jit(solution)/shard_map/all_gather | solution.py:68
  148.8 52.9 %reduce-scatter.6.cloned.1.call-start = ((), (), s32[]{:S(2)}) async-start(), calls=%async_computation.6 | async-start | bytes 327680 | tf_op jit(solution)/shard_map/reduce_scatter | solution.py:89
  171.6 4.5 %copy-start = (bf16[1024,2048]{1,0:T(8,128)(2,1)S(1)}, bf16[1024,2048]{1,0:T(8,128)(2,1)}, u32[]{:S(2)}) copy-start(bf16[1024,2048]{1,0:T(8,128)(2,1)} %param.13) | copy-start | bytes 12582916
  176.1 5.0 %copy-start.1 = (bf16[16,2048,128]{2,0,1:T(8,128)(2,1)}, bf16[16,2048,128]{2,0,1:T(8,128)(2,1)S(1)}, u32[]{:S(2)}) copy-start(bf16[16,2048,128]{2,0,1:T(8,128)(2,1)S(1)} %convert_select_fusion) | copy-start | bytes 25165828
  181.9 20.8 %copy-start.2 = (bf16[1024,1024]{1,0:T(8,128)(2,1)S(1)}, bf16[1024,1024]{1,0:T(8,128)(2,1)}, u32[]{:S(2)}) copy-start(bf16[1024,1024]{1,0:T(8,128)(2,1)} %all-gather.3.cloned.1.call-done) | copy-start | bytes 6291460
  181.9 42.5 %reduce-scatter.8.cloned.1.call-start = ((), (), s32[]{:S(2)}) async-start(), calls=%async_computation.7 | async-start | bytes 327680 | tf_op jit(solution)/shard_map/reduce_scatter | solution.py:126
  206.1 18.4 %copy-start.6 = (f32[1,32,1024]{2,1,0:T(8,128)S(1)}, f32[1,32,1024]{2,1,0:T(8,128)}, u32[]{:S(2)}) copy-start(f32[1,32,1024]{2,1,0:T(8,128)} %param.17) | copy-start | bytes 393220
  206.1 18.4 %copy-start.7 = (f32[1,32,1024]{2,1,0:T(8,128)S(1)}, f32[1,32,1024]{2,1,0:T(8,128)}, u32[]{:S(2)}) copy-start(f32[1,32,1024]{2,1,0:T(8,128)} %param.20) | copy-start | bytes 393220
  206.1 18.4 %copy-start.8 = (f32[1,32,1024]{2,1,0:T(8,128)S(1)}, f32[1,32,1024]{2,1,0:T(8,128)}, u32[]{:S(2)}) copy-start(f32[1,32,1024]{2,1,0:T(8,128)} %param.21) | copy-start | bytes 393220
Sparse Core Ops, SparseCore 0:
  9.6 50.6 all-gather.2
  117.3 28.1 reduce-scatter.3
  149.0 22.5 all-gather.4
  182.1 19.6 reduce-scatter.5
  206.2 18.2 reduce-scatter.7
where the time goes:
time: 233 us
  waiting for transfers between devices  102 us (44%)
  matrix products  57.1 us (25%)
  blocking collectives  27.3 us (12%)
  local copies, waits for them, and re-layouts  22.4 us (10%)
  between operations  14.6 us (6%)
  other arithmetic  8.26 us (4%)
    all_gather x1, waiting for transfers between devices, shards(): cot_full = lax.all_gather(output_gradient, 'tensor', axis=1, tiled=True)  41.9 us
    all_gather x1, waiting for transfers between devices, shards(): lax.all_gather(down_factor_half, 'dp', axis=0, tiled=True)  22.4 us
    reduce_scatter x1, waiting for transfers between devices, shards(): lax.psum_scatter(part_a.astype(jnp.bfloat16), 'dp', scatter_dimension=0,...  21.2 us
    dot_general x1, local copies, waits for them, and re-layouts, shards(): jnp.einsum('bpd,bpr->bdr', x_blocks, full_u, preferred_element_type=jnp.f...  17.7 us
    all_gather x1, blocking collectives, shards(): lax.all_gather(scaled_u, 'tensor', axis=1, tiled=True)  14.3 us
    dot_general x1, matrix products, shards(): jnp.einsum('bpr,bdr->bpd', full_u, used_a, preferred_element_type=jnp.flo...  11.9 us
    dot_general x1, matrix products, shards(): jnp.einsum('bpd,bpr->bdr', x_blocks, full_u, preferred_element_type=jnp.f...  10.3 us
    dot_general x1, matrix products, shards(): part_a = jnp.einsum('bt,bdr->tdr', hit_float, block_a, precision=highest)  10.1 us
  transfers between devices with their start and end apart: 5, of which 5 were waited for; matrix products, arithmetic and copies ran while one was open for 11% of the time, Pallas kernels for 0%

commit v1 on v0

v1 whole, which is shorter than its diff:
```python
import functools

import jax
import jax.numpy as jnp
from jax import lax
from jax.experimental import pallas as pl
from jax.experimental.pallas import tpu as pltpu
from jax.sharding import PartitionSpec as P

adapter_alpha_scale = 16.0
beta_one = 0.9
beta_two = 0.999
adam_eps = 1e-08
learn_rate = 0.001
adam_step = 10
half = jnp.bfloat16
wide = jnp.float32
MIB = 1 << 20
NT = (((1,), (1,)), ((), ()))
TN = (((0,), (0,)), ((), ()))
NN = (((1,), (0,)), ((), ()))


def mm(a, b, dims):
    return lax.dot_general(a, b, dims, preferred_element_type=wide)


def moment_update_rule(param, first, second, grad):
    new_first = beta_one * first + (1.0 - beta_one) * grad
    new_second = beta_two * second + (1.0 - beta_two) * grad * grad
    fixed_first = new_first / (1.0 - beta_one**adam_step)
    fixed_second = new_second / (1.0 - beta_two**adam_step)
    return (
        param - learn_rate * fixed_first / (jnp.sqrt(fixed_second) + adam_eps),
        new_first,
        new_second,
    )


def bit_order(n):
    if n == 1:
        return [0]
    inner = [2 * i for i in bit_order(n // 2)]
    return inner + [i + 1 for i in inner]


def line_ring(n):
    return [0] + list(range(1, n, 2)) + list(range(n - 2 + n % 2, 0, -2))


def swap(v, axis, n, bits):
    return lax.ppermute(v, axis, [(i, i ^ bits) for i in range(n)])


def kernel_params(mib):
    return pltpu.CompilerParams(vmem_limit_bytes=mib * MIB)


def cost(flops, nbytes):
    return pl.CostEstimate(flops=int(flops), bytes_accessed=int(nbytes), transcendentals=0)


def hidden_kernel(order, ranks, x_ref, even_ref, odd_ref, info_ref, out_ref):
    slot = info_ref[0:1, :]
    x = x_ref[...]
    total = None
    per = len(order) // 2
    for side, ref in enumerate((even_ref, odd_ref)):
        prod = mm(ref[...], x, NT)
        for i in range(per):
            piece = prod[i * ranks : (i + 1) * ranks]
            piece = jnp.where(slot == float(order[side * per + i]), piece, 0.0)
            total = piece if total is None else total + piece
    out_ref[...] = total.astype(half)


def hidden_call(x, even, odd, info, order, ranks):
    tok, width = x.shape
    blk = min(256, tok)
    return pl.pallas_call(
        functools.partial(hidden_kernel, order, ranks),
        grid=(tok // blk,),
        in_specs=[
            pl.BlockSpec((blk, width), lambda i: (i, 0)),
            pl.BlockSpec(even.shape, lambda i: (0, 0)),
            pl.BlockSpec(odd.shape, lambda i: (0, 0)),
            pl.BlockSpec((info.shape[0], blk), lambda i: (0, i)),
        ],
        out_specs=pl.BlockSpec((ranks, blk), lambda i: (0, i)),
        out_shape=jax.ShapeDtypeStruct((ranks, tok), half),
        compiler_params=kernel_params(32),
        cost_estimate=cost(2 * tok * width * ranks * len(order), 2 * (x.size + 2 * even.size)),
        name="hidden",
    )(x, even, odd, info)


def upward_kernel(parts, src_ref, *refs):
    cots, (even_ref, odd_ref, coef_ref, out_ref) = refs[:parts], refs[parts:]
    kw = cots[0].shape[1]
    rows = cots[0].shape[0]
    per = even_ref.shape[0]
    blocks = coef_ref.shape[0]
    for side, ref in enumerate((even_ref, odd_ref)):
        acc = None
        for i in range(parts):
            cols = pl.ds(pl.multiple_of(src_ref[i] * kw, kw), kw)
            prod = mm(cots[i][...], ref[:, cols], NT)
            acc = prod if acc is None else acc + prod
        coef = coef_ref[:, :, side * per : (side + 1) * per]
        acc = acc.reshape(blocks, rows // blocks, per) * coef
        out_ref[:, side * per : (side + 1) * per] = acc.reshape(rows, per).astype(half)


def upward_call(cots, even, odd, coef, src):
    rows, kw = cots[0].shape
    per = even.shape[0]
    blocks = coef.shape[0]
    return pl.pallas_call(
        functools.partial(upward_kernel, len(cots)),
        grid_spec=pltpu.PrefetchScalarGridSpec(
            num_scalar_prefetch=1,
            grid=(1,),
            in_specs=[pl.BlockSpec((rows, kw), lambda i, s: (0, 0))] * len(cots)
            + [
                pl.BlockSpec(even.shape, lambda i, s: (0, 0)),
                pl.BlockSpec(odd.shape, lambda i, s: (0, 0)),
                pl.BlockSpec(coef.shape, lambda i, s: (0, 0, 0)),
            ],
            out_specs=pl.BlockSpec((rows, 2 * per), lambda i, s: (0, 0)),
        ),
        out_shape=jax.ShapeDtypeStruct((rows, 2 * per), half),
        compiler_params=kernel_params(32),
        cost_estimate=cost(4 * rows * kw * len(cots) * per, 2 * (rows * kw * len(cots) + 2 * even.size)),
        name="upward",
    )(src, *cots, even, odd, coef)


def down_kernel(chunks, ranks, *refs):
    x_ref, us, (keep_ref, send_ref) = refs[0], refs[1 : 1 + chunks], refs[1 + chunks :]
    acc = None
    at = 0
    for u in us:
        rows = u.shape[0]
        prod = mm(x_ref[at : at + rows, :], u[...], TN)
        acc = prod if acc is None else acc + prod
        at += rows
    per = keep_ref.shape[0]
    for i in range(per):
        keep_ref[i] = acc[:, i * ranks : (i + 1) * ranks].astype(half)
        send_ref[i] = acc[:, (per + i) * ranks : (per + i + 1) * ranks].astype(half)


def down_call(x, us, ranks, start, count):
    tok = x.shape[0]
    slots = us[0].shape[1] // ranks
    blk = min(512, count)
    shape = jax.ShapeDtypeStruct((slots // 2, count, ranks), half)
    first = start // blk
    return pl.pallas_call(
        functools.partial(down_kernel, len(us), ranks),
        grid=(count // blk,),
        in_specs=[pl.BlockSpec((tok, blk), lambda i: (0, first + i))]
        + [pl.BlockSpec(u.shape, lambda i: (0, 0)) for u in us],
        out_specs=[pl.BlockSpec((slots // 2, blk, ranks), lambda i: (0, i, 0))] * 2,
        out_shape=[shape, shape],
        compiler_params=kernel_params(32),
        cost_estimate=cost(2 * tok * count * slots * ranks, 2 * (tok * count + slots * ranks * (tok + count))),
        name="down_grad",
    )(x, *us)


def up_kernel(order, chunks, parts, n_hs, extra, src_ref, *refs):
    hs = refs[:n_hs]
    info_ref, counts_ref = refs[n_hs : n_hs + 2]
    cots = refs[n_hs + 2 : n_hs + 2 + chunks * parts]
    keep_ref, send_ref = refs[n_hs + 2 + chunks * parts :]
    own = hs[0].shape[0]
    per = len(order) // 2
    total = hs[0][...].astype(wide)
    for h in hs[1:]:
        total = total + h[...].astype(wide)
    rank_at = src_ref[parts] * own + lax.broadcasted_iota(jnp.int32, total.shape, 0)
    slot, rank, scale = info_ref[0:1, :], info_ref[1:2, :], info_ref[2:3, :]
    total = jnp.where(rank_at.astype(wide) < rank, total * scale, 0.0).astype(half)
    lhs = jnp.concatenate(
        [jnp.where(slot == float(j), total, jnp.zeros_like(total)) for j in order], axis=0
    )
    for i in range(parts):
        acc = None
        at = 0
        for c in range(chunks):
            cot = cots[c * parts + i]
            prod = mm(lhs[:, at : at + cot.shape[0]], cot[...], NN)
            acc = prod if acc is None else acc + prod
            at += cot.shape[0]
        kw = acc.shape[1]
        cols = pl.ds(pl.multiple_of(src_ref[i] * kw, kw), kw)
        acc = acc.astype(half)
        for k in range(per):
            keep_ref[k, :own, cols] = acc[k * own : (k + 1) * own]
            send_ref[k, :own, cols] = acc[(per + k) * own : (per + k + 1) * own]
    row = lax.broadcasted_iota(jnp.int32, (extra, keep_ref.shape[2]), 0)
    for k in range(per):
        for ref, at in ((keep_ref, k), (send_ref, per + k)):
            tail = jnp.where(row == 0, counts_ref[0, at], jnp.where(row == 1, counts_ref[1, at], 0.0))
            ref[k, own:, :] = tail.astype(half)


def up_call(hs, info, counts, chunk_cots, src, order, extra=16):
    parts = len(chunk_cots[0])
    own, tok = hs[0].shape
    cots = [c for chunk in chunk_cots for c in chunk]
    kw = cots[0].shape[1]
    shape = jax.ShapeDtypeStruct((len(order) // 2, own + extra, kw * parts), half)
    whole = lambda a: pl.BlockSpec(a.shape, lambda i, s, n=len(a.shape): (0,) * n)
    return pl.pallas_call(
        functools.partial(up_kernel, order, len(chunk_cots), parts, len(hs), extra),
        grid_spec=pltpu.PrefetchScalarGridSpec(
            num_scalar_prefetch=1,
            grid=(1,),
            in_specs=[whole(h) for h in hs]
            + [whole(info), pl.BlockSpec(memory_space=pltpu.SMEM)]
            + [whole(c) for c in cots],
            out_specs=[whole(shape)] * 2,
        ),
        out_shape=[shape, shape],
        compiler_params=kernel_params(32),
        cost_estimate=cost(2 * len(order) * own * tok * kw * parts, 4 * tok * kw * parts),
        name="up_grad",
    )(src, *hs, info, counts, *cots)


def up_plain(hs, info, counts, chunk_cots, z, order, extra=16):
    own = hs[0].shape[0]
    total = sum(h.astype(wide) for h in hs)
    rank_at = (z * own + jnp.arange(own, dtype=jnp.int32)).astype(wide)
    total = jnp.where(rank_at[:, None] < info[1:2], total * info[2:3], 0.0).astype(half)
    lhs = jnp.concatenate([jnp.where(info[0:1] == float(j), total, 0) for j in order], axis=0)
    cot = jnp.concatenate([chunk[0] for chunk in chunk_cots], axis=0)
    grads = mm(lhs, cot, NN).astype(half).reshape(len(order), own, cot.shape[1])
    tail = jnp.pad(counts.T, ((0, 0), (0, extra - 2))).astype(half)[:, :, None]
    tail = jnp.broadcast_to(tail, (len(order), extra, cot.shape[1]))
    both = jnp.concatenate([grads, tail], axis=1)
    return both[: len(order) // 2], both[len(order) // 2 :]


def acts_kernel(chunks, parts, src_ref, *refs):
    w_ref, even_ref, odd_ref = refs[:3]
    cots = refs[3 : 3 + chunks * parts]
    us = refs[3 + chunks * parts : 3 + chunks * parts + chunks]
    out_ref = refs[-1]
    per = even_ref.shape[0]
    at = 0
    for c in range(chunks):
        rows = us[c].shape[0]
        acc = mm(us[c][:, :per], even_ref[...], NN) + mm(us[c][:, per:], odd_ref[...], NN)
        for i in range(parts):
            cot = cots[c * parts + i]
            kw = cot.shape[1]
            cols = pl.ds(pl.multiple_of(src_ref[i] * kw, kw), kw)
            acc = acc + mm(cot[...], w_ref[:, cols], NT)
        out_ref[at : at + rows, :] = acc.astype(half)
        at += rows


def acts_call(w, even, odd, chunk_cots, us, src):
    width, kfull = w.shape
    per = even.shape[0]
    parts = len(chunk_cots[0])
    tok = sum(u.shape[0] for u in us)
    blk = min(512, width)
    cots = [c for chunk in chunk_cots for c in chunk]
    whole = lambda a: pl.BlockSpec(a.shape, lambda i, s: (0, 0))
    return pl.pallas_call(
        functools.partial(acts_kernel, len(us), parts),
        grid_spec=pltpu.PrefetchScalarGridSpec(
            num_scalar_prefetch=1,
            grid=(width // blk,),
            in_specs=[
                pl.BlockSpec((blk, kfull), lambda i, s: (i, 0)),
                pl.BlockSpec((per, blk), lambda i, s: (0, i)),
                pl.BlockSpec((per, blk), lambda i, s: (0, i)),
            ]
            + [whole(c) for c in cots]
            + [whole(u) for u in us],
            out_specs=pl.BlockSpec((tok, blk), lambda i, s: (0, i)),
        ),
        out_shape=jax.ShapeDtypeStruct((tok, width), half),
        compiler_params=kernel_params(40),
        cost_estimate=cost(2 * tok * width * (kfull + 2 * per), 2 * (w.size + 2 * even.size + tok * (width + kfull))),
        name="grad_acts",
    )(src, w, even, odd, *cots, *us)


def shards(
    n_dp,
    n_tensor,
    activations,
    output_gradient,
    value_weight,
    adapter_down_factors,
    adapter_up_factors,
    down_first_moment,
    down_second_moment,
    up_first_moment,
    up_second_moment,
    block_tenant,
    block_live_tokens,
    tenant_storage_slot,
    tenant_adapter_rank,
):
    tok, width = activations.shape
    blocks = block_tenant.shape[0]
    blk_len = tok // blocks
    slots = tenant_storage_slot.shape[0]
    assert adapter_down_factors.shape[0] == 1 and slots == n_dp
    ranks = adapter_down_factors.shape[2]
    own_ranks = adapter_up_factors.shape[1]
    value_width = adapter_up_factors.shape[2]
    z = lax.axis_index("tensor")
    d = lax.axis_index("dp")
    order = bit_order(slots)
    levels = [1 << b for b in range(slots.bit_length() - 1)]

    tenant_ids = jnp.arange(slots, dtype=jnp.int32)
    matches = block_tenant[:, None] == tenant_ids[None, :]
    slot_of = jnp.sum(jnp.where(matches, tenant_storage_slot[None, :], 0), axis=1)
    rank_of = jnp.sum(jnp.where(matches, tenant_adapter_rank[None, :], 0), axis=1)
    scale_of = adapter_alpha_scale / rank_of.astype(wide)
    near_of = jnp.bitwise_xor(slot_of, d)
    order_row = jnp.array(order, jnp.int32)
    hit = near_of[:, None] == order_row[None, :]
    rank_live = jnp.arange(ranks, dtype=jnp.int32)[None, :] < rank_of[:, None]
    coef = jnp.where(hit[:, :, None] & rank_live[:, None, :], scale_of[:, None, None], 0.0)
    coef = coef.reshape(blocks, 1, slots * ranks)
    info = jnp.stack([near_of.astype(wide), rank_of.astype(wide), scale_of], axis=0)
    info = jnp.repeat(jnp.pad(info, ((0, 5), (0, 0))), blk_len, axis=1)
    counts = jnp.sum(jnp.where(hit, block_live_tokens[:, None], 0), axis=0)
    counts = jnp.stack([counts // 32, counts % 32]).astype(wide)
    row_live = jnp.arange(blk_len, dtype=jnp.int32)[None, :] < block_live_tokens[:, None]

    ring = line_ring(n_tensor)
    ring_at = [ring.index(i) for i in range(n_tensor)]
    ring_pairs = [(ring[i], ring[(i + 1) % n_tensor]) for i in range(n_tensor)]
    place = jnp.array(ring_at, jnp.int32)[z]
    src = jnp.array(ring, jnp.int32)[(place - jnp.arange(n_tensor, dtype=jnp.int32)) % n_tensor]
    src = jnp.concatenate([src, z.astype(jnp.int32)[None]])
    masked = jnp.where(row_live.reshape(tok, 1), output_gradient, jnp.zeros((), half))
    chunks = 2
    chunk_rows = tok // chunks
    chunk_cots = []
    for c in range(chunks):
        chunk_cots.append([masked[c * chunk_rows : (c + 1) * chunk_rows]])
    for _ in range(n_tensor - 1):
        for c in range(chunks):
            chunk_cots[c].append(lax.ppermute(chunk_cots[c][-1], "tensor", ring_pairs))

    if output_gradient.shape[1] % 128:
        away = (place - jnp.array(ring_at, jnp.int32)) % n_tensor
        chunk_cots = [
            [jnp.moveaxis(jnp.stack(c)[away], 0, 1).reshape(chunk_rows, value_width)]
            for c in chunk_cots
        ]
        src = jnp.concatenate([jnp.zeros((1,), jnp.int32), src[-1:]])

    even_a = adapter_down_factors[0].astype(half).T
    for bits in reversed(levels[1:]):
        even_a = jnp.concatenate([even_a, swap(even_a, "dp", n_dp, bits)], axis=0)
    odd_a = swap(even_a, "dp", n_dp, 1)

    own_b = adapter_up_factors[0].astype(half)
    pieces = jnp.stack([own_b] + [swap(own_b, "tensor", n_tensor, k) for k in range(1, n_tensor)])
    even_b = pieces[jnp.bitwise_xor(z, jnp.arange(n_tensor))].reshape(ranks, value_width)
    for bits in reversed(levels[1:]):
        even_b = jnp.concatenate([even_b, swap(even_b, "dp", n_dp, bits)], axis=0)
    odd_b = swap(even_b, "dp", n_dp, 1)

    hidden_part = hidden_call(activations, even_a, odd_a, info, order, ranks)
    hs = [lax.dynamic_slice_in_dim(hidden_part, z * own_ranks, own_ranks, 0)]
    for k in range(1, n_tensor):
        theirs = lax.dynamic_slice_in_dim(
            hidden_part, jnp.bitwise_xor(z, k) * own_ranks, own_ranks, 0
        )
        hs.append(swap(theirs, "tensor", n_tensor, k))

    per_chunk = blocks // chunks
    us = [
        upward_call(chunk_cots[c], even_b, odd_b, coef[c * per_chunk : (c + 1) * per_chunk], src)
        for c in range(chunks)
    ]

    def scatter(keep, send):
        total = keep.astype(wide) + swap(send, "dp", n_dp, 1).astype(wide)
        for bits in levels[1:]:
            n = total.shape[0] // 2
            total = total[:n] + swap(total[n:].astype(half), "dp", n_dp, bits).astype(wide)
        return total[0]

    down_sums = []
    pieces_down = 2
    for p in range(pieces_down):
        rows = width // pieces_down
        keep, send = down_call(activations, us, ranks, p * rows, rows)
        down_sums.append(scatter(keep, send))
    if own_ranks % 16:
        keep, send = up_plain(hs, info, counts, chunk_cots, z, order)
    else:
        keep, send = up_call(hs, info, counts, chunk_cots, src, order)
    up_sum = scatter(keep, send)
    denom = jnp.maximum(up_sum[own_ranks, 0] * 32.0 + up_sum[own_ranks + 1, 0], 1.0)
    grad_acts = acts_call(value_weight, even_a, odd_a, chunk_cots, us, src)

    down_grad = jnp.concatenate(down_sums, axis=0)[None] / denom
    up_grad = up_sum[None, :own_ranks] / denom
    return (
        grad_acts,
        *moment_update_rule(adapter_down_factors, down_first_moment, down_second_moment, down_grad),
        *moment_update_rule(adapter_up_factors, up_first_moment, up_second_moment, up_grad),
    )


def solution(mesh):
    tokens = P(("groups", "dp"), "tensor")
    factors = P(("groups", "dp"), "tensor", None)
    placed = (tokens, tokens, P("tensor", None), *([factors] * 6), P(("groups", "dp")), P(("groups", "dp")), P("groups"), P("groups"))
    return jax.shard_map(
        functools.partial(shards, mesh.shape["dp"], mesh.shape["tensor"]),
        mesh=mesh,
        in_specs=placed,
        out_specs=(tokens, *([factors] * 6)),
        check_vma=False,
    )
```

time: 233 us -> 108 us (0.46)
  waiting for transfers between devices: 102 us -> 37.2 us
  matrix products: 57.1 us -> 0 us
  starting transfers between devices: 0.6 us -> 29.8 us
  blocking collectives: 27.3 us -> 0 us
  Pallas kernels: 0 us -> 21.7 us
  local copies, waits for them, and re-layouts: 22.4 us -> 7.1 us
  between operations: 14.6 us -> 2.36 us
    all_gather x2 -> x0, waiting for transfers between devices: 64.3 us -> none  [the longest x1 41.9 us: shards(): cot_full = lax.all_gather(output_gradient, 'tensor', axis=1, tiled=True)]
    dot_general x10 -> x0, matrix products: 57.1 us -> none  [the longest x1 11.9 us: shards(): jnp.einsum('bpr,bdr->bpd', full_u, used_a, preferred_element_type=jnp.flo...]
    reduce_scatter x3 -> x0, waiting for transfers between devices: 37.4 us -> none  [the longest x1 21.2 us: shards(): lax.psum_scatter(part_a.astype(jnp.bfloat16), 'dp', scatter_dimension=0,...]
    ppermute x0 -> x22, waiting for transfers between devices: none -> 37.2 us  [the longest x16 26.9 us: swap(): return lax.ppermute(v, axis, [(i, i ^ bits) for i in range(n)])]
    ppermute x0 -> x22, starting transfers between devices: none -> 29.8 us  [the longest x16 19.2 us: swap(): return lax.ppermute(v, axis, [(i, i ^ bits) for i in range(n)])]
    pallas_call x0 -> x7, Pallas kernels: none -> 21.7 us  [the longest x1 9.76 us: acts_call(): pl.pallas_call(functools.partial(acts_kernel, len(us), parts), grid_spec=...]
    all_gather x2 -> x0, blocking collectives: 21.5 us -> none  [the longest x1 14.3 us: shards(): lax.all_gather(scaled_u, 'tensor', axis=1, tiled=True)]
    dot_general x1 -> x0, local copies, waits for them, and re-layouts: 17.7 us -> none  [shards(): jnp.einsum('bpd,bpr->bdr', x_blocks, full_u, preferred_element_type=jnp.f...]
  transfers between devices with their start and end apart: 5 -> 22, of which waited for: 5 -> 13; matrix products, arithmetic and copies ran while one was open for 11% -> 6% of each run, Pallas kernels for 0% -> 15%
where the time goes in v1:
time: 108 us; the launch traced here: 107 us
  waiting for transfers between devices  37.2 us (34%)
  starting transfers between devices  29.8 us (28%)
  Pallas kernels  21.7 us (20%)
  other arithmetic  9.35 us (9%)
  local copies, waits for them, and re-layouts  7.1 us (7%)
  between operations  2.36 us (2%)
    ppermute x16, waiting for transfers between devices, swap(): return lax.ppermute(v, axis, [(i, i ^ bits) for i in range(n)])  26.9 us
    ppermute x16, starting transfers between devices, swap(): return lax.ppermute(v, axis, [(i, i ^ bits) for i in range(n)])  19.2 us
    ppermute x6, starting transfers between devices, shards(): chunk_cots[c].append(lax.ppermute(chunk_cots[c][-1], 'tensor', ring_pairs))  10.6 us
    ppermute x6, waiting for transfers between devices, shards(): chunk_cots[c].append(lax.ppermute(chunk_cots[c][-1], 'tensor', ring_pairs))  10.3 us
    pallas_call x1, Pallas kernels, acts_call(): pl.pallas_call(functools.partial(acts_kernel, len(us), parts), grid_spec=...  9.76 us
    pallas_call x1, Pallas kernels, hidden_call(): pl.pallas_call(functools.partial(hidden_kernel, order, ranks), grid=(tok...  4.32 us
    unnamed x25, local copies, waits for them, and re-layouts  3.7 us
    pallas_call x2, Pallas kernels, down_call(): pl.pallas_call(functools.partial(down_kernel, len(us), ranks), grid=(coun...  3.51 us
  transfers between devices with their start and end apart: 22, of which 13 were waited for; matrix products, arithmetic and copies ran while one was open for 6% of the time, Pallas kernels for 15%

profile of v1, /device:TPU:0, one launch (start us, length us, event | category | flops | bytes accessed | tf_op | source)
XLA Modules:
  0.0 107.5 jit_solution(8013610012807423833)
XLA Ops:
  0.7 1.4 %copy.24 = bf16[1,2048,128]{1,2,0:T(8,128)(2,1)S(1)} copy(f32[1,2048,128]{2,1,0:T(8,128)} %param.19) | data formatting | bytes 1572864 | tf_op args[3]
  2.1 3.0 %collective-permute-start = (bf16[128,2048]{1,0:T(8,128)(2,1)S(1)}, bf16[128,2048]{1,0:T(8,128)(2,1)}, u32[]{:S(2)}, u32[]{:S(2)}) collective-permute-start(bf16[128,2048]{1,0:T(8,128)(2,1)S(1)} %bitcast.43), channel_id=1, source_target_pairs={{0,8},{4,12},{8,0},{12,4},{1,9},{5,13},{9,1},{13,5},{2,10},{6,14},... | collective-permute-start | bytes 1572872 | tf_op jit(solution)/shard_map/ppermute | solution.py:52
  7.2 1.6 %collective-permute-start.5 = (bf16[512,256]{1,0:T(8,128)(2,1)S(1)}, bf16[512,256]{1,0:T(8,128)(2,1)S(1)}, u32[]{:S(2)}, u32[]{:S(2)}) collective-permute-start(bf16[512,256]{1,0:T(8,128)(2,1)S(1)} %get-tuple-element.29.refs_0_.refs_7_.refs_10_), channel_id=1, source_target_pairs={{0,1},{1,3},{3,2},{2,0},{4,5},{5,7},{7,6},{6,4},{8,9},{9,11},{11,1... | collective-permute-start | bytes 786440 | tf_op jit(solution)/shard_map/ppermute | solution.py:356
  8.9 2.6 %collective-permute-start.2 = (bf16[512,256]{1,0:T(8,128)(2,1)S(1)}, bf16[512,256]{1,0:T(8,128)(2,1)S(1)}, u32[]{:S(2)}, u32[]{:S(2)}) collective-permute-start(bf16[512,256]{1,0:T(8,128)(2,1)S(1)} %get-tuple-element.30.refs_0_.refs_3_.refs_6_), channel_id=1, source_target_pairs={{0,1},{1,3},{3,2},{2,0},{4,5},{5,7},{7,6},{6,4},{8,9},{9,11},{11,1... | collective-permute-start | bytes 786440 | tf_op jit(solution)/shard_map/ppermute | solution.py:356
  12.3 4.8 %collective-permute-done = bf16[128,2048]{1,0:T(8,128)(2,1)} collective-permute-done((bf16[128,2048]{1,0:T(8,128)(2,1)S(1)}, bf16[128,2048]{1,0:T(8,128)(2,1)}, u32[]{:S(2)}, u32[]{:S(2)}) %collective-permute-start) | collective-permute-done | bytes 524320 | tf_op jit(solution)/shard_map/ppermute | solution.py:52
  20.6 1.9 %collective-permute-start.6 = (bf16[512,256]{1,0:T(8,128)(2,1)S(1)}, bf16[512,256]{1,0:T(8,128)(2,1)S(1)}, u32[]{:S(2)}, u32[]{:S(2)}) collective-permute-start(bf16[512,256]{1,0:T(8,128)(2,1)S(1)} %collective-permute-done.5.refs_1_.refs_8_.refs_11_), channel_id=1, source_target_pairs={{0,1},{1,3},{3,2},{2,0},{4,5},{5,7},{7,6},{6,4},{8,9},{9,11},{11,1... | collective-permute-start | bytes 786440 | tf_op jit(solution)/shard_map/ppermute | solution.py:356
  22.5 2.6 %collective-permute-start.3 = (bf16[512,256]{1,0:T(8,128)(2,1)S(1)}, bf16[512,256]{1,0:T(8,128)(2,1)S(1)}, u32[]{:S(2)}, u32[]{:S(2)}) collective-permute-start(bf16[512,256]{1,0:T(8,128)(2,1)S(1)} %collective-permute-done.2.refs_1_.refs_4_.refs_7_), channel_id=1, source_target_pairs={{0,1},{1,3},{3,2},{2,0},{4,5},{5,7},{7,6},{6,4},{8,9},{9,11},{11,1... | collective-permute-start | bytes 786440 | tf_op jit(solution)/shard_map/ppermute | solution.py:356
  25.1 5.6 %collective-permute-done.6.refs_2_.refs_9_.refs_12_ = bf16[512,256]{1,0:T(8,128)(2,1)S(1)} collective-permute-done((bf16[512,256]{1,0:T(8,128)(2,1)S(1)}, bf16[512,256]{1,0:T(8,128)(2,1)S(1)}, u32[]{:S(2)}, u32[]{:S(2)}) %collective-permute-start.6) | collective-permute-done | bytes 262176 | tf_op jit(solution)/shard_map/ppermute | solution.py:356
  31.7 4.7 %collective-permute-done.3.refs_2_.refs_5_.refs_8_ = bf16[512,256]{1,0:T(8,128)(2,1)S(1)} collective-permute-done((bf16[512,256]{1,0:T(8,128)(2,1)S(1)}, bf16[512,256]{1,0:T(8,128)(2,1)S(1)}, u32[]{:S(2)}, u32[]{:S(2)}) %collective-permute-start.3) | collective-permute-done | bytes 262176 | tf_op jit(solution)/shard_map/ppermute | solution.py:356
  37.3 2.2 %copy-done = bf16[1024,2048]{1,0:T(8,128)(2,1)S(1)} copy-done((bf16[1024,2048]{1,0:T(8,128)(2,1)S(1)}, bf16[1024,2048]{1,0:T(8,128)(2,1)}, u32[]{:S(2)}) %copy-start) | copy-done | bytes 4194328
  39.5 4.3 %hidden.1 = bf16[128,1024]{1,0:T(8,128)(2,1)S(1)} custom-call(bf16[1024,2048]{1,0:T(8,128)(2,1)S(1)} %copy-done, bf16[256,2048]{1,0:T(8,128)(2,1)S(1)} %pad_maximum_fusion.refs_1_.even_ref, bf16[256,2048]{1,0:T(8,128)(2,1)} %collective-permute-done.1.refs_2_.odd_ref, f32[8,1024]{1,0:T(8,128)S(1)} %reshape.326.info_ref.refs_4_), custom_call_target="tpu_custom_call" | custom-call | flops 2147483648 | bytes 6291456 | tf_op jit(solution)/shard_map/hidden/pallas_call | solution.py:80
  43.9 2.9 %collective-permute-start.19 = (bf16[32,1024]{1,0:T(8,128)(2,1)S(1)}, bf16[32,1024]{1,0:T(8,128)(2,1)S(1)}, u32[]{:S(2)}, u32[]{:S(2)}) collective-permute-start(bf16[32,1024]{1,0:T(8,128)(2,1)S(1)} %get-tuple-element.31), channel_id=1, source_target_pairs={{0,3},{1,2},{2,1},{3,0},{4,7},{5,6},{6,5},{7,4},{8,11},{9,10},{10,... | collective-permute-start | bytes 196616 | tf_op jit(solution)/shard_map/ppermute | solution.py:52
  46.8 2.0 %collective-permute-start.18 = (bf16[32,1024]{1,0:T(8,128)(2,1)S(1)}, bf16[32,1024]{1,0:T(8,128)(2,1)S(1)}, u32[]{:S(2)}, u32[]{:S(2)}) collective-permute-start(bf16[32,1024]{1,0:T(8,128)(2,1)S(1)} %get-tuple-element.32), channel_id=1, source_target_pairs={{0,2},{1,3},{2,0},{3,1},{4,6},{5,7},{6,4},{7,5},{8,10},{9,11},{10,... | collective-permute-start | bytes 196616 | tf_op jit(solution)/shard_map/ppermute | solution.py:52
  48.9 1.9 %collective-permute-done.19.refs_3_ = bf16[32,1024]{1,0:T(8,128)(2,1)S(1)} collective-permute-done((bf16[32,1024]{1,0:T(8,128)(2,1)S(1)}, bf16[32,1024]{1,0:T(8,128)(2,1)S(1)}, u32[]{:S(2)}, u32[]{:S(2)}) %collective-permute-start.19) | collective-permute-done | bytes 65568 | tf_op jit(solution)/shard_map/ppermute | solution.py:52
  50.8 3.1 %collective-permute-done.18.refs_2_ = bf16[32,1024]{1,0:T(8,128)(2,1)S(1)} collective-permute-done((bf16[32,1024]{1,0:T(8,128)(2,1)S(1)}, bf16[32,1024]{1,0:T(8,128)(2,1)S(1)}, u32[]{:S(2)}, u32[]{:S(2)}) %collective-permute-start.18) | collective-permute-done | bytes 65568 | tf_op jit(solution)/shard_map/ppermute | solution.py:52
  54.2 1.5 %up_grad.1 = (bf16[2,48,1024]{2,1,0:T(8,128)(2,1)S(1)}, bf16[2,48,1024]{2,1,0:T(8,128)(2,1)S(1)}) custom-call(s32[5]{0:T(128)S(1)} %pad_add_fusion.src_ref, bf16[32,1024]{1,0:T(8,128)(2,1)S(1)} %get-tuple-element.34.refs_0_, bf16[32,1024]{1,0:T(8,128)(2,1)S(1)} %collective-permute-done.17.refs_1_, bf16[32,1024]{1,0:T(8,128)(2,1)S(1)} %collective-permute-done.18.refs_2_, ...), custom_call_target="tpu_custom_call" | custom-call | flops 268435456 | bytes 4194304 | tf_op jit(solution)/shard_map/up_grad/pallas_call | solution.py:216
  55.9 1.4 %collective-permute-done.20 = bf16[2,48,1024]{2,1,0:T(8,128)(2,1)S(1)} collective-permute-done((bf16[2,48,1024]{2,1,0:T(8,128)(2,1)S(1)}, bf16[2,48,1024]{2,1,0:T(8,128)(2,1)S(1)}, u32[]{:S(2)}, u32[]{:S(2)}) %collective-permute-start.20) | collective-permute-done | bytes 196640 | tf_op jit(solution)/shard_map/ppermute | solution.py:52
  57.4 1.6 %collective-permute-start.21 = (bf16[1,48,1024]{2,1,0:T(8,128)(2,1)S(1)}, bf16[1,48,1024]{2,1,0:T(8,128)(2,1)S(1)}, u32[]{:S(2)}, u32[]{:S(2)}) collective-permute-start(bf16[1,48,1024]{2,1,0:T(8,128)(2,1)S(1)} %slice.94), channel_id=1, source_target_pairs={{0,8},{4,12},{8,0},{12,4},{1,9},{5,13},{9,1},{13,5},{2,10},{6,14},... | collective-permute-start | bytes 294920 | tf_op jit(solution)/shard_map/ppermute | solution.py:52
  58.9 3.3 %collective-permute-done.21 = bf16[1,48,1024]{2,1,0:T(8,128)(2,1)S(1)} collective-permute-done((bf16[1,48,1024]{2,1,0:T(8,128)(2,1)S(1)}, bf16[1,48,1024]{2,1,0:T(8,128)(2,1)S(1)}, u32[]{:S(2)}, u32[]{:S(2)}) %collective-permute-start.21) | collective-permute-done | bytes 98336 | tf_op jit(solution)/shard_map/ppermute | solution.py:52
  64.9 2.3 %collective-permute-start.10 = (bf16[32,1024]{1,0:T(8,128)(2,1)S(1)}, bf16[32,1024]{1,0:T(8,128)(2,1)S(1)}, u32[]{:S(2)}, u32[]{:S(2)}) collective-permute-start(bf16[32,1024]{1,0:T(8,128)(2,1)S(1)} %bitcast.48), channel_id=1, source_target_pairs={{0,3},{1,2},{2,1},{3,0},{4,7},{5,6},{6,5},{7,4},{8,11},{9,10},{10,... | collective-permute-start | bytes 196616 | tf_op jit(solution)/shard_map/ppermute | solution.py:52
  67.3 2.0 %collective-permute-start.8 = (bf16[32,1024]{1,0:T(8,128)(2,1)S(1)}, bf16[32,1024]{1,0:T(8,128)(2,1)S(1)}, u32[]{:S(2)}, u32[]{:S(2)}) collective-permute-start(bf16[32,1024]{1,0:T(8,128)(2,1)S(1)} %bitcast.50), channel_id=1, source_target_pairs={{0,1},{1,0},{2,3},{3,2},{4,5},{5,4},{6,7},{7,6},{8,9},{9,8},{10,11... | collective-permute-start | bytes 196616 | tf_op jit(solution)/shard_map/ppermute | solution.py:52
  69.3 1.8 %collective-permute-done.10 = bf16[32,1024]{1,0:T(8,128)(2,1)S(1)} collective-permute-done((bf16[32,1024]{1,0:T(8,128)(2,1)S(1)}, bf16[32,1024]{1,0:T(8,128)(2,1)S(1)}, u32[]{:S(2)}, u32[]{:S(2)}) %collective-permute-start.10) | collective-permute-done | bytes 65568 | tf_op jit(solution)/shard_map/ppermute | solution.py:52
  71.1 1.8 %collective-permute-done.9 = bf16[32,1024]{1,0:T(8,128)(2,1)S(1)} collective-permute-done((bf16[32,1024]{1,0:T(8,128)(2,1)S(1)}, bf16[32,1024]{1,0:T(8,128)(2,1)S(1)}, u32[]{:S(2)}, u32[]{:S(2)}) %collective-permute-start.9) | collective-permute-done | bytes 65568 | tf_op jit(solution)/shard_map/ppermute | solution.py:52
  74.2 1.5 %collective-permute-start.11 = (bf16[128,1024]{1,0:T(8,128)(2,1)}, bf16[128,1024]{1,0:T(8,128)(2,1)S(1)}, u32[]{:S(2)}, u32[]{:S(2)}) collective-permute-start(bf16[128,1024]{1,0:T(8,128)(2,1)} %bitcast.45), channel_id=1, source_target_pairs={{0,8},{4,12},{8,0},{12,4},{1,9},{5,13},{9,1},{13,5},{2,10},{6,14},... | collective-permute-start | bytes 786440 | tf_op jit(solution)/shard_map/ppermute | solution.py:52
  75.8 5.6 %collective-permute-done.11 = bf16[128,1024]{1,0:T(8,128)(2,1)S(1)} collective-permute-done((bf16[128,1024]{1,0:T(8,128)(2,1)}, bf16[128,1024]{1,0:T(8,128)(2,1)S(1)}, u32[]{:S(2)}, u32[]{:S(2)}) %collective-permute-start.11) | collective-permute-done | bytes 262176 | tf_op jit(solution)/shard_map/ppermute | solution.py:52
  82.6 1.8 %collective-permute-done.12.refs_5_ = bf16[256,1024]{1,0:T(8,128)(2,1)S(1)} collective-permute-done((bf16[256,1024]{1,0:T(8,128)(2,1)S(1)}, bf16[256,1024]{1,0:T(8,128)(2,1)S(1)}, u32[]{:S(2)}, u32[]{:S(2)}) %collective-permute-start.12) | collective-permute-done | bytes 524320 | tf_op jit(solution)/shard_map/ppermute | solution.py:52
  86.9 1.8 %down_grad.2 = (bf16[2,1024,128]{2,1,0:T(8,128)(2,1)S(1)}, bf16[2,1024,128]{2,1,0:T(8,128)(2,1)S(1)}) custom-call(bf16[1024,2048]{1,0:T(8,128)(2,1)S(1)} %copy-done.1, bf16[512,512]{1,0:T(8,128)(2,1)S(1)} %upward.2.refs_11_.refs_1_, bf16[512,512]{1,0:T(8,128)(2,1)S(1)} %upward.3.refs_12_.refs_2_), custom_call_target="tpu_custom_call" | custom-call | flops 1073741824 | bytes 4194304 | tf_op jit(solution)/shard_map/down_grad/pallas_call | solution.py:159
  88.9 1.8 %down_grad.3 = (bf16[2,1024,128]{2,1,0:T(8,128)(2,1)S(1)}, bf16[2,1024,128]{2,1,0:T(8,128)(2,1)S(1)}) custom-call(bf16[1024,2048]{1,0:T(8,128)(2,1)S(1)} %copy-done.1, bf16[512,512]{1,0:T(8,128)(2,1)S(1)} %upward.2.refs_11_.refs_1_, bf16[512,512]{1,0:T(8,128)(2,1)S(1)} %upward.3.refs_12_.refs_2_), custom_call_target="tpu_custom_call" | custom-call | flops 1073741824 | bytes 4194304 | tf_op jit(solution)/shard_map/down_grad/pallas_call | solution.py:159
  91.3 1.6 %collective-permute-start.14 = (bf16[1,1024,128]{2,1,0:T(8,128)(2,1)S(1)}, bf16[1,1024,128]{2,1,0:T(8,128)(2,1)S(1)}, u32[]{:S(2)}, u32[]{:S(2)}) collective-permute-start(bf16[1,1024,128]{2,1,0:T(8,128)(2,1)S(1)} %slice.93), channel_id=1, source_target_pairs={{0,8},{4,12},{8,0},{12,4},{1,9},{5,13},{9,1},{13,5},{2,10},{6,14},... | collective-permute-start | bytes 786440 | tf_op jit(solution)/shard_map/ppermute | solution.py:52
  93.0 1.4 %collective-permute-start.16 = (bf16[1,1024,128]{2,1,0:T(8,128)(2,1)S(1)}, bf16[1,1024,128]{2,1,0:T(8,128)(2,1)S(1)}, u32[]{:S(2)}, u32[]{:S(2)}) collective-permute-start(bf16[1,1024,128]{2,1,0:T(8,128)(2,1)S(1)} %slice.92), channel_id=1, source_target_pairs={{0,8},{4,12},{8,0},{12,4},{1,9},{5,13},{9,1},{13,5},{2,10},{6,14},... | collective-permute-start | bytes 786440 | tf_op jit(solution)/shard_map/ppermute | solution.py:52
  94.4 9.8 %grad_acts.1 = bf16[1024,2048]{1,0:T(8,128)(2,1)} custom-call(s32[5]{0:T(128)S(1)} %pad_add_fusion.src_ref, bf16[2048,1024]{1,0:T(8,128)(2,1)S(1)} %copy-done.2, bf16[256,2048]{1,0:T(8,128)(2,1)S(1)} %pad_maximum_fusion.refs_1_.even_ref, bf16[256,2048]{1,0:T(8,128)(2,1)} %collective-permute-done.1.refs_2_.odd_ref, ...), custom_call_target="tpu_custom_call" | custom-call | flops 6442450944 | bytes 12582912 | tf_op jit(solution)/shard_map/grad_acts/pallas_call | solution.py:274
  105.4 2.1 %divide_subtract_fusion = (f32[1,2048,128]{2,1,0:T(8,128)}, f32[1,2048,128]{2,1,0:T(8,128)}, f32[1,2048,128]{2,1,0:T(8,128)}) fusion(f32[1,2048,128]{2,1,0:T(8,128)S(1)} %copy-done.4, f32[]{:T(128)} %bitcast.18, f32[1,1024,128]{2,1,0:T(8,128)S(1)} %slice_add_fusion, f32[1,1024,128]{2,1,0:T(8,128)S(1)} %slice_add_fusion.1, f32[1,2048,128]{2,1,0:T(8,128)S(1)} %copy-done.5, ...), kind=kLoop, calls=%fused_computation.6 | loop fusion | flops 3670016 | bytes 7340036 | tf_op jit(solution)/shard_map/sub | solution.py:34
  (87 shorter events, 17.5 us)
Async XLA Ops:
  0.6 17.7 %copy-start.3 = (s32[4]{0:T(128)S(1)}, s32[4]{0:T(128)}, u32[]{:S(2)}) copy-start(s32[4]{0:T(128)} %constant.100.clone) | copy-start | bytes 52
  0.6 19.9 %copy-start.11 = (s32[4]{0:T(128)S(1)}, s32[4]{0:T(128)}, u32[]{:S(2)}) copy-start(s32[4]{0:T(128)} %constant.99.clone) | copy-start | bytes 52
  0.7 19.9 %copy-start.10 = (s32[16]{0:T(128)S(1)}, s32[16]{0:T(128)}, u32[]{:S(2)}) copy-start(s32[16]{0:T(128)} %param.26) | copy-start | bytes 196
  2.1 15.0 %collective-permute-start = (bf16[128,2048]{1,0:T(8,128)(2,1)S(1)}, bf16[128,2048]{1,0:T(8,128)(2,1)}, u32[]{:S(2)}, u32[]{:S(2)}) collective-permute-start(bf16[128,2048]{1,0:T(8,128)(2,1)S(1)} %bitcast.43), channel_id=1, source_target_pairs={{0,8},{4,12},{8,0},{12,4},{1,9},{5,13},{9,1},{13,5},{2,10},{6,14},... | collective-permute-start | bytes 1572872 | tf_op jit(solution)/shard_map/ppermute | solution.py:52
  7.2 13.4 %collective-permute-start.5 = (bf16[512,256]{1,0:T(8,128)(2,1)S(1)}, bf16[512,256]{1,0:T(8,128)(2,1)S(1)}, u32[]{:S(2)}, u32[]{:S(2)}) collective-permute-start(bf16[512,256]{1,0:T(8,128)(2,1)S(1)} %get-tuple-element.29.refs_0_.refs_7_.refs_10_), channel_id=1, source_target_pairs={{0,1},{1,3},{3,2},{2,0},{4,5},{5,7},{7,6},{6,4},{8,9},{9,11},{11,1... | collective-permute-start | bytes 786440 | tf_op jit(solution)/shard_map/ppermute | solution.py:356
  8.9 13.6 %collective-permute-start.2 = (bf16[512,256]{1,0:T(8,128)(2,1)S(1)}, bf16[512,256]{1,0:T(8,128)(2,1)S(1)}, u32[]{:S(2)}, u32[]{:S(2)}) collective-permute-start(bf16[512,256]{1,0:T(8,128)(2,1)S(1)} %get-tuple-element.30.refs_0_.refs_3_.refs_6_), channel_id=1, source_target_pairs={{0,1},{1,3},{3,2},{2,0},{4,5},{5,7},{7,6},{6,4},{8,9},{9,11},{11,1... | collective-permute-start | bytes 786440 | tf_op jit(solution)/shard_map/ppermute | solution.py:356
  18.3 19.0 %collective-permute-start.1 = (bf16[256,2048]{1,0:T(8,128)(2,1)S(1)}, bf16[256,2048]{1,0:T(8,128)(2,1)}, u32[]{:S(2)}, u32[]{:S(2)}) collective-permute-start(bf16[256,2048]{1,0:T(8,128)(2,1)S(1)} %pad_maximum_fusion.refs_1_.even_ref), channel_id=1, source_target_pairs={{0,4},{4,0},{8,12},{12,8},{1,5},{5,1},{9,13},{13,9},{2,6},{6,2},{1... | collective-permute-start | bytes 3145736 | tf_op jit(solution)/shard_map/ppermute | solution.py:52
  20.6 10.1 %collective-permute-start.6 = (bf16[512,256]{1,0:T(8,128)(2,1)S(1)}, bf16[512,256]{1,0:T(8,128)(2,1)S(1)}, u32[]{:S(2)}, u32[]{:S(2)}) collective-permute-start(bf16[512,256]{1,0:T(8,128)(2,1)S(1)} %collective-permute-done.5.refs_1_.refs_8_.refs_11_), channel_id=1, source_target_pairs={{0,1},{1,3},{3,2},{2,0},{4,5},{5,7},{7,6},{6,4},{8,9},{9,11},{11,1... | collective-permute-start | bytes 786440 | tf_op jit(solution)/shard_map/ppermute | solution.py:356
  22.5 13.9 %collective-permute-start.3 = (bf16[512,256]{1,0:T(8,128)(2,1)S(1)}, bf16[512,256]{1,0:T(8,128)(2,1)S(1)}, u32[]{:S(2)}, u32[]{:S(2)}) collective-permute-start(bf16[512,256]{1,0:T(8,128)(2,1)S(1)} %collective-permute-done.2.refs_1_.refs_4_.refs_7_), channel_id=1, source_target_pairs={{0,1},{1,3},{3,2},{2,0},{4,5},{5,7},{7,6},{6,4},{8,9},{9,11},{11,1... | collective-permute-start | bytes 786440 | tf_op jit(solution)/shard_map/ppermute | solution.py:356
  30.7 18.2 %collective-permute-start.7 = (bf16[512,256]{1,0:T(8,128)(2,1)S(1)}, bf16[512,256]{1,0:T(8,128)(2,1)S(1)}, u32[]{:S(2)}, u32[]{:S(2)}) collective-permute-start(bf16[512,256]{1,0:T(8,128)(2,1)S(1)} %collective-permute-done.6.refs_2_.refs_9_.refs_12_), channel_id=1, source_target_pairs={{0,1},{1,3},{3,2},{2,0},{4,5},{5,7},{7,6},{6,4},{8,9},{9,11},{11,1... | collective-permute-start | bytes 786440 | tf_op jit(solution)/shard_map/ppermute | solution.py:356
  36.4 12.6 %collective-permute-start.4 = (bf16[512,256]{1,0:T(8,128)(2,1)S(1)}, bf16[512,256]{1,0:T(8,128)(2,1)S(1)}, u32[]{:S(2)}, u32[]{:S(2)}) collective-permute-start(bf16[512,256]{1,0:T(8,128)(2,1)S(1)} %collective-permute-done.3.refs_2_.refs_5_.refs_8_), channel_id=1, source_target_pairs={{0,1},{1,3},{3,2},{2,0},{4,5},{5,7},{7,6},{6,4},{8,9},{9,11},{11,1... | collective-permute-start | bytes 786440 | tf_op jit(solution)/shard_map/ppermute | solution.py:356
  43.8 20.3 %copy-start.7 = (f32[1,32,1024]{2,1,0:T(8,128)S(1)}, f32[1,32,1024]{2,1,0:T(8,128)}, u32[]{:S(2)}) copy-start(f32[1,32,1024]{2,1,0:T(8,128)} %param.20) | copy-start | bytes 393220
  43.9 20.3 %copy-start.8 = (f32[1,32,1024]{2,1,0:T(8,128)S(1)}, f32[1,32,1024]{2,1,0:T(8,128)}, u32[]{:S(2)}) copy-start(f32[1,32,1024]{2,1,0:T(8,128)} %param.23) | copy-start | bytes 393220
  43.9 20.3 %copy-start.9 = (f32[1,32,1024]{2,1,0:T(8,128)S(1)}, f32[1,32,1024]{2,1,0:T(8,128)}, u32[]{:S(2)}) copy-start(f32[1,32,1024]{2,1,0:T(8,128)} %param.24) | copy-start | bytes 393220
  43.9 6.9 %collective-permute-start.19 = (bf16[32,1024]{1,0:T(8,128)(2,1)S(1)}, bf16[32,1024]{1,0:T(8,128)(2,1)S(1)}, u32[]{:S(2)}, u32[]{:S(2)}) collective-permute-start(bf16[32,1024]{1,0:T(8,128)(2,1)S(1)} %get-tuple-element.31), channel_id=1, source_target_pairs={{0,3},{1,2},{2,1},{3,0},{4,7},{5,6},{6,5},{7,4},{8,11},{9,10},{10,... | collective-permute-start | bytes 196616 | tf_op jit(solution)/shard_map/ppermute | solution.py:52
  46.8 7.1 %collective-permute-start.18 = (bf16[32,1024]{1,0:T(8,128)(2,1)S(1)}, bf16[32,1024]{1,0:T(8,128)(2,1)S(1)}, u32[]{:S(2)}, u32[]{:S(2)}) collective-permute-start(bf16[32,1024]{1,0:T(8,128)(2,1)S(1)} %get-tuple-element.32), channel_id=1, source_target_pairs={{0,2},{1,3},{2,0},{3,1},{4,6},{5,7},{6,4},{7,5},{8,10},{9,11},{10,... | collective-permute-start | bytes 196616 | tf_op jit(solution)/shard_map/ppermute | solution.py:52
  48.8 5.4 %collective-permute-start.17 = (bf16[32,1024]{1,0:T(8,128)(2,1)S(1)}, bf16[32,1024]{1,0:T(8,128)(2,1)S(1)}, u32[]{:S(2)}, u32[]{:S(2)}) collective-permute-start(bf16[32,1024]{1,0:T(8,128)(2,1)S(1)} %get-tuple-element.33), channel_id=1, source_target_pairs={{0,1},{1,0},{2,3},{3,2},{4,5},{5,4},{6,7},{7,6},{8,9},{9,8},{10,11... | collective-permute-start | bytes 196616 | tf_op jit(solution)/shard_map/ppermute | solution.py:52
  55.8 1.5 %collective-permute-start.20 = (bf16[2,48,1024]{2,1,0:T(8,128)(2,1)S(1)}, bf16[2,48,1024]{2,1,0:T(8,128)(2,1)S(1)}, u32[]{:S(2)}, u32[]{:S(2)}) collective-permute-start(bf16[2,48,1024]{2,1,0:T(8,128)(2,1)S(1)} %get-tuple-element.18), channel_id=1, source_target_pairs={{0,4},{4,0},{8,12},{12,8},{1,5},{5,1},{9,13},{13,9},{2,6},{6,2},{1... | collective-permute-start | bytes 589832 | tf_op jit(solution)/shard_map/ppermute | solution.py:52
  57.4 4.9 %collective-permute-start.21 = (bf16[1,48,1024]{2,1,0:T(8,128)(2,1)S(1)}, bf16[1,48,1024]{2,1,0:T(8,128)(2,1)S(1)}, u32[]{:S(2)}, u32[]{:S(2)}) collective-permute-start(bf16[1,48,1024]{2,1,0:T(8,128)(2,1)S(1)} %slice.94), channel_id=1, source_target_pairs={{0,8},{4,12},{8,0},{12,4},{1,9},{5,13},{9,1},{13,5},{2,10},{6,14},... | collective-permute-start | bytes 294920 | tf_op jit(solution)/shard_map/ppermute | solution.py:52
  64.9 6.2 %collective-permute-start.10 = (bf16[32,1024]{1,0:T(8,128)(2,1)S(1)}, bf16[32,1024]{1,0:T(8,128)(2,1)S(1)}, u32[]{:S(2)}, u32[]{:S(2)}) collective-permute-start(bf16[32,1024]{1,0:T(8,128)(2,1)S(1)} %bitcast.48), channel_id=1, source_target_pairs={{0,3},{1,2},{2,1},{3,0},{4,7},{5,6},{6,5},{7,4},{8,11},{9,10},{10,... | collective-permute-start | bytes 196616 | tf_op jit(solution)/shard_map/ppermute | solution.py:52
  67.3 5.6 %collective-permute-start.9 = (bf16[32,1024]{1,0:T(8,128)(2,1)S(1)}, bf16[32,1024]{1,0:T(8,128)(2,1)S(1)}, u32[]{:S(2)}, u32[]{:S(2)}) collective-permute-start(bf16[32,1024]{1,0:T(8,128)(2,1)S(1)} %bitcast.49), channel_id=1, source_target_pairs={{0,2},{1,3},{2,0},{3,1},{4,6},{5,7},{6,4},{7,5},{8,10},{9,11},{10,... | collective-permute-start | bytes 196616 | tf_op jit(solution)/shard_map/ppermute | solution.py:52
  67.3 5.6 %collective-permute-start.8 = (bf16[32,1024]{1,0:T(8,128)(2,1)S(1)}, bf16[32,1024]{1,0:T(8,128)(2,1)S(1)}, u32[]{:S(2)}, u32[]{:S(2)}) collective-permute-start(bf16[32,1024]{1,0:T(8,128)(2,1)S(1)} %bitcast.50), channel_id=1, source_target_pairs={{0,1},{1,0},{2,3},{3,2},{4,5},{5,4},{6,7},{7,6},{8,9},{9,8},{10,11... | collective-permute-start | bytes 196616 | tf_op jit(solution)/shard_map/ppermute | solution.py:52
  74.2 12.8 %copy-start.1 = (bf16[1024,2048]{1,0:T(8,128)(2,1)S(1)}, bf16[1024,2048]{1,0:T(8,128)(2,1)}, u32[]{:S(2)}) copy-start(bf16[1024,2048]{1,0:T(8,128)(2,1)} %x_ref.1) | copy-start | bytes 12582916
  74.2 7.2 %collective-permute-start.11 = (bf16[128,1024]{1,0:T(8,128)(2,1)}, bf16[128,1024]{1,0:T(8,128)(2,1)S(1)}, u32[]{:S(2)}, u32[]{:S(2)}) collective-permute-start(bf16[128,1024]{1,0:T(8,128)(2,1)} %bitcast.45), channel_id=1, source_target_pairs={{0,8},{4,12},{8,0},{12,4},{1,9},{5,13},{9,1},{13,5},{2,10},{6,14},... | collective-permute-start | bytes 786440 | tf_op jit(solution)/shard_map/ppermute | solution.py:52
  82.4 2.0 %collective-permute-start.12 = (bf16[256,1024]{1,0:T(8,128)(2,1)S(1)}, bf16[256,1024]{1,0:T(8,128)(2,1)S(1)}, u32[]{:S(2)}, u32[]{:S(2)}) collective-permute-start(bf16[256,1024]{1,0:T(8,128)(2,1)S(1)} %pad_maximum_fusion.1.refs_4_), channel_id=1, source_target_pairs={{0,4},{4,0},{8,12},{12,8},{1,5},{5,1},{9,13},{13,9},{2,6},{6,2},{1... | collective-permute-start | bytes 1572872 | tf_op jit(solution)/shard_map/ppermute | solution.py:52
  88.7 2.4 %collective-permute-start.13 = (bf16[2,1024,128]{2,1,0:T(8,128)(2,1)S(1)}, bf16[2,1024,128]{2,1,0:T(8,128)(2,1)S(1)}, u32[]{:S(2)}, u32[]{:S(2)}) collective-permute-start(bf16[2,1024,128]{2,1,0:T(8,128)(2,1)S(1)} %get-tuple-element.14), channel_id=1, source_target_pairs={{0,4},{4,0},{8,12},{12,8},{1,5},{5,1},{9,13},{13,9},{2,6},{6,2},{1... | collective-permute-start | bytes 1572872 | tf_op jit(solution)/shard_map/ppermute | solution.py:52
  90.7 2.1 %collective-permute-start.15 = (bf16[2,1024,128]{2,1,0:T(8,128)(2,1)S(1)}, bf16[2,1024,128]{2,1,0:T(8,128)(2,1)S(1)}, u32[]{:S(2)}, u32[]{:S(2)}) collective-permute-start(bf16[2,1024,128]{2,1,0:T(8,128)(2,1)S(1)} %get-tuple-element.16), channel_id=1, source_target_pairs={{0,4},{4,0},{8,12},{12,8},{1,5},{5,1},{9,13},{13,9},{2,6},{6,2},{1... | collective-permute-start | bytes 1572872 | tf_op jit(solution)/shard_map/ppermute | solution.py:52
  91.3 12.9 %collective-permute-start.14 = (bf16[1,1024,128]{2,1,0:T(8,128)(2,1)S(1)}, bf16[1,1024,128]{2,1,0:T(8,128)(2,1)S(1)}, u32[]{:S(2)}, u32[]{:S(2)}) collective-permute-start(bf16[1,1024,128]{2,1,0:T(8,128)(2,1)S(1)} %slice.93), channel_id=1, source_target_pairs={{0,8},{4,12},{8,0},{12,4},{1,9},{5,13},{9,1},{13,5},{2,10},{6,14},... | collective-permute-start | bytes 786440 | tf_op jit(solution)/shard_map/ppermute | solution.py:52
  93.0 12.4 %copy-start.4 = (f32[1,2048,128]{2,1,0:T(8,128)S(1)}, f32[1,2048,128]{2,1,0:T(8,128)}, u32[]{:S(2)}) copy-start(f32[1,2048,128]{2,1,0:T(8,128)} %param.19) | copy-start | bytes 3145732
  93.0 12.4 %copy-start.5 = (f32[1,2048,128]{2,1,0:T(8,128)S(1)}, f32[1,2048,128]{2,1,0:T(8,128)}, u32[]{:S(2)}) copy-start(f32[1,2048,128]{2,1,0:T(8,128)} %param.21) | copy-start | bytes 3145732
  93.0 12.4 %copy-start.6 = (f32[1,2048,128]{2,1,0:T(8,128)S(1)}, f32[1,2048,128]{2,1,0:T(8,128)}, u32[]{:S(2)}) copy-start(f32[1,2048,128]{2,1,0:T(8,128)} %param.22) | copy-start | bytes 3145732
  93.0 12.3 %collective-permute-start.16 = (bf16[1,1024,128]{2,1,0:T(8,128)(2,1)S(1)}, bf16[1,1024,128]{2,1,0:T(8,128)(2,1)S(1)}, u32[]{:S(2)}, u32[]{:S(2)}) collective-permute-start(bf16[1,1024,128]{2,1,0:T(8,128)(2,1)S(1)} %slice.92), channel_id=1, source_target_pairs={{0,8},{4,12},{8,0},{12,4},{1,9},{5,13},{9,1},{13,5},{2,10},{6,14},... | collective-permute-start | bytes 786440 | tf_op jit(solution)/shard_map/ppermute | solution.py:52
  (2 other events, 7.9 us)

commit v2 on v0

v2 whole, which is shorter than its diff:
```python
import functools

import jax
import jax.numpy as jnp
from jax import lax
from jax.experimental import pallas as pl
from jax.experimental.pallas import tpu as pltpu
from jax.sharding import PartitionSpec as P

adapter_alpha_scale = 16.0
beta_one = 0.9
beta_two = 0.999
adam_eps = 1e-08
learn_rate = 0.001
adam_step = 10
half = jnp.bfloat16
wide = jnp.float32
MIB = 1 << 20
NT = (((1,), (1,)), ((), ()))
TN = (((0,), (0,)), ((), ()))
NN = (((1,), (0,)), ((), ()))


def mm(a, b, dims):
    return lax.dot_general(a, b, dims, preferred_element_type=wide)


def moment_update_rule(param, first, second, grad):
    new_first = beta_one * first + (1.0 - beta_one) * grad
    new_second = beta_two * second + (1.0 - beta_two) * grad * grad
    fixed_first = new_first / (1.0 - beta_one**adam_step)
    fixed_second = new_second / (1.0 - beta_two**adam_step)
    return (
        param - learn_rate * fixed_first / (jnp.sqrt(fixed_second) + adam_eps),
        new_first,
        new_second,
    )


def bit_order(n):
    if n == 1:
        return [0]
    inner = [2 * i for i in bit_order(n // 2)]
    return inner + [i + 1 for i in inner]


def line_ring(n):
    return [0] + list(range(1, n, 2)) + list(range(n - 2 + n % 2, 0, -2))


def swap(v, axis, n, bits):
    return lax.ppermute(v, axis, [(i, i ^ bits) for i in range(n)])


def kernel_params(mib):
    return pltpu.CompilerParams(vmem_limit_bytes=mib * MIB)


def cost(flops, nbytes):
    return pl.CostEstimate(flops=int(flops), bytes_accessed=int(nbytes), transcendentals=0)


def block_table(refs, b, d):
    tenant_ref, slot_ref, rank_ref = refs
    tenant = tenant_ref[b]
    return jnp.bitwise_xor(slot_ref[tenant], d), rank_ref[tenant]


def inverse_rank(rank, shape):
    return adapter_alpha_scale / jnp.full(shape, rank, jnp.int32).astype(wide)


def sources(z, n):
    ring = line_ring(n)
    out = []
    for i in range(n):
        came = [ring[(ring.index(k) - i) % n] for k in range(n)]
        at = came[0]
        for k in range(1, n):
            at = jnp.where(z == k, came[k], at)
        out.append(at)
    return out


def smem():
    return pl.BlockSpec(memory_space=pltpu.SMEM)


def resident(a):
    return pl.BlockSpec(a.shape, lambda *_, n=len(a.shape): (0,) * n)


def vmem():
    return pl.BlockSpec(memory_space=pltpu.VMEM)


def starts_of(live_ref):
    starts, at = [], 0
    for b in range(live_ref.shape[0]):
        starts.append(at)
        at = at + live_ref[b]
    return starts, at


def stage_kernel(from_ref, to_ref, sem):
    copy = pltpu.make_async_copy(from_ref, to_ref, sem)
    copy.start()
    copy.wait()


def stage_call(a):
    return pl.pallas_call(
        stage_kernel,
        in_specs=[pl.BlockSpec(memory_space=pl.ANY)],
        out_specs=vmem(),
        out_shape=jax.ShapeDtypeStruct(a.shape, a.dtype),
        scratch_shapes=[pltpu.SemaphoreType.DMA],
        compiler_params=kernel_params(16),
        cost_estimate=cost(0, 4 * a.size),
        name="stage",
    )(a)


def round_kernel(a_ref, out_ref):
    out_ref[...] = a_ref[0].T.astype(half)


def round_call(a):
    _, width, ranks = a.shape
    blk = width
    return pl.pallas_call(
        round_kernel,
        grid=(width // blk,),
        in_specs=[pl.BlockSpec((1, blk, ranks), lambda i: (0, i, 0))],
        out_specs=pl.BlockSpec((ranks, blk), lambda i: (0, i)),
        out_shape=jax.ShapeDtypeStruct((ranks, width), half),
        compiler_params=kernel_params(16),
        cost_estimate=cost(0, 6 * a.size),
        name="round_factors",
    )(a)


def compact_kernel(live_ref, b_ref, cot_ref, up_ref, first_ref, rest_ref, all_ref):
    up_ref[...] = b_ref[0].astype(half)
    blocks = live_ref.shape[0]
    blk_len = cot_ref.shape[0] // blocks
    starts, _ = starts_of(live_ref)
    all_ref[...] = jnp.zeros_like(all_ref)
    panels, _, lanes = all_ref.shape
    row = lax.broadcasted_iota(jnp.int32, (blk_len, lanes), 0)
    for b in range(blocks):
        for p in range(panels):
            piece = cot_ref[b * blk_len : (b + 1) * blk_len, p * lanes : (p + 1) * lanes].astype(wide)
            all_ref[p, pl.ds(starts[b], blk_len), :] = jnp.where(row < live_ref[b], piece, 0.0)
    room = first_ref.shape[0]
    for p in range(panels):
        cols = slice(p * lanes, (p + 1) * lanes)
        first_ref[:, cols] = all_ref[p, :room, :].astype(half)
        rest_ref[0, :, cols] = all_ref[p, room:, :].astype(half)


def compact_call(live, b, cot, room, copies):
    tok, kw = cot.shape
    shapes = [
        jax.ShapeDtypeStruct(b.shape[1:], half),
        jax.ShapeDtypeStruct((room, kw), half),
        jax.ShapeDtypeStruct((copies, tok - room, kw), half),
    ]
    specs = [resident(shapes[0]), resident(shapes[1]), pl.BlockSpec((1, tok - room, kw), lambda i: (0, 0, 0))]
    return pl.pallas_call(
        compact_kernel,
        grid=(1,),
        in_specs=[smem(), resident(b), resident(cot)],
        out_specs=specs,
        out_shape=shapes,
        scratch_shapes=[pltpu.VMEM((kw // min(kw, 128), tok, min(kw, 128)), wide)],
        compiler_params=kernel_params(56),
        cost_estimate=cost(0, 4 * tok * kw),
        name="compact",
    )(live, b, cot)


def ordered_kernel(z_ref, *refs):
    out_ref = refs[-1]
    own = refs[0].shape[0]
    for k, ref in enumerate(refs[:-1]):
        at = pl.multiple_of(jnp.bitwise_xor(z_ref[0], k) * own, own)
        out_ref[pl.ds(at, own), :] = ref[...]


def ordered_call(z, pieces):
    own, cols = pieces[0].shape
    n = len(pieces)
    if own % 16:
        return jnp.stack(pieces)[jnp.bitwise_xor(z[0], jnp.arange(n))].reshape(n * own, cols)
    return pl.pallas_call(
        ordered_kernel,
        in_specs=[smem()] + [vmem()] * n,
        out_specs=vmem(),
        out_shape=jax.ShapeDtypeStruct((n * own, cols), half),
        compiler_params=kernel_params(16),
        cost_estimate=cost(0, 4 * n * own * cols),
        name="ordered",
    )(z, *pieces)


def hidden_kernel(order, groups, d_ref, z_ref, live_ref, *refs):
    tables, x_ref, a_refs = refs[:3], refs[3], refs[4 : 4 + len(order)]
    out_refs, (all_ref, prod_ref, rows_ref, flat_ref) = refs[4 + len(order) : -4], refs[-4:]
    ranks = a_refs[0].shape[0]
    step = pl.program_id(0)

    @pl.when(step == 0)
    def _():
        for i, ref in enumerate(a_refs):
            all_ref[i * ranks : (i + 1) * ranks, :] = ref[...]

    blk = prod_ref.shape[0]
    prod_ref[...] = mm(x_ref[pl.ds(pl.multiple_of(step * blk, blk), blk), :], all_ref[...], NT)
    blocks = live_ref.shape[0]
    blk_len = rows_ref.shape[0] // blocks
    per_step = blk // blk_len
    first = step * per_step
    start = jnp.int32(0)
    for b in range(blocks):
        start = start + jnp.where(b < first, live_ref[b], 0)
    for b in range(per_step):
        near, _ = block_table(tables, first + b, d_ref[0])
        at = jnp.int32(0)
        for i, j in enumerate(order):
            at = jnp.where(near == j, i, at)
        cols = pl.ds(pl.multiple_of(at * ranks, ranks), ranks)
        rows_ref[pl.ds(start, blk_len), :] = prod_ref[b * blk_len : (b + 1) * blk_len, cols]
        start = start + live_ref[first + b]

    @pl.when(step == pl.num_programs(0) - 1)
    def _():
        flat_ref[...] = rows_ref[...].T
        own = ranks // groups
        for k, out_ref in enumerate(out_refs):
            at = pl.multiple_of(jnp.bitwise_xor(z_ref[0], k) * own, own)
            out_ref[...] = flat_ref[pl.ds(at, own), :].astype(half)


def hidden_call(d, z, live, tables, x, downs, order, groups):
    tok, width = x.shape
    ranks = downs[0].shape[0]
    blk = min(256, tok)
    own = ranks // groups
    shape = jax.ShapeDtypeStruct((own, tok), half)
    return pl.pallas_call(
        functools.partial(hidden_kernel, order, groups),
        grid=(tok // blk,),
        in_specs=[smem()] * 6
        + [vmem()]
        + [resident(a) for a in downs],
        out_specs=[resident(shape)] * groups,
        out_shape=[shape] * groups,
        scratch_shapes=[
            pltpu.VMEM((len(downs) * ranks, width), half),
            pltpu.VMEM((blk, len(downs) * ranks), wide),
            pltpu.VMEM((tok, ranks), wide),
            pltpu.VMEM((ranks, tok), wide),
        ],
        compiler_params=kernel_params(24),
        cost_estimate=cost(2 * tok * width * ranks * len(order), 2 * (x.size + 4 * downs[0].size)),
        name="hidden",
    )(d, z, live, *tables, x, *downs)


def upward_kernel(order, parts, d_ref, z_ref, live_ref, *refs):
    tables, cots, rest_ref = refs[:3], refs[3 : 3 + parts], refs[3 + parts]
    b_refs = refs[4 + parts : -5]
    full_ref, packed_ref, all_ref, acc_ref, rows_ref = refs[-5:]
    ranks = b_refs[0].shape[0]
    room, kw = cots[0].shape
    for i, ref in enumerate(b_refs):
        all_ref[i * ranks : (i + 1) * ranks, :] = ref[...]

    src = sources(z_ref[0], parts)

    def product(at, rows, pieces):
        acc = None
        for i, piece in enumerate(pieces):
            cols = pl.ds(pl.multiple_of(src[i] * kw, kw), kw)
            prod = mm(piece, all_ref[:, cols], NT)
            acc = prod if acc is None else acc + prod
        for i in range(len(order)):
            acc_ref[i, at : at + rows, :] = acc[:, i * ranks : (i + 1) * ranks]

    product(0, room, [ref[...] for ref in cots])
    starts, total = starts_of(live_ref)

    @pl.when(total > room)
    def _():
        product(room, rest_ref.shape[1], [rest_ref[i] for i in range(parts)])

    blocks = live_ref.shape[0]
    blk_len = full_ref.shape[0] // blocks
    rank_at = lax.broadcasted_iota(jnp.int32, (1, ranks), 1)
    row = lax.broadcasted_iota(jnp.int32, (blk_len, ranks), 0)
    for b in range(blocks):
        near, rank = block_table(tables, b, d_ref[0])
        scale = jnp.where(rank_at < rank, inverse_rank(rank, (1, ranks)), 0.0)
        for i, j in enumerate(order):
            cols = slice(i * ranks, (i + 1) * ranks)
            piece = acc_ref[i, pl.ds(starts[b], blk_len), :] * jnp.where(near == j, scale, 0.0)
            piece = jnp.where(row < live_ref[b], piece, 0.0)
            full_ref[b * blk_len : (b + 1) * blk_len, cols] = piece.astype(half)
            rows_ref[i, pl.ds(starts[b], blk_len), :] = piece
    for i in range(len(order)):
        packed_ref[:, i * ranks : (i + 1) * ranks] = rows_ref[i].astype(half)


def upward_call(d, z, live, tables, cots, rest, ups, order):
    ranks, value_width = ups[0].shape
    every = len(ups) * ranks
    tok = cots[0].shape[0] + rest.shape[1]
    shape = jax.ShapeDtypeStruct((tok, every), half)
    return pl.pallas_call(
        functools.partial(upward_kernel, order, len(cots)),
        in_specs=[smem()] * 6 + [vmem()] * (len(cots) + 1 + len(ups)),
        out_specs=[vmem()] * 2,
        out_shape=[shape, shape],
        scratch_shapes=[
            pltpu.VMEM((every, value_width), half),
            pltpu.VMEM((len(ups), tok, ranks), wide),
            pltpu.VMEM((len(ups), tok, ranks), wide),
        ],
        compiler_params=kernel_params(24),
        cost_estimate=cost(2 * tok * value_width * every, 2 * (tok * value_width + 2 * every * value_width)),
        name="upward",
    )(d, z, live, *tables, *cots, rest, *ups)


def down_kernel(ranks, start, x_ref, u_ref, keep_ref, send_ref):
    blk = keep_ref.shape[1]
    cols = pl.ds(pl.multiple_of(start + pl.program_id(0) * blk, blk), blk)
    acc = mm(x_ref[:, cols], u_ref[...], TN)
    per = keep_ref.shape[0]
    for i in range(per):
        keep_ref[i] = acc[:, i * ranks : (i + 1) * ranks].astype(half)
        send_ref[i] = acc[:, (per + i) * ranks : (per + i + 1) * ranks].astype(half)


def down_call(x, u, ranks, start, count):
    tok = x.shape[0]
    slots = u.shape[1] // ranks
    blk = min(512, count)
    shape = jax.ShapeDtypeStruct((slots // 2, count, ranks), half)
    return pl.pallas_call(
        functools.partial(down_kernel, ranks, start),
        grid=(count // blk,),
        in_specs=[vmem(), vmem()],
        out_specs=[pl.BlockSpec((slots // 2, blk, ranks), lambda i: (0, i, 0))] * 2,
        out_shape=[shape, shape],
        compiler_params=kernel_params(24),
        cost_estimate=cost(2 * tok * count * slots * ranks, 2 * (tok * count + slots * ranks * (tok + count))),
        name="down_grad",
    )(x, u)


def up_kernel(order, parts, n_hs, tail_rows, d_ref, z_ref, live_ref, *refs):
    tables, hs = refs[:3], refs[3 : 3 + n_hs]
    cots, rest_ref = refs[3 + n_hs : 3 + n_hs + parts], refs[3 + n_hs + parts]
    keep_ref, send_ref, acc_ref = refs[-3:]
    own, tok = hs[0].shape
    per = len(order) // 2
    blocks = live_ref.shape[0]
    total = hs[0][...].astype(wide)
    for h in hs[1:]:
        total = total + h[...].astype(wide)
    starts, live_rows = starts_of(live_ref)
    lane = lax.broadcasted_iota(jnp.int32, (1, tok), 1)
    slot = jnp.zeros((1, tok), jnp.int32)
    rank = jnp.ones((1, tok), jnp.int32)
    counts = [jnp.int32(0) for _ in order]
    for b in range(blocks):
        near, rank_b = block_table(tables, b, d_ref[0])
        slot = jnp.where(lane >= starts[b], near, slot)
        rank = jnp.where(lane >= starts[b], rank_b, rank)
        counts = [c + jnp.where(near == j, live_ref[b], 0) for c, j in zip(counts, order)]
    src = sources(z_ref[0], parts)
    rank_at = z_ref[0] * own + lax.broadcasted_iota(jnp.int32, total.shape, 0)
    scale = adapter_alpha_scale / rank.astype(wide)
    total = jnp.where((rank_at < rank) & (lane < live_rows), total * scale, 0.0)
    lhs = jnp.concatenate([jnp.where(slot == j, total, 0.0).astype(half) for j in order], axis=0)
    room, kw = cots[0].shape
    for i in range(parts):
        cols = pl.ds(pl.multiple_of(src[i] * kw, kw), kw)
        acc_ref[:, cols] = mm(lhs[:, :room], cots[i][...], NN)

    @pl.when(live_rows > room)
    def _():
        for i in range(parts):
            cols = pl.ds(pl.multiple_of(src[i] * kw, kw), kw)
            acc_ref[:, cols] = acc_ref[:, cols] + mm(lhs[:, room:], rest_ref[i], NN)

    row = lax.broadcasted_iota(jnp.int32, (tail_rows, keep_ref.shape[2]), 0)
    for k in range(per):
        for ref, at in ((keep_ref, k), (send_ref, per + k)):
            ref[k, :own, :] = acc_ref[at * own : (at + 1) * own, :].astype(half)
            tail = jnp.where(row == 0, counts[at] // 32, jnp.where(row == 1, counts[at] % 32, 0))
            ref[k, own:, :] = tail.astype(wide).astype(half)


def up_call(d, z, live, tables, hs, cots, rest, order, tail_rows=16):
    own, tok = hs[0].shape
    parts = len(cots)
    width = parts * cots[0].shape[1]
    shape = jax.ShapeDtypeStruct((len(order) // 2, own + tail_rows, width), half)
    return pl.pallas_call(
        functools.partial(up_kernel, order, parts, len(hs), tail_rows),
        in_specs=[smem()] * 6 + [vmem()] * (len(hs) + len(cots) + 1),
        out_specs=[vmem()] * 2,
        out_shape=[shape, shape],
        scratch_shapes=[pltpu.VMEM((len(order) * own, width), wide)],
        compiler_params=kernel_params(24),
        cost_estimate=cost(2 * len(order) * own * tok * width, 4 * tok * width),
        name="up_grad",
    )(d, z, live, *tables, *hs, *cots, rest)


def up_plain(d, z, live, tables, hs, cots, rest, order, tail_rows=16):
    tenant, slot_of, rank_of = tables
    own, tok = hs[0].shape
    room = tok - rest.shape[1]
    pick = tenant[:, None] == jnp.arange(slot_of.shape[0])[None, :]
    near = jnp.bitwise_xor(jnp.sum(jnp.where(pick, slot_of[None, :], 0), axis=1), d)
    rank = jnp.sum(jnp.where(pick, rank_of[None, :], 0), axis=1)
    ends = jnp.cumsum(live)
    lane = jnp.arange(tok, dtype=jnp.int32)[None, :]
    mine = (lane >= (ends - live)[:, None]) & (lane < ends[:, None])
    slot = jnp.sum(jnp.where(mine, near[:, None], 0), axis=0)[None, :]
    rank = jnp.maximum(jnp.sum(jnp.where(mine, rank[:, None], 0), axis=0), 1)[None, :]
    total = sum(h.astype(wide) for h in hs)
    rank_at = z * own + jnp.arange(own, dtype=jnp.int32)[:, None]
    total = total * (adapter_alpha_scale / rank.astype(wide))
    total = jnp.where((rank_at < rank) & (lane < ends[-1]), total, 0.0)
    lhs = jnp.concatenate([jnp.where(slot == j, total, 0).astype(half) for j in order], axis=0)
    cot = [jnp.concatenate(cots, axis=1)]
    cot.append(jnp.where(ends[-1] > room, jnp.concatenate(list(rest), axis=1), 0))
    cot = jnp.concatenate(cot, axis=0)
    grads = mm(lhs, cot, NN).astype(half).reshape(len(order), own, cot.shape[1])
    counts = jnp.sum(jnp.where(near[:, None] == jnp.array(order)[None, :], live[:, None], 0), axis=0)
    tail = jnp.pad(jnp.stack([counts // 32, counts % 32], axis=1), ((0, 0), (0, tail_rows - 2)))
    tail = jnp.broadcast_to(tail.astype(half)[:, :, None], (len(order), tail_rows, cot.shape[1]))
    both = jnp.concatenate([grads, tail], axis=1)
    return both[: len(order) // 2], both[len(order) // 2 :]


def base_kernel(parts, z_ref, live_ref, w_ref, *refs):
    cots, out_ref = refs[:-1], refs[-1]
    room, kw = cots[0].shape
    _, total = starts_of(live_ref)
    src = sources(z_ref[0], parts)
    blk = out_ref.shape[1] // pl.num_programs(0)
    cols = pl.ds(pl.multiple_of(pl.program_id(0) * blk, blk), blk)
    tile = min(256, room)
    for at in range(0, room, tile):

        @pl.when(at < total)
        def _(at=at):
            acc = None
            for i, cot in enumerate(cots):
                w = w_ref[cols, pl.ds(pl.multiple_of(src[i] * kw, kw), kw)]
                prod = mm(cot[at : at + tile, :], w, NT)
                acc = prod if acc is None else acc + prod
            out_ref[at : at + tile, cols] = acc


def base_call(z, live, w, cots, parts):
    room, kw = cots[0].shape
    width = w.shape[0]
    blk = min(512, width)
    return pl.pallas_call(
        functools.partial(base_kernel, parts),
        grid=(width // blk,),
        in_specs=[smem(), smem(), vmem()] + [vmem()] * len(cots),
        out_specs=vmem(),
        out_shape=jax.ShapeDtypeStruct((room, width), wide),
        compiler_params=kernel_params(16),
        cost_estimate=cost(2 * room * width * kw * len(cots), 4 * room * width),
        name="base",
    )(z, live, w, *cots)


def acts_kernel(parts, early, z_ref, live_ref, w_ref, u_ref, base_ref, rest_ref, *refs):
    cots, a_refs = refs[: parts - early], refs[parts - early : -3]
    out_ref, all_ref, acc_ref = refs[-3:]
    room, kw = cots[0].shape
    ranks = a_refs[0].shape[0]
    starts, total = starts_of(live_ref)
    src = sources(z_ref[0], parts)
    for i, ref in enumerate(a_refs):
        all_ref[i * ranks : (i + 1) * ranks, :] = ref[...]
    tok, blk = out_ref.shape
    cols = pl.ds(pl.multiple_of(pl.program_id(0) * blk, blk), blk)
    panels, _, lanes = acc_ref.shape

    def product(at, rows, acc, pieces):
        acc_u = mm(u_ref[at : at + rows, :], all_ref[...], NN)
        acc = acc_u if acc is None else acc + acc_u
        for i, piece in pieces:
            w = w_ref[cols, pl.ds(pl.multiple_of(src[i] * kw, kw), kw)]
            acc = acc + mm(piece, w, NT)
        for p in range(panels):
            acc_ref[p, at : at + rows, :] = acc[:, p * lanes : (p + 1) * lanes]

    tile = min(256, room)
    for at in range(0, room, tile):

        @pl.when(at < total)
        def _(at=at):
            first = base_ref[at : at + tile, cols] if early else None
            product(at, tile, first, [(early + i, cot[at : at + tile, :]) for i, cot in enumerate(cots)])

    @pl.when(total > room)
    def _():
        product(room, tok - room, None, [(i, rest_ref[i]) for i in range(parts)])

    blocks = live_ref.shape[0]
    blk_len = tok // blocks
    row = lax.broadcasted_iota(jnp.int32, (blk_len, lanes), 0)
    for b in range(blocks):
        for p in range(panels):
            piece = acc_ref[p, pl.ds(starts[b], blk_len), :]
            piece = jnp.where(row < live_ref[b], piece, 0.0)
            out_ref[b * blk_len : (b + 1) * blk_len, p * lanes : (p + 1) * lanes] = piece.astype(half)


def acts_call(z, live, w, u, base, cots, rest, downs):
    width, kfull = w.shape
    tok, every = u.shape
    ranks = downs[0].shape[0]
    blk = min(512, width)
    parts = rest.shape[0]
    return pl.pallas_call(
        functools.partial(acts_kernel, parts, parts - len(cots)),
        grid=(width // blk,),
        in_specs=[smem(), smem(), vmem(), vmem(), vmem(), vmem()]
        + [vmem()] * len(cots)
        + [pl.BlockSpec((ranks, blk), lambda i: (0, i))] * len(downs),
        out_specs=pl.BlockSpec((tok, blk), lambda i: (0, i)),
        out_shape=jax.ShapeDtypeStruct((tok, width), half),
        scratch_shapes=[
            pltpu.VMEM((every, blk), half),
            pltpu.VMEM((blk // 128, tok, 128), wide),
        ],
        compiler_params=kernel_params(24),
        cost_estimate=cost(2 * tok * width * (kfull + every), 2 * (w.size + every * width + tok * (width + kfull))),
        name="grad_acts",
    )(z, live, w, u, base, rest, *cots, *downs)


def together(*values):
    return lax.optimization_barrier(values)


def after(value, *others):
    return lax.optimization_barrier((value, *others))[0]


def shards(
    n_dp,
    n_tensor,
    activations,
    output_gradient,
    value_weight,
    adapter_down_factors,
    adapter_up_factors,
    down_first_moment,
    down_second_moment,
    up_first_moment,
    up_second_moment,
    block_tenant,
    block_live_tokens,
    tenant_storage_slot,
    tenant_adapter_rank,
):
    tok, width = activations.shape
    live = block_live_tokens
    slots = tenant_storage_slot.shape[0]
    assert adapter_down_factors.shape[0] == 1 and slots == n_dp
    ranks = adapter_down_factors.shape[2]
    own_ranks = adapter_up_factors.shape[1]
    kw = output_gradient.shape[1]
    z = lax.axis_index("tensor").astype(jnp.int32)
    d = lax.axis_index("dp").astype(jnp.int32)
    z_one, d_one = z[None], d[None]
    order = bit_order(slots)
    levels = [1 << b for b in range(slots.bit_length() - 1)]
    tables = (block_tenant, tenant_storage_slot, tenant_adapter_rank)
    ring = line_ring(n_tensor)
    ring_pairs = [(ring[i], ring[(i + 1) % n_tensor]) for i in range(n_tensor)]

    def onward(v):
        return lax.ppermute(v, "tensor", ring_pairs)

    room = tok * 3 // 4
    own_b, first, rest = compact_call(live, adapter_up_factors, output_gradient, room, n_tensor)

    def rest_of(v):
        out = [v[0]]
        for _ in range(n_tensor - 1):
            out.append(onward(out[-1]))
        return jnp.stack(out)

    cots = [first, onward(first)]
    ups = [own_b, swap(own_b, "tensor", n_tensor, 1)]
    own_a = round_call(after(adapter_down_factors, first))
    x = stage_call(after(activations, first))
    weight = stage_call(after(value_weight, first))

    cots[1], own_a, ups[1], x, weight = together(cots[1], own_a, ups[1], x, weight)
    cots.append(onward(cots[1]))
    bits = 2
    while bits < n_tensor:
        ups = ups + [swap(v, "tensor", n_tensor, bits) for v in ups]
        bits *= 2
    far = list(reversed(levels))
    downs = [own_a]
    for bits in far[:-1]:
        downs = downs + [swap(v, "dp", n_dp, bits) for v in downs]
    rest = lax.cond(jnp.sum(live) > room, rest_of, lambda v: v, after(rest, cots[1]))
    early = 2 if kw % 128 == 0 and n_tensor > 2 else 0
    base = base_call(z_one, live, weight, cots[:early], n_tensor) if early else jnp.zeros((8, 128), wide)

    cots[2], rest, base, *both = together(cots[2], rest, base, *downs, *ups)
    downs, ups = both[: len(downs)], both[len(downs) :]
    while len(cots) < n_tensor:
        cots.append(onward(cots[-1]))
    downs = downs + [swap(v, "dp", n_dp, far[-1]) for v in downs]
    ups = [ordered_call(z_one, ups)]
    for bits in far[:-1]:
        ups = ups + [swap(v, "dp", n_dp, bits) for v in ups]
    hs = list(hidden_call(d_one, z_one, live, tables, x, downs, order, n_tensor))

    hs = [hs[0]] + [swap(hs[k], "tensor", n_tensor, k) for k in range(1, n_tensor)]
    cots[-1], *both = together(cots[-1], *hs, *ups)
    hs, ups = both[: len(hs)], both[len(hs) :]
    ups = ups + [swap(v, "dp", n_dp, far[-1]) for v in ups]
    if kw % 128:
        at = jnp.array([ring.index(i) for i in range(n_tensor)], jnp.int32)
        away = (at[z] - at) % n_tensor
        in_order = lambda v: jnp.moveaxis(v[away], 0, 1).reshape(v.shape[1], n_tensor * kw)
        cots = [in_order(jnp.stack(cots))]
        rest = in_order(rest)[None]
    u, packed_u = upward_call(d_one, z_one, live, tables, cots, rest, ups, order)

    def other_sums(total, *others):
        for bits in levels[1:]:
            n = total.shape[0] // 2
            got = after(swap(total[n:].astype(half), "dp", n_dp, bits), *others)
            total = total[:n] + got.astype(wide)
        return total[0]

    rows = width // 2
    keep_0, send_0 = down_call(x, u, ranks, 0, rows)
    got_0 = swap(send_0, "dp", n_dp, 1)
    keep_1, send_1 = down_call(x, after(u, send_0), ranks, rows, rows)
    got_1 = swap(send_1, "dp", n_dp, 1)
    hs[0] = after(hs[0], send_1)
    if own_ranks % 16:
        keep_up, send_up = up_plain(d, z, live, tables, hs, cots, rest, order)
    else:
        keep_up, send_up = up_call(d_one, z_one, live, tables, hs, cots, rest, order)
    got_up = swap(send_up, "dp", n_dp, 1)
    down_0 = keep_0.astype(wide) + after(got_0, send_up).astype(wide)
    down_1 = keep_1.astype(wide) + after(got_1, down_0).astype(wide)
    up_sum = keep_up.astype(wide) + after(got_up, down_1).astype(wide)
    grad_acts = acts_call(
        z_one, live, weight, after(packed_u, down_1, up_sum), base, cots[early:], rest, downs
    )
    up_sum = other_sums(up_sum, grad_acts)
    denom = jnp.maximum(up_sum[own_ranks, 0] * 32.0 + up_sum[own_ranks + 1, 0], 1.0)

    up_grad = up_sum[None, :own_ranks] / denom
    new_up = moment_update_rule(adapter_up_factors, up_first_moment, up_second_moment, up_grad)
    down_sums = [other_sums(down_0, grad_acts), other_sums(down_1, grad_acts)]
    down_grad = jnp.concatenate(down_sums, axis=0)[None] / denom
    new_down = moment_update_rule(adapter_down_factors, down_first_moment, down_second_moment, down_grad)
    return (grad_acts, *new_down, *new_up)


def solution(mesh):
    tokens = P(("groups", "dp"), "tensor")
    factors = P(("groups", "dp"), "tensor", None)
    placed = (tokens, tokens, P("tensor", None), *([factors] * 6), P(("groups", "dp")), P(("groups", "dp")), P("groups"), P("groups"))
    return jax.shard_map(
        functools.partial(shards, mesh.shape["dp"], mesh.shape["tensor"]),
        mesh=mesh,
        in_specs=placed,
        out_specs=(tokens, *([factors] * 6)),
        check_vma=False,
    )
```

time: 233 us -> 84.3 us (0.36)
  waiting for transfers between devices: 102 us -> 15.2 us
  matrix products: 57.1 us -> 0 us
  blocking collectives: 27.3 us -> 0 us
  Pallas kernels: 0 us -> 24 us
  starting transfers between devices: 0.6 us -> 21.1 us
  between operations: 14.6 us -> 3.2 us
  local copies, waits for them, and re-layouts: 22.4 us -> 16.5 us
  other arithmetic: 8.26 us -> 3.94 us
    all_gather x2 -> x0, waiting for transfers between devices: 64.3 us -> none  [the longest x1 41.9 us: shards(): cot_full = lax.all_gather(output_gradient, 'tensor', axis=1, tiled=True)]
    dot_general x10 -> x0, matrix products: 57.1 us -> none  [the longest x1 11.9 us: shards(): jnp.einsum('bpr,bdr->bpd', full_u, used_a, preferred_element_type=jnp.flo...]
    reduce_scatter x3 -> x0, waiting for transfers between devices: 37.4 us -> none  [the longest x1 21.2 us: shards(): lax.psum_scatter(part_a.astype(jnp.bfloat16), 'dp', scatter_dimension=0,...]
    pallas_call x0 -> x12, Pallas kernels: none -> 24 us  [the longest x1 6.56 us: acts_call(): pl.pallas_call(functools.partial(acts_kernel, parts, parts - len(cots)),...]
    all_gather x2 -> x0, blocking collectives: 21.5 us -> none  [the longest x1 14.3 us: shards(): lax.all_gather(scaled_u, 'tensor', axis=1, tiled=True)]
    ppermute x0 -> x21, starting transfers between devices: none -> 21.1 us  [the longest x18 17.8 us: swap(): return lax.ppermute(v, axis, [(i, i ^ bits) for i in range(n)])]
    dot_general x1 -> x0, local copies, waits for them, and re-layouts: 17.7 us -> none  [shards(): jnp.einsum('bpd,bpr->bdr', x_blocks, full_u, preferred_element_type=jnp.f...]
    unnamed x20 -> x52, local copies, waits for them, and re-layouts: 0.06 us -> 15.9 us
  transfers between devices with their start and end apart: 5 -> 21, of which waited for: 5 -> 10; matrix products, arithmetic and copies ran while one was open for 11% -> 3% of each run, Pallas kernels for 0% -> 22%
where the time goes in v2:
time: 84.3 us; the launch traced here: 83.9 us
  Pallas kernels  24 us (28%)
  starting transfers between devices  21.1 us (25%)
  local copies, waits for them, and re-layouts  16.5 us (20%)
  waiting for transfers between devices  15.2 us (18%)
  other arithmetic  3.94 us (5%)
  between operations  3.2 us (4%)
    ppermute x18, starting transfers between devices, swap(): return lax.ppermute(v, axis, [(i, i ^ bits) for i in range(n)])  17.8 us
    unnamed x52, local copies, waits for them, and re-layouts  15.9 us
    ppermute x18, waiting for transfers between devices, swap(): return lax.ppermute(v, axis, [(i, i ^ bits) for i in range(n)])  15.2 us
    pallas_call x1, Pallas kernels, acts_call(): pl.pallas_call(functools.partial(acts_kernel, parts, parts - len(cots)),...  6.56 us
    pallas_call x1, Pallas kernels, hidden_call(): pl.pallas_call(functools.partial(hidden_kernel, order, groups), grid=(tok...  4.81 us
    pallas_call x1, Pallas kernels, base_call(): pl.pallas_call(functools.partial(base_kernel, parts), grid=(width // blk,...  3.37 us
    ppermute x3, starting transfers between devices, onward(): return lax.ppermute(v, 'tensor', ring_pairs)  3.25 us
    pallas_call x2, Pallas kernels, down_call(): pl.pallas_call(functools.partial(down_kernel, ranks, start), grid=(count...  3.16 us
  transfers between devices with their start and end apart: 21, of which 10 were waited for; matrix products, arithmetic and copies ran while one was open for 3% of the time, Pallas kernels for 22%

profile of v2, /device:TPU:0, one launch (start us, length us, event | category | flops | bytes accessed | tf_op | source)
XLA Modules:
  0.0 83.9 jit_solution(10048564819280941606)
XLA Ops:
  0.6 2.1 %compact.1 = (bf16[32,1024]{1,0:T(8,128)(2,1)}, bf16[768,256]{1,0:T(8,128)(2,1)}, bf16[4,256,256]{2,1,0:T(8,128)(2,1)S(1)}) custom-call(s32[16]{0:T(128)} %live_ref.11, f32[1,32,1024]{2,1,0:T(8,128)} %b_ref.1, bf16[1024,256]{1,0:T(8,128)(2,1)} %cot_ref.1), custom_call_target="tpu_custom_call" | custom-call | bytes 1048576 | tf_op jit(solution)/shard_map/compact/pallas_call | solution.py:170
  2.7 3.0 %collective-permute-start.3 = (bf16[768,256]{1,0:T(8,128)(2,1)}, bf16[768,256]{1,0:T(8,128)(2,1)S(1)}, u32[]{:S(2)}, u32[]{:S(2)}) collective-permute-start(bf16[768,256]{1,0:T(8,128)(2,1)} %get-tuple-element.61.refs_0_.refs_3_.refs_7_), channel_id=1, source_target_pairs={{0,1},{1,3},{3,2},{2,0},{4,5},{5,7},{7,6},{6,4},{8,9},{9,11},{11,1... | collective-permute-start | bytes 1179656 | tf_op jit(solution)/shard_map/ppermute | solution.py:598
  5.7 2.6 %collective-permute-start.4 = (bf16[32,1024]{1,0:T(8,128)(2,1)}, bf16[32,1024]{1,0:T(8,128)(2,1)S(1)}, u32[]{:S(2)}, u32[]{:S(2)}) collective-permute-start(bf16[32,1024]{1,0:T(8,128)(2,1)} %get-tuple-element.80.refs_0_), channel_id=1, source_target_pairs={{0,1},{1,0},{2,3},{3,2},{4,5},{5,4},{6,7},{7,6},{8,9},{9,8},{10,11... | collective-permute-start | bytes 196616 | tf_op jit(solution)/shard_map/ppermute | solution.py:52
  8.3 1.2 %copy-done.9 = f32[1,2048,128]{2,1,0:T(8,128)S(1)} copy-done((f32[1,2048,128]{2,1,0:T(8,128)S(1)}, f32[1,2048,128]{2,1,0:T(8,128)}, u32[]{:S(2)}) %copy-start.9) | copy-done | bytes 1048600
  9.8 2.2 %copy-done.7 = bf16[1024,2048]{1,0:T(8,128)(2,1)S(1)} copy-done((bf16[1024,2048]{1,0:T(8,128)(2,1)S(1)}, bf16[1024,2048]{1,0:T(8,128)(2,1)}, u32[]{:S(2)}) %copy-start.7) | copy-done | bytes 4194328
  12.3 2.1 %copy-done = bf16[1024,2048]{1,0:T(8,128)(2,1)} copy-done((bf16[1024,2048]{1,0:T(8,128)(2,1)}, bf16[1024,2048]{1,0:T(8,128)(2,1)S(1)}, u32[]{:S(2)}) %copy-start) | copy-done | bytes 4194328
  14.4 1.3 %copy-done.8 = bf16[2048,1024]{1,0:T(8,128)(2,1)S(1)} copy-done((bf16[2048,1024]{1,0:T(8,128)(2,1)S(1)}, bf16[2048,1024]{1,0:T(8,128)(2,1)}, u32[]{:S(2)}) %copy-start.8) | copy-done | bytes 4194328
  16.0 2.0 %copy-done.3 = bf16[2048,1024]{1,0:T(8,128)(2,1)} copy-done((bf16[2048,1024]{1,0:T(8,128)(2,1)}, bf16[2048,1024]{1,0:T(8,128)(2,1)S(1)}, u32[]{:S(2)}) %copy-start.3) | copy-done | bytes 4194328
  18.0 1.5 %collective-permute-start.6 = (bf16[128,2048]{1,0:T(8,128)(2,1)S(1)}, bf16[128,2048]{1,0:T(8,128)(2,1)S(1)}, u32[]{:S(2)}, u32[]{:S(2)}) collective-permute-start(bf16[128,2048]{1,0:T(8,128)(2,1)S(1)} %round_factors.1.refs_4_.refs_2_), channel_id=1, source_target_pairs={{0,8},{4,12},{8,0},{12,4},{1,9},{5,13},{9,1},{13,5},{2,10},{6,14},... | collective-permute-start | bytes 1572872 | tf_op jit(solution)/shard_map/ppermute | solution.py:52
  19.7 2.7 %collective-permute-start.7 = (bf16[32,1024]{1,0:T(8,128)(2,1)S(1)}, bf16[32,1024]{1,0:T(8,128)(2,1)S(1)}, u32[]{:S(2)}, u32[]{:S(2)}) collective-permute-start(bf16[32,1024]{1,0:T(8,128)(2,1)S(1)} %copy-done.12), channel_id=1, source_target_pairs={{0,2},{1,3},{2,0},{3,1},{4,6},{5,7},{6,4},{7,5},{8,10},{9,11},{10,... | collective-permute-start | bytes 196616 | tf_op jit(solution)/shard_map/ppermute | solution.py:52
  24.0 2.2 %copy-done.4 = bf16[2048,1024]{1,0:T(8,128)(2,1)S(1)} copy-done((bf16[2048,1024]{1,0:T(8,128)(2,1)S(1)}, bf16[2048,1024]{1,0:T(8,128)(2,1)}, u32[]{:S(2)}) %copy-start.4) | copy-done | bytes 4194328
  26.2 3.4 %base.1.base_ref = f32[768,2048]{1,0:T(8,128)S(1)} custom-call(s32[1]{0:T(128)} %bitcast.4.z_ref, s32[16]{0:T(128)S(1)} %copy-done.13, bf16[2048,1024]{1,0:T(8,128)(2,1)S(1)} %copy-done.4, bf16[768,256]{1,0:T(8,128)(2,1)S(1)} %copy-done.11, bf16[768,256]{1,0:T(8,128)(2,1)S(1)} %collective-permute-done.3.refs_1_.refs_4_.refs_8_), custom_call_target="tpu_custom_call" | custom-call | flops 1610612736 | bytes 6291456 | tf_op jit(solution)/shard_map/base/pallas_call | solution.py:476
  29.6 2.7 %copy-done.6 = f32[768,2048]{1,0:T(8,128)} copy-done((f32[768,2048]{1,0:T(8,128)}, f32[768,2048]{1,0:T(8,128)S(1)}, u32[]{:S(2)}) %copy-start.6) | copy-done | bytes 6291480
  32.2 3.4 %collective-permute-done.7.refs_2_ = bf16[32,1024]{1,0:T(8,128)(2,1)S(1)} collective-permute-done((bf16[32,1024]{1,0:T(8,128)(2,1)S(1)}, bf16[32,1024]{1,0:T(8,128)(2,1)S(1)}, u32[]{:S(2)}, u32[]{:S(2)}) %collective-permute-start.7) | collective-permute-done | bytes 65568 | tf_op jit(solution)/shard_map/ppermute | solution.py:52
  36.9 1.3 %collective-permute-start.15 = (bf16[128,1024]{1,0:T(8,128)(2,1)S(1)}, bf16[128,1024]{1,0:T(8,128)(2,1)S(1)}, u32[]{:S(2)}, u32[]{:S(2)}) collective-permute-start(bf16[128,1024]{1,0:T(8,128)(2,1)S(1)} %ordered.1.refs_8_), channel_id=1, source_target_pairs={{0,8},{4,12},{8,0},{12,4},{1,9},{5,13},{9,1},{13,5},{2,10},{6,14},... | collective-permute-start | bytes 786440 | tf_op jit(solution)/shard_map/ppermute | solution.py:52
  39.2 2.2 %copy-done.1 = bf16[1024,2048]{1,0:T(8,128)(2,1)S(1)} copy-done((bf16[1024,2048]{1,0:T(8,128)(2,1)S(1)}, bf16[1024,2048]{1,0:T(8,128)(2,1)}, u32[]{:S(2)}) %copy-start.1) | copy-done | bytes 4194328
  41.4 4.8 %hidden.1 = (bf16[32,1024]{1,0:T(8,128)(2,1)S(1)}, bf16[32,1024]{1,0:T(8,128)(2,1)S(1)}, bf16[32,1024]{1,0:T(8,128)(2,1)S(1)}, bf16[32,1024]{1,0:T(8,128)(2,1)S(1)}) custom-call(s32[1]{0:T(128)} %bitcast.5.d_ref, s32[1]{0:T(128)} %bitcast.4.z_ref, s32[16]{0:T(128)S(1)} %copy-done.13, s32[16]{0:T(128)S(1)} %copy-done.14, s32[4]{0:T(128)S(1)} %copy-done.15, ...), custom_call_target="tpu_custom_call" | custom-call | flops 2147483648 | bytes 6291456 | tf_op jit(solution)/shard_map/hidden/pallas_call | solution.py:251
  46.4 1.6 %collective-permute-start.13 = (bf16[32,1024]{1,0:T(8,128)(2,1)S(1)}, bf16[32,1024]{1,0:T(8,128)(2,1)S(1)}, u32[]{:S(2)}, u32[]{:S(2)}) collective-permute-start(bf16[32,1024]{1,0:T(8,128)(2,1)S(1)} %get-tuple-element.78), channel_id=1, source_target_pairs={{0,2},{1,3},{2,0},{3,1},{4,6},{5,7},{6,4},{7,5},{8,10},{9,11},{10,... | collective-permute-start | bytes 196616 | tf_op jit(solution)/shard_map/ppermute | solution.py:52
  48.0 2.6 %collective-permute-start.14 = (bf16[32,1024]{1,0:T(8,128)(2,1)S(1)}, bf16[32,1024]{1,0:T(8,128)(2,1)S(1)}, u32[]{:S(2)}, u32[]{:S(2)}) collective-permute-start(bf16[32,1024]{1,0:T(8,128)(2,1)S(1)} %get-tuple-element.79), channel_id=1, source_target_pairs={{0,3},{1,2},{2,1},{3,0},{4,7},{5,6},{6,5},{7,4},{8,11},{9,10},{10,... | collective-permute-start | bytes 196616 | tf_op jit(solution)/shard_map/ppermute | solution.py:52
  51.4 3.5 %collective-permute-done.13.refs_5_ = bf16[32,1024]{1,0:T(8,128)(2,1)S(1)} collective-permute-done((bf16[32,1024]{1,0:T(8,128)(2,1)S(1)}, bf16[32,1024]{1,0:T(8,128)(2,1)S(1)}, u32[]{:S(2)}, u32[]{:S(2)}) %collective-permute-start.13) | collective-permute-done | bytes 65568 | tf_op jit(solution)/shard_map/ppermute | solution.py:52
  55.4 1.0 %collective-permute-done.16.refs_10_ = bf16[128,1024]{1,0:T(8,128)(2,1)S(1)} collective-permute-done((bf16[128,1024]{1,0:T(8,128)(2,1)S(1)}, bf16[128,1024]{1,0:T(8,128)(2,1)S(1)}, u32[]{:S(2)}, u32[]{:S(2)}) %collective-permute-start.16) | collective-permute-done | bytes 262176 | tf_op jit(solution)/shard_map/ppermute | solution.py:52
  56.8 2.1 %upward.1 = (bf16[1024,512]{1,0:T(8,128)(2,1)S(1)}, bf16[1024,512]{1,0:T(8,128)(2,1)S(1)}) custom-call(s32[1]{0:T(128)} %bitcast.5.d_ref, s32[1]{0:T(128)} %bitcast.4.z_ref, s32[16]{0:T(128)S(1)} %copy-done.13, s32[16]{0:T(128)S(1)} %copy-done.14, s32[4]{0:T(128)S(1)} %copy-done.15, s32[4]{0:T(128)S(1)} %copy-done.16, bf16[768,256]{1,0:T(8,128)(2,1)S(1)} %copy-done.11, ...), custom_call_target="tpu_custom_call" | custom-call | flops 1073741824 | bytes 4194304 | tf_op jit(solution)/shard_map/upward/pallas_call | solution.py:320
  58.9 1.6 %down_grad.2 = (bf16[2,1024,128]{2,1,0:T(8,128)(2,1)S(1)}, bf16[2,1024,128]{2,1,0:T(8,128)(2,1)S(1)}) custom-call(bf16[1024,2048]{1,0:T(8,128)(2,1)S(1)} %copy-done.2, bf16[1024,512]{1,0:T(8,128)(2,1)S(1)} %get-tuple-element.91.u_ref), custom_call_target="tpu_custom_call" | custom-call | flops 1073741824 | bytes 4194304 | tf_op jit(solution)/shard_map/down_grad/pallas_call | solution.py:351
  60.8 1.6 %down_grad.3 = (bf16[2,1024,128]{2,1,0:T(8,128)(2,1)S(1)}, bf16[2,1024,128]{2,1,0:T(8,128)(2,1)S(1)}) custom-call(bf16[1024,2048]{1,0:T(8,128)(2,1)S(1)} %copy-done.2, bf16[1024,512]{1,0:T(8,128)(2,1)S(1)} %get-tuple-element.91.u_ref), custom_call_target="tpu_custom_call" | custom-call | flops 1073741824 | bytes 4194304 | tf_op jit(solution)/shard_map/down_grad/pallas_call | solution.py:351
  62.8 1.1 %up_grad.1 = (bf16[2,48,1024]{2,1,0:T(8,128)(2,1)S(1)}, bf16[2,48,1024]{2,1,0:T(8,128)(2,1)S(1)}) custom-call(s32[1]{0:T(128)} %bitcast.5.d_ref, s32[1]{0:T(128)} %bitcast.4.z_ref, s32[16]{0:T(128)S(1)} %copy-done.13, s32[16]{0:T(128)S(1)} %copy-done.14, s32[4]{0:T(128)S(1)} %copy-done.15, s32[4]{0:T(128)S(1)} %copy-done.16, ...), custom_call_target="tpu_custom_call" | custom-call | flops 268435456 | bytes 4194304 | tf_op jit(solution)/shard_map/up_grad/pallas_call | solution.py:412
  64.5 0.9 %collective-permute-done.20 = bf16[2,48,1024]{2,1,0:T(8,128)(2,1)S(1)} collective-permute-done((bf16[2,48,1024]{2,1,0:T(8,128)(2,1)S(1)}, bf16[2,48,1024]{2,1,0:T(8,128)(2,1)S(1)}, u32[]{:S(2)}, u32[]{:S(2)}) %collective-permute-start.20) | collective-permute-done | bytes 196640 | tf_op jit(solution)/shard_map/ppermute | solution.py:52
  65.5 1.0 %collective-permute-start.23 = (bf16[1,48,1024]{2,1,0:T(8,128)(2,1)S(1)}, bf16[1,48,1024]{2,1,0:T(8,128)(2,1)S(1)}, u32[]{:S(2)}, u32[]{:S(2)}) collective-permute-start(bf16[1,48,1024]{2,1,0:T(8,128)(2,1)S(1)} %slice.66), channel_id=1, source_target_pairs={{0,8},{4,12},{8,0},{12,4},{1,9},{5,13},{9,1},{13,5},{2,10},{6,14},... | collective-permute-start | bytes 294920 | tf_op jit(solution)/shard_map/ppermute | solution.py:52
  66.5 1.1 %collective-permute-start.21 = (bf16[1,1024,128]{2,1,0:T(8,128)(2,1)S(1)}, bf16[1,1024,128]{2,1,0:T(8,128)(2,1)S(1)}, u32[]{:S(2)}, u32[]{:S(2)}) collective-permute-start(bf16[1,1024,128]{2,1,0:T(8,128)(2,1)S(1)} %slice.65), channel_id=1, source_target_pairs={{0,8},{4,12},{8,0},{12,4},{1,9},{5,13},{9,1},{13,5},{2,10},{6,14},... | collective-permute-start | bytes 786440 | tf_op jit(solution)/shard_map/ppermute | solution.py:52
  67.6 0.9 %collective-permute-start.22 = (bf16[1,1024,128]{2,1,0:T(8,128)(2,1)S(1)}, bf16[1,1024,128]{2,1,0:T(8,128)(2,1)S(1)}, u32[]{:S(2)}, u32[]{:S(2)}) collective-permute-start(bf16[1,1024,128]{2,1,0:T(8,128)(2,1)S(1)} %slice.64), channel_id=1, source_target_pairs={{0,8},{4,12},{8,0},{12,4},{1,9},{5,13},{9,1},{13,5},{2,10},{6,14},... | collective-permute-start | bytes 786440 | tf_op jit(solution)/shard_map/ppermute | solution.py:52
  68.5 6.6 %grad_acts.1 = bf16[1024,2048]{1,0:T(8,128)(2,1)} custom-call(s32[1]{0:T(128)} %bitcast.4.z_ref, s32[16]{0:T(128)S(1)} %copy-done.13, bf16[2048,1024]{1,0:T(8,128)(2,1)S(1)} %copy-done.5, bf16[1024,512]{1,0:T(8,128)(2,1)S(1)} %get-tuple-element.105.u_ref, f32[768,2048]{1,0:T(8,128)S(1)} %bitcast.10, bf16[4,256,256]{2,1,0:T(8,128)(2,1)S(1)} %copy-done.20, ...), custom_call_target="tpu_custom_call" | custom-call | flops 6442450944 | bytes 12582912 | tf_op jit(solution)/shard_map/grad_acts/pallas_call | solution.py:538
  78.1 3.6 %collective-permute-done.22 = bf16[1,1024,128]{2,1,0:T(8,128)(2,1)S(1)} collective-permute-done((bf16[1,1024,128]{2,1,0:T(8,128)(2,1)S(1)}, bf16[1,1024,128]{2,1,0:T(8,128)(2,1)S(1)}, u32[]{:S(2)}, u32[]{:S(2)}) %collective-permute-start.22) | collective-permute-done | bytes 262176 | tf_op jit(solution)/shard_map/ppermute | solution.py:52
  81.8 2.1 %divide_subtract_fusion = (f32[1,2048,128]{2,1,0:T(8,128)}, f32[1,2048,128]{2,1,0:T(8,128)}, f32[1,2048,128]{2,1,0:T(8,128)}) fusion(f32[1,2048,128]{2,1,0:T(8,128)S(1)} %copy-done.10, f32[]{:T(128)} %bitcast.7, f32[1,1024,128]{2,1,0:T(8,128)S(1)} %get-tuple-element.120, f32[1,1024,128]{2,1,0:T(8,128)S(1)} %get-tuple-element.121, ...), kind=kLoop, calls=%fused_computation.5 | loop fusion | flops 3670016 | bytes 7340036 | tf_op jit(solution)/shard_map/sub | solution.py:34
  (88 shorter events, 8.8 us)
Async XLA Ops:
  2.7 15.3 %collective-permute-start.3 = (bf16[768,256]{1,0:T(8,128)(2,1)}, bf16[768,256]{1,0:T(8,128)(2,1)S(1)}, u32[]{:S(2)}, u32[]{:S(2)}) collective-permute-start(bf16[768,256]{1,0:T(8,128)(2,1)} %get-tuple-element.61.refs_0_.refs_3_.refs_7_), channel_id=1, source_target_pairs={{0,1},{1,3},{3,2},{2,0},{4,5},{5,7},{7,6},{6,4},{8,9},{9,11},{11,1... | collective-permute-start | bytes 1179656 | tf_op jit(solution)/shard_map/ppermute | solution.py:598
  5.7 12.2 %collective-permute-start.4 = (bf16[32,1024]{1,0:T(8,128)(2,1)}, bf16[32,1024]{1,0:T(8,128)(2,1)S(1)}, u32[]{:S(2)}, u32[]{:S(2)}) collective-permute-start(bf16[32,1024]{1,0:T(8,128)(2,1)} %get-tuple-element.80.refs_0_), channel_id=1, source_target_pairs={{0,1},{1,0},{2,3},{3,2},{4,5},{5,4},{6,7},{7,6},{8,9},{9,8},{10,11... | collective-permute-start | bytes 196616 | tf_op jit(solution)/shard_map/ppermute | solution.py:52
  15.7 8.3 %copy-start.11 = (bf16[768,256]{1,0:T(8,128)(2,1)S(1)}, bf16[768,256]{1,0:T(8,128)(2,1)}, u32[]{:S(2)}) copy-start(bf16[768,256]{1,0:T(8,128)(2,1)} %get-tuple-element.61.refs_0_.refs_3_.refs_7_) | copy-start | bytes 1179652
  18.0 18.3 %collective-permute-start.6 = (bf16[128,2048]{1,0:T(8,128)(2,1)S(1)}, bf16[128,2048]{1,0:T(8,128)(2,1)S(1)}, u32[]{:S(2)}, u32[]{:S(2)}) collective-permute-start(bf16[128,2048]{1,0:T(8,128)(2,1)S(1)} %round_factors.1.refs_4_.refs_2_), channel_id=1, source_target_pairs={{0,8},{4,12},{8,0},{12,4},{1,9},{5,13},{9,1},{13,5},{2,10},{6,14},... | collective-permute-start | bytes 1572872 | tf_op jit(solution)/shard_map/ppermute | solution.py:52
  19.5 16.8 %collective-permute-start.5 = (bf16[768,256]{1,0:T(8,128)(2,1)S(1)}, bf16[768,256]{1,0:T(8,128)(2,1)S(1)}, u32[]{:S(2)}, u32[]{:S(2)}) collective-permute-start(bf16[768,256]{1,0:T(8,128)(2,1)S(1)} %collective-permute-done.3.refs_1_.refs_4_.refs_8_), channel_id=1, source_target_pairs={{0,1},{1,3},{3,2},{2,0},{4,5},{5,7},{7,6},{6,4},{8,9},{9,11},{11,1... | collective-permute-start | bytes 1179656 | tf_op jit(solution)/shard_map/ppermute | solution.py:598
  19.7 15.9 %collective-permute-start.7 = (bf16[32,1024]{1,0:T(8,128)(2,1)S(1)}, bf16[32,1024]{1,0:T(8,128)(2,1)S(1)}, u32[]{:S(2)}, u32[]{:S(2)}) collective-permute-start(bf16[32,1024]{1,0:T(8,128)(2,1)S(1)} %copy-done.12), channel_id=1, source_target_pairs={{0,2},{1,3},{2,0},{3,1},{4,6},{5,7},{6,4},{7,5},{8,10},{9,11},{10,... | collective-permute-start | bytes 196616 | tf_op jit(solution)/shard_map/ppermute | solution.py:52
  23.7 12.6 %collective-permute-start.8 = (bf16[32,1024]{1,0:T(8,128)(2,1)S(1)}, bf16[32,1024]{1,0:T(8,128)(2,1)S(1)}, u32[]{:S(2)}, u32[]{:S(2)}) collective-permute-start(bf16[32,1024]{1,0:T(8,128)(2,1)S(1)} %collective-permute-done.4.refs_1_), channel_id=1, source_target_pairs={{0,2},{1,3},{2,0},{3,1},{4,6},{5,7},{6,4},{7,5},{8,10},{9,11},{10,... | collective-permute-start | bytes 196616 | tf_op jit(solution)/shard_map/ppermute | solution.py:52
  26.2 13.0 %copy-start.14 = (s32[16]{0:T(128)S(1)}, s32[16]{0:T(128)}, u32[]{:S(2)}) copy-start(s32[16]{0:T(128)} %refs_0_.5) | copy-start | bytes 196
  26.2 13.0 %copy-start.15 = (s32[4]{0:T(128)S(1)}, s32[4]{0:T(128)}, u32[]{:S(2)}) copy-start(s32[4]{0:T(128)} %refs_1_.5) | copy-start | bytes 52
  26.2 13.0 %copy-start.16 = (s32[4]{0:T(128)S(1)}, s32[4]{0:T(128)}, u32[]{:S(2)}) copy-start(s32[4]{0:T(128)} %refs_2_.5) | copy-start | bytes 52
  36.3 2.0 %collective-permute-start.10 = (bf16[128,2048]{1,0:T(8,128)(2,1)S(1)}, bf16[128,2048]{1,0:T(8,128)(2,1)S(1)}, u32[]{:S(2)}, u32[]{:S(2)}) collective-permute-start(bf16[128,2048]{1,0:T(8,128)(2,1)S(1)} %round_factors.1.refs_4_.refs_2_), channel_id=1, source_target_pairs={{0,4},{4,0},{8,12},{12,8},{1,5},{5,1},{9,13},{13,9},{2,6},{6,2},{1... | collective-permute-start | bytes 1572872 | tf_op jit(solution)/shard_map/ppermute | solution.py:52
  36.4 2.8 %collective-permute-start.11 = (bf16[128,2048]{1,0:T(8,128)(2,1)S(1)}, bf16[128,2048]{1,0:T(8,128)(2,1)}, u32[]{:S(2)}, u32[]{:S(2)}) collective-permute-start(bf16[128,2048]{1,0:T(8,128)(2,1)S(1)} %collective-permute-done.6.refs_5_.refs_3_), channel_id=1, source_target_pairs={{0,4},{4,0},{8,12},{12,8},{1,5},{5,1},{9,13},{13,9},{2,6},{6,2},{1... | collective-permute-start | bytes 1572872 | tf_op jit(solution)/shard_map/ppermute | solution.py:52
  36.9 13.8 %collective-permute-start.9 = (bf16[768,256]{1,0:T(8,128)(2,1)S(1)}, bf16[768,256]{1,0:T(8,128)(2,1)S(1)}, u32[]{:S(2)}, u32[]{:S(2)}) collective-permute-start(bf16[768,256]{1,0:T(8,128)(2,1)S(1)} %collective-permute-done.5.refs_5_.refs_9_.refs_0_), channel_id=1, source_target_pairs={{0,1},{1,3},{3,2},{2,0},{4,5},{5,7},{7,6},{6,4},{8,9},{9,11},{11,1... | collective-permute-start | bytes 1179656 | tf_op jit(solution)/shard_map/ppermute | solution.py:598
  36.9 19.9 %copy-start.20 = (bf16[4,256,256]{2,1,0:T(8,128)(2,1)S(1)}, bf16[4,256,256]{2,1,0:T(8,128)(2,1)}, u32[]{:S(2)}) copy-start(bf16[4,256,256]{2,1,0:T(8,128)(2,1)} %copy-done.19) | copy-start | bytes 1572868
  36.9 13.7 %collective-permute-start.15 = (bf16[128,1024]{1,0:T(8,128)(2,1)S(1)}, bf16[128,1024]{1,0:T(8,128)(2,1)S(1)}, u32[]{:S(2)}, u32[]{:S(2)}) collective-permute-start(bf16[128,1024]{1,0:T(8,128)(2,1)S(1)} %ordered.1.refs_8_), channel_id=1, source_target_pairs={{0,8},{4,12},{8,0},{12,4},{1,9},{5,13},{9,1},{13,5},{2,10},{6,14},... | collective-permute-start | bytes 786440 | tf_op jit(solution)/shard_map/ppermute | solution.py:52
  41.4 17.6 %copy-start.2 = (bf16[1024,2048]{1,0:T(8,128)(2,1)S(1)}, bf16[1024,2048]{1,0:T(8,128)(2,1)}, u32[]{:S(2)}) copy-start(bf16[1024,2048]{1,0:T(8,128)(2,1)} %copy-done) | copy-start | bytes 12582916
  46.2 5.2 %collective-permute-start.12 = (bf16[32,1024]{1,0:T(8,128)(2,1)S(1)}, bf16[32,1024]{1,0:T(8,128)(2,1)S(1)}, u32[]{:S(2)}, u32[]{:S(2)}) collective-permute-start(bf16[32,1024]{1,0:T(8,128)(2,1)S(1)} %get-tuple-element.77), channel_id=1, source_target_pairs={{0,1},{1,0},{2,3},{3,2},{4,5},{5,4},{6,7},{7,6},{8,9},{9,8},{10,11... | collective-permute-start | bytes 196616 | tf_op jit(solution)/shard_map/ppermute | solution.py:52
  46.4 8.5 %collective-permute-start.13 = (bf16[32,1024]{1,0:T(8,128)(2,1)S(1)}, bf16[32,1024]{1,0:T(8,128)(2,1)S(1)}, u32[]{:S(2)}, u32[]{:S(2)}) collective-permute-start(bf16[32,1024]{1,0:T(8,128)(2,1)S(1)} %get-tuple-element.78), channel_id=1, source_target_pairs={{0,2},{1,3},{2,0},{3,1},{4,6},{5,7},{6,4},{7,5},{8,10},{9,11},{10,... | collective-permute-start | bytes 196616 | tf_op jit(solution)/shard_map/ppermute | solution.py:52
  48.0 6.9 %collective-permute-start.14 = (bf16[32,1024]{1,0:T(8,128)(2,1)S(1)}, bf16[32,1024]{1,0:T(8,128)(2,1)S(1)}, u32[]{:S(2)}, u32[]{:S(2)}) collective-permute-start(bf16[32,1024]{1,0:T(8,128)(2,1)S(1)} %get-tuple-element.79), channel_id=1, source_target_pairs={{0,3},{1,2},{2,1},{3,0},{4,7},{5,6},{6,5},{7,4},{8,11},{9,10},{10,... | collective-permute-start | bytes 196616 | tf_op jit(solution)/shard_map/ppermute | solution.py:52
  54.9 1.5 %collective-permute-start.16 = (bf16[128,1024]{1,0:T(8,128)(2,1)S(1)}, bf16[128,1024]{1,0:T(8,128)(2,1)S(1)}, u32[]{:S(2)}, u32[]{:S(2)}) collective-permute-start(bf16[128,1024]{1,0:T(8,128)(2,1)S(1)} %ordered.1.refs_8_), channel_id=1, source_target_pairs={{0,4},{4,0},{8,12},{12,8},{1,5},{5,1},{9,13},{13,9},{2,6},{6,2},{1... | collective-permute-start | bytes 786440 | tf_op jit(solution)/shard_map/ppermute | solution.py:52
  54.9 1.9 %collective-permute-start.17 = (bf16[128,1024]{1,0:T(8,128)(2,1)S(1)}, bf16[128,1024]{1,0:T(8,128)(2,1)S(1)}, u32[]{:S(2)}, u32[]{:S(2)}) collective-permute-start(bf16[128,1024]{1,0:T(8,128)(2,1)S(1)} %collective-permute-done.15.refs_9_), channel_id=1, source_target_pairs={{0,4},{4,0},{8,12},{12,8},{1,5},{5,1},{9,13},{13,9},{2,6},{6,2},{1... | collective-permute-start | bytes 786440 | tf_op jit(solution)/shard_map/ppermute | solution.py:52
  58.9 9.6 %slice-start = ((s8[6291456]{0:T(1024)(128)(4,1)}), s8[4194304]{0:T(1024)(128)(4,1)S(1)}, s32[]{:S(2)}) async-start(s8[6291456]{0:T(1024)(128)(4,1)} %bitcast.9), calls=%async_computation | async-start | bytes 8388608
  60.5 8.0 %slice-start.1 = ((s8[6291456]{0:T(1024)(128)(4,1)}), s8[2097152]{0:T(1024)(128)(4,1)S(1)}, s32[]{:S(2)}) async-start(s8[6291456]{0:T(1024)(128)(4,1)} %bitcast.9), calls=%async_computation.1 | async-start | bytes 4194304
  60.6 3.5 %collective-permute-start.19 = (bf16[2,1024,128]{2,1,0:T(8,128)(2,1)S(1)}, bf16[2,1024,128]{2,1,0:T(8,128)(2,1)S(1)}, u32[]{:S(2)}, u32[]{:S(2)}) collective-permute-start(bf16[2,1024,128]{2,1,0:T(8,128)(2,1)S(1)} %get-tuple-element.90), channel_id=1, source_target_pairs={{0,4},{4,0},{8,12},{12,8},{1,5},{5,1},{9,13},{13,9},{2,6},{6,2},{1... | collective-permute-start | bytes 1572872 | tf_op jit(solution)/shard_map/ppermute | solution.py:52
  62.3 2.0 %collective-permute-start.18 = (bf16[2,1024,128]{2,1,0:T(8,128)(2,1)S(1)}, bf16[2,1024,128]{2,1,0:T(8,128)(2,1)S(1)}, u32[]{:S(2)}, u32[]{:S(2)}) collective-permute-start(bf16[2,1024,128]{2,1,0:T(8,128)(2,1)S(1)} %get-tuple-element.93), channel_id=1, source_target_pairs={{0,4},{4,0},{8,12},{12,8},{1,5},{5,1},{9,13},{13,9},{2,6},{6,2},{1... | collective-permute-start | bytes 1572872 | tf_op jit(solution)/shard_map/ppermute | solution.py:52
  63.9 1.5 %collective-permute-start.20 = (bf16[2,48,1024]{2,1,0:T(8,128)(2,1)S(1)}, bf16[2,48,1024]{2,1,0:T(8,128)(2,1)S(1)}, u32[]{:S(2)}, u32[]{:S(2)}) collective-permute-start(bf16[2,48,1024]{2,1,0:T(8,128)(2,1)S(1)} %get-tuple-element.100), channel_id=1, source_target_pairs={{0,4},{4,0},{8,12},{12,8},{1,5},{5,1},{9,13},{13,9},{2,6},{6,2},{1... | collective-permute-start | bytes 589832 | tf_op jit(solution)/shard_map/ppermute | solution.py:52
  65.5 11.8 %copy-start.21 = (f32[1,32,1024]{2,1,0:T(8,128)S(1)}, f32[1,32,1024]{2,1,0:T(8,128)}, u32[]{:S(2)}) copy-start(f32[1,32,1024]{2,1,0:T(8,128)} %b_ref.1) | copy-start | bytes 393220
  65.5 11.8 %copy-start.22 = (f32[1,32,1024]{2,1,0:T(8,128)S(1)}, f32[1,32,1024]{2,1,0:T(8,128)}, u32[]{:S(2)}) copy-start(f32[1,32,1024]{2,1,0:T(8,128)} %param.22) | copy-start | bytes 393220
  65.5 11.8 %copy-start.23 = (f32[1,32,1024]{2,1,0:T(8,128)S(1)}, f32[1,32,1024]{2,1,0:T(8,128)}, u32[]{:S(2)}) copy-start(f32[1,32,1024]{2,1,0:T(8,128)} %param.23) | copy-start | bytes 393220
  65.5 9.6 %collective-permute-start.23 = (bf16[1,48,1024]{2,1,0:T(8,128)(2,1)S(1)}, bf16[1,48,1024]{2,1,0:T(8,128)(2,1)S(1)}, u32[]{:S(2)}, u32[]{:S(2)}) collective-permute-start(bf16[1,48,1024]{2,1,0:T(8,128)(2,1)S(1)} %slice.66), channel_id=1, source_target_pairs={{0,8},{4,12},{8,0},{12,4},{1,9},{5,13},{9,1},{13,5},{2,10},{6,14},... | collective-permute-start | bytes 294920 | tf_op jit(solution)/shard_map/ppermute | solution.py:52
  66.5 11.6 %collective-permute-start.21 = (bf16[1,1024,128]{2,1,0:T(8,128)(2,1)S(1)}, bf16[1,1024,128]{2,1,0:T(8,128)(2,1)S(1)}, u32[]{:S(2)}, u32[]{:S(2)}) collective-permute-start(bf16[1,1024,128]{2,1,0:T(8,128)(2,1)S(1)} %slice.65), channel_id=1, source_target_pairs={{0,8},{4,12},{8,0},{12,4},{1,9},{5,13},{9,1},{13,5},{2,10},{6,14},... | collective-permute-start | bytes 786440 | tf_op jit(solution)/shard_map/ppermute | solution.py:52
  67.6 14.0 %collective-permute-start.22 = (bf16[1,1024,128]{2,1,0:T(8,128)(2,1)S(1)}, bf16[1,1024,128]{2,1,0:T(8,128)(2,1)S(1)}, u32[]{:S(2)}, u32[]{:S(2)}) collective-permute-start(bf16[1,1024,128]{2,1,0:T(8,128)(2,1)S(1)} %slice.64), channel_id=1, source_target_pairs={{0,8},{4,12},{8,0},{12,4},{1,9},{5,13},{9,1},{13,5},{2,10},{6,14},... | collective-permute-start | bytes 786440 | tf_op jit(solution)/shard_map/ppermute | solution.py:52
  (15 other events, 59.4 us)

commit v3 on v2

--- a/solution.py
+++ b/solution.py
@@ -44,6 +44,11 @@
     return inner + [i + 1 for i in inner]
 
 
+def paired(order):
+    q = len(order) // 4
+    return order[:q] + order[2 * q : 3 * q] + order[q : 2 * q] + order[3 * q :]
+
+
 def line_ring(n):
     return [0] + list(range(1, n, 2)) + list(range(n - 2 + n % 2, 0, -2))
 
@@ -121,27 +126,7 @@
     )(a)
 
 
-def round_kernel(a_ref, out_ref):
-    out_ref[...] = a_ref[0].T.astype(half)
-
-
-def round_call(a):
-    _, width, ranks = a.shape
-    blk = width
-    return pl.pallas_call(
-        round_kernel,
-        grid=(width // blk,),
-        in_specs=[pl.BlockSpec((1, blk, ranks), lambda i: (0, i, 0))],
-        out_specs=pl.BlockSpec((ranks, blk), lambda i: (0, i)),
-        out_shape=jax.ShapeDtypeStruct((ranks, width), half),
-        compiler_params=kernel_params(16),
-        cost_estimate=cost(0, 6 * a.size),
-        name="round_factors",
-    )(a)
-
-
-def compact_kernel(live_ref, b_ref, cot_ref, up_ref, first_ref, rest_ref, all_ref):
-    up_ref[...] = b_ref[0].astype(half)
+def pack_kernel(live_ref, a_ref, b_ref, cot_ref, down_ref, up_ref, first_ref, rest_ref, all_ref):
     blocks = live_ref.shape[0]
     blk_len = cot_ref.shape[0] // blocks
     starts, _ = starts_of(live_ref)
@@ -157,63 +142,85 @@
         cols = slice(p * lanes, (p + 1) * lanes)
         first_ref[:, cols] = all_ref[p, :room, :].astype(half)
         rest_ref[0, :, cols] = all_ref[p, room:, :].astype(half)
-
-
-def compact_call(live, b, cot, room, copies):
+    up_ref[...] = b_ref[0].astype(half)
+    down_ref[...] = a_ref[0].T.astype(half)
+
+
+def pack_call(live, a, b, cot, room, copies):
     tok, kw = cot.shape
     shapes = [
+        jax.ShapeDtypeStruct((a.shape[2], a.shape[1]), half),
         jax.ShapeDtypeStruct(b.shape[1:], half),
         jax.ShapeDtypeStruct((room, kw), half),
         jax.ShapeDtypeStruct((copies, tok - room, kw), half),
     ]
-    specs = [resident(shapes[0]), resident(shapes[1]), pl.BlockSpec((1, tok - room, kw), lambda i: (0, 0, 0))]
-    return pl.pallas_call(
-        compact_kernel,
+    specs = [resident(v) for v in shapes[:-1]] + [pl.BlockSpec((1, tok - room, kw), lambda i: (0, 0, 0))]
+    return pl.pallas_call(
+        pack_kernel,
         grid=(1,),
-        in_specs=[smem(), resident(b), resident(cot)],
+        in_specs=[smem(), resident(a), resident(b), resident(cot)],
         out_specs=specs,
         out_shape=shapes,
         scratch_shapes=[pltpu.VMEM((kw // min(kw, 128), tok, min(kw, 128)), wide)],
         compiler_params=kernel_params(56),
-        cost_estimate=cost(0, 4 * tok * kw),
-        name="compact",
-    )(live, b, cot)
-
-
-def ordered_kernel(z_ref, *refs):
+        cost_estimate=cost(0, 4 * tok * kw + 6 * (a.size + b.size)),
+        name="pack",
+    )(live, a, b, cot)
+
+
+def ordered_kernel(z_ref, live_ref, tenant_ref, slot_ref, *refs):
     out_ref = refs[-1]
     own = refs[0].shape[0]
     for k, ref in enumerate(refs[:-1]):
         at = pl.multiple_of(jnp.bitwise_xor(z_ref[0], k) * own, own)
         out_ref[pl.ds(at, own), :] = ref[...]
-
-
-def ordered_call(z, pieces):
+    ranks = own * (len(refs) - 1)
+    shape = (out_ref.shape[0] - ranks, out_ref.shape[1])
+    row, lane = lax.broadcasted_iota(jnp.int32, shape, 0), lax.broadcasted_iota(jnp.int32, shape, 1)
+    tail = jnp.zeros(shape, jnp.int32)
+    for q in range(slot_ref.shape[0]):
+        count = jnp.int32(0)
+        for b in range(live_ref.shape[0]):
+            count = count + jnp.where(slot_ref[tenant_ref[b]] == q, live_ref[b], 0)
+        digit = jnp.where(row == 0, count // 32, jnp.where(row == 1, count % 32, 0))
+        tail = jnp.where(lane == q, digit, tail)
+    out_ref[ranks:, :] = tail.astype(wide).astype(half)
+
+
+def ordered_call(z, live, tables, pieces, tail_rows=16):
     own, cols = pieces[0].shape
     n = len(pieces)
+    tenant, slot_of, _ = tables
     if own % 16:
-        return jnp.stack(pieces)[jnp.bitwise_xor(z[0], jnp.arange(n))].reshape(n * own, cols)
+        rows = jnp.stack(pieces)[jnp.bitwise_xor(z[0], jnp.arange(n))].reshape(n * own, cols)
+        pick = tenant[:, None] == jnp.arange(slot_of.shape[0])[None, :]
+        slot = jnp.sum(jnp.where(pick, slot_of[None, :], 0), axis=1)
+        mine = slot[:, None] == jnp.arange(slot_of.shape[0])[None, :]
+        counts = jnp.sum(jnp.where(mine, live[:, None], 0), axis=0)
+        tail = jnp.stack([counts // 32, counts % 32]).astype(wide).astype(half)
+        return jnp.concatenate([rows, jnp.pad(tail, ((0, tail_rows - 2), (0, cols - slot_of.shape[0])))], axis=0)
     return pl.pallas_call(
         ordered_kernel,
-        in_specs=[smem()] + [vmem()] * n,
+        in_specs=[smem()] * 4 + [vmem()] * n,
         out_specs=vmem(),
-        out_shape=jax.ShapeDtypeStruct((n * own, cols), half),
+        out_shape=jax.ShapeDtypeStruct((n * own + tail_rows, cols), half),
         compiler_params=kernel_params(16),
         cost_estimate=cost(0, 4 * n * own * cols),
         name="ordered",
-    )(z, *pieces)
+    )(z, live, tenant, slot_of, *pieces)
 
 
 def hidden_kernel(order, groups, d_ref, z_ref, live_ref, *refs):
-    tables, x_ref, a_refs = refs[:3], refs[3], refs[4 : 4 + len(order)]
-    out_refs, (all_ref, prod_ref, rows_ref, flat_ref) = refs[4 + len(order) : -4], refs[-4:]
-    ranks = a_refs[0].shape[0]
+    tables, x_ref, a_refs, out_refs = refs[:3], refs[3], refs[4 : -4 - groups], refs[-4 - groups : -4]
+    all_ref, prod_ref, rows_ref, flat_ref = refs[-4:]
+    ranks = rows_ref.shape[1]
     step = pl.program_id(0)
 
     @pl.when(step == 0)
     def _():
+        rows = a_refs[0].shape[0]
         for i, ref in enumerate(a_refs):
-            all_ref[i * ranks : (i + 1) * ranks, :] = ref[...]
+            all_ref[i * rows : (i + 1) * rows, :] = ref[...]
 
     blk = prod_ref.shape[0]
     prod_ref[...] = mm(x_ref[pl.ds(pl.multiple_of(step * blk, blk), blk), :], all_ref[...], NT)
@@ -244,7 +251,8 @@
 
 def hidden_call(d, z, live, tables, x, downs, order, groups):
     tok, width = x.shape
-    ranks = downs[0].shape[0]
+    every = sum(a.shape[0] for a in downs)
+    ranks = every // len(order)
     blk = min(256, tok)
     own = ranks // groups
     shape = jax.ShapeDtypeStruct((own, tok), half)
@@ -257,12 +265,12 @@
         out_specs=[resident(shape)] * groups,
         out_shape=[shape] * groups,
         scratch_shapes=[
-            pltpu.VMEM((len(downs) * ranks, width), half),
-            pltpu.VMEM((blk, len(downs) * ranks), wide),
+            pltpu.VMEM((every, width), half),
+            pltpu.VMEM((blk, every), wide),
             pltpu.VMEM((tok, ranks), wide),
             pltpu.VMEM((ranks, tok), wide),
         ],
-        compiler_params=kernel_params(24),
+        compiler_params=kernel_params(56),
         cost_estimate=cost(2 * tok * width * ranks * len(order), 2 * (x.size + 4 * downs[0].size)),
         name="hidden",
     )(d, z, live, *tables, x, *downs)
@@ -270,12 +278,18 @@
 
 def upward_kernel(order, parts, d_ref, z_ref, live_ref, *refs):
     tables, cots, rest_ref = refs[:3], refs[3 : 3 + parts], refs[3 + parts]
-    b_refs = refs[4 + parts : -5]
-    full_ref, packed_ref, all_ref, acc_ref, rows_ref = refs[-5:]
-    ranks = b_refs[0].shape[0]
+    b_refs = refs[4 + parts : -6]
+    full_ref, packed_ref, count_ref, all_ref, acc_ref, rows_ref = refs[-6:]
+    ranks = acc_ref.shape[2]
     room, kw = cots[0].shape
+    count = jnp.zeros((1, b_refs[0].shape[1]), wide)
     for i, ref in enumerate(b_refs):
-        all_ref[i * ranks : (i + 1) * ranks, :] = ref[...]
+        all_ref[i * ranks : (i + 1) * ranks, :] = ref[:ranks, :]
+        tail = ref[ranks:, :].astype(wide)
+        count = count + tail[0:1] * 32.0 + tail[1:2]
+    lane = lax.broadcasted_iota(jnp.int32, count.shape, 1)
+    count = jnp.sum(jnp.where(lane == d_ref[0], count, 0.0), axis=1, keepdims=True)
+    count_ref[...] = jnp.broadcast_to(jnp.maximum(count, 1.0), count_ref.shape)
 
     src = sources(z_ref[0], parts)
 
@@ -297,31 +311,32 @@
 
     blocks = live_ref.shape[0]
     blk_len = full_ref.shape[0] // blocks
+    panels = paired(order)
     rank_at = lax.broadcasted_iota(jnp.int32, (1, ranks), 1)
     row = lax.broadcasted_iota(jnp.int32, (blk_len, ranks), 0)
     for b in range(blocks):
         near, rank = block_table(tables, b, d_ref[0])
         scale = jnp.where(rank_at < rank, inverse_rank(rank, (1, ranks)), 0.0)
         for i, j in enumerate(order):
-            cols = slice(i * ranks, (i + 1) * ranks)
             piece = acc_ref[i, pl.ds(starts[b], blk_len), :] * jnp.where(near == j, scale, 0.0)
             piece = jnp.where(row < live_ref[b], piece, 0.0)
-            full_ref[b * blk_len : (b + 1) * blk_len, cols] = piece.astype(half)
+            at = panels.index(j)
+            full_ref[b * blk_len : (b + 1) * blk_len, at * ranks : (at + 1) * ranks] = piece.astype(half)
             rows_ref[i, pl.ds(starts[b], blk_len), :] = piece
     for i in range(len(order)):
         packed_ref[:, i * ranks : (i + 1) * ranks] = rows_ref[i].astype(half)
 
 
-def upward_call(d, z, live, tables, cots, rest, ups, order):
-    ranks, value_width = ups[0].shape
+def upward_call(d, z, live, tables, cots, rest, ups, order, ranks):
+    value_width = ups[0].shape[1]
     every = len(ups) * ranks
     tok = cots[0].shape[0] + rest.shape[1]
     shape = jax.ShapeDtypeStruct((tok, every), half)
     return pl.pallas_call(
         functools.partial(upward_kernel, order, len(cots)),
         in_specs=[smem()] * 6 + [vmem()] * (len(cots) + 1 + len(ups)),
-        out_specs=[vmem()] * 2,
-        out_shape=[shape, shape],
+        out_specs=[vmem()] * 3,
+        out_shape=[shape, shape, jax.ShapeDtypeStruct((8, value_width), wide)],
         scratch_shapes=[
             pltpu.VMEM((every, value_width), half),
             pltpu.VMEM((len(ups), tok, ranks), wide),
@@ -333,34 +348,32 @@
     )(d, z, live, *tables, *cots, rest, *ups)
 
 
-def down_kernel(ranks, start, x_ref, u_ref, keep_ref, send_ref):
-    blk = keep_ref.shape[1]
-    cols = pl.ds(pl.multiple_of(start + pl.program_id(0) * blk, blk), blk)
-    acc = mm(x_ref[:, cols], u_ref[...], TN)
-    per = keep_ref.shape[0]
-    for i in range(per):
+def down_kernel(ranks, first, x_ref, u_ref, keep_ref, send_ref):
+    count, blk, _ = keep_ref.shape
+    x = x_ref[:, pl.ds(pl.multiple_of(pl.program_id(0) * blk, blk), blk)]
+    acc = mm(x, u_ref[:, first * ranks : (first + 2 * count) * ranks], TN)
+    for i in range(count):
         keep_ref[i] = acc[:, i * ranks : (i + 1) * ranks].astype(half)
-        send_ref[i] = acc[:, (per + i) * ranks : (per + i + 1) * ranks].astype(half)
-
-
-def down_call(x, u, ranks, start, count):
-    tok = x.shape[0]
-    slots = u.shape[1] // ranks
-    blk = min(512, count)
-    shape = jax.ShapeDtypeStruct((slots // 2, count, ranks), half)
-    return pl.pallas_call(
-        functools.partial(down_kernel, ranks, start),
-        grid=(count // blk,),
+        send_ref[i] = acc[:, (count + i) * ranks : (count + i + 1) * ranks].astype(half)
+
+
+def down_call(x, u, ranks, first, count):
+    tok, width = x.shape
+    blk = min(512, width)
+    shape = jax.ShapeDtypeStruct((count, width, ranks), half)
+    return pl.pallas_call(
+        functools.partial(down_kernel, ranks, first),
+        grid=(width // blk,),
         in_specs=[vmem(), vmem()],
-        out_specs=[pl.BlockSpec((slots // 2, blk, ranks), lambda i: (0, i, 0))] * 2,
+        out_specs=[pl.BlockSpec((count, blk, ranks), lambda i: (0, i, 0))] * 2,
         out_shape=[shape, shape],
         compiler_params=kernel_params(24),
-        cost_estimate=cost(2 * tok * count * slots * ranks, 2 * (tok * count + slots * ranks * (tok + count))),
+        cost_estimate=cost(0, 4 * tok),
         name="down_grad",
     )(x, u)
 
 
-def up_kernel(order, parts, n_hs, tail_rows, d_ref, z_ref, live_ref, *refs):
+def up_kernel(order, parts, n_hs, d_ref, z_ref, live_ref, *refs):
     tables, hs = refs[:3], refs[3 : 3 + n_hs]
     cots, rest_ref = refs[3 + n_hs : 3 + n_hs + parts], refs[3 + n_hs + parts]
     keep_ref, send_ref, acc_ref = refs[-3:]
@@ -374,12 +387,10 @@
     lane = lax.broadcasted_iota(jnp.int32, (1, tok), 1)
     slot = jnp.zeros((1, tok), jnp.int32)
     rank = jnp.ones((1, tok), jnp.int32)
-    counts = [jnp.int32(0) for _ in order]
     for b in range(blocks):
         near, rank_b = block_table(tables, b, d_ref[0])
         slot = jnp.where(lane >= starts[b], near, slot)
         rank = jnp.where(lane >= starts[b], rank_b, rank)
-        counts = [c + jnp.where(near == j, live_ref[b], 0) for c, j in zip(counts, order)]
     src = sources(z_ref[0], parts)
     rank_at = z_ref[0] * own + lax.broadcasted_iota(jnp.int32, total.shape, 0)
     scale = adapter_alpha_scale / rank.astype(wide)
@@ -396,21 +407,18 @@
             cols = pl.ds(pl.multiple_of(src[i] * kw, kw), kw)
             acc_ref[:, cols] = acc_ref[:, cols] + mm(lhs[:, room:], rest_ref[i], NN)
 
-    row = lax.broadcasted_iota(jnp.int32, (tail_rows, keep_ref.shape[2]), 0)
     for k in range(per):
         for ref, at in ((keep_ref, k), (send_ref, per + k)):
-            ref[k, :own, :] = acc_ref[at * own : (at + 1) * own, :].astype(half)
-            tail = jnp.where(row == 0, counts[at] // 32, jnp.where(row == 1, counts[at] % 32, 0))
-            ref[k, own:, :] = tail.astype(wide).astype(half)
-
-
-def up_call(d, z, live, tables, hs, cots, rest, order, tail_rows=16):
+            ref[k] = acc_ref[at * own : (at + 1) * own, :].astype(half)
+
+
+def up_call(d, z, live, tables, hs, cots, rest, order):
     own, tok = hs[0].shape
     parts = len(cots)
     width = parts * cots[0].shape[1]
-    shape = jax.ShapeDtypeStruct((len(order) // 2, own + tail_rows, width), half)
-    return pl.pallas_call(
-        functools.partial(up_kernel, order, parts, len(hs), tail_rows),
+    shape = jax.ShapeDtypeStruct((len(order) // 2, own, width), half)
+    return pl.pallas_call(
+        functools.partial(up_kernel, order, parts, len(hs)),
         in_specs=[smem()] * 6 + [vmem()] * (len(hs) + len(cots) + 1),
         out_specs=[vmem()] * 2,
         out_shape=[shape, shape],
@@ -421,7 +429,7 @@
     )(d, z, live, *tables, *hs, *cots, rest)
 
 
-def up_plain(d, z, live, tables, hs, cots, rest, order, tail_rows=16):
+def up_plain(d, z, live, tables, hs, cots, rest, order):
     tenant, slot_of, rank_of = tables
     own, tok = hs[0].shape
     room = tok - rest.shape[1]
@@ -442,11 +450,7 @@
     cot.append(jnp.where(ends[-1] > room, jnp.concatenate(list(rest), axis=1), 0))
     cot = jnp.concatenate(cot, axis=0)
     grads = mm(lhs, cot, NN).astype(half).reshape(len(order), own, cot.shape[1])
-    counts = jnp.sum(jnp.where(near[:, None] == jnp.array(order)[None, :], live[:, None], 0), axis=0)
-    tail = jnp.pad(jnp.stack([counts // 32, counts % 32], axis=1), ((0, 0), (0, tail_rows - 2)))
-    tail = jnp.broadcast_to(tail.astype(half)[:, :, None], (len(order), tail_rows, cot.shape[1]))
-    both = jnp.concatenate([grads, tail], axis=1)
-    return both[: len(order) // 2], both[len(order) // 2 :]
+    return grads[: len(order) // 2], grads[len(order) // 2 :]
 
 
 def base_kernel(parts, z_ref, live_ref, w_ref, *refs):
@@ -548,7 +552,7 @@
             pltpu.VMEM((blk // 128, tok, 128), wide),
         ],
         compiler_params=kernel_params(24),
-        cost_estimate=cost(2 * tok * width * (kfull + every), 2 * (w.size + every * width + tok * (width + kfull))),
+        cost_estimate=cost(0, 4 * tok),
         name="grad_acts",
     )(z, live, w, u, base, rest, *cots, *downs)
 
@@ -581,7 +585,7 @@
     tok, width = activations.shape
     live = block_live_tokens
     slots = tenant_storage_slot.shape[0]
-    assert adapter_down_factors.shape[0] == 1 and slots == n_dp
+    assert adapter_down_factors.shape[0] == 1 and slots == n_dp and n_dp >= 4
     ranks = adapter_down_factors.shape[2]
     own_ranks = adapter_up_factors.shape[1]
     kw = output_gradient.shape[1]
@@ -598,7 +602,9 @@
         return lax.ppermute(v, "tensor", ring_pairs)
 
     room = tok * 3 // 4
-    own_b, first, rest = compact_call(live, adapter_up_factors, output_gradient, room, n_tensor)
+    own_a, own_b, first, rest = pack_call(
+        live, adapter_down_factors, adapter_up_factors, output_gradient, room, n_tensor
+    )
 
     def rest_of(v):
         out = [v[0]]
@@ -608,36 +614,36 @@
 
     cots = [first, onward(first)]
     ups = [own_b, swap(own_b, "tensor", n_tensor, 1)]
-    own_a = round_call(after(adapter_down_factors, first))
-    x = stage_call(after(activations, first))
-    weight = stage_call(after(value_weight, first))
-
-    cots[1], own_a, ups[1], x, weight = together(cots[1], own_a, ups[1], x, weight)
+    far = list(reversed(levels))
+    downs = [own_a]
+    for bits in far[:-1]:
+        downs = downs + [swap(v, "dp", n_dp, bits) for v in downs]
+
+    rest = lax.cond(jnp.sum(live) > room, rest_of, lambda v: v, rest)
+
+    cots[1], rest, *ups = together(cots[1], rest, *ups)
     cots.append(onward(cots[1]))
     bits = 2
     while bits < n_tensor:
         ups = ups + [swap(v, "tensor", n_tensor, bits) for v in ups]
         bits *= 2
-    far = list(reversed(levels))
-    downs = [own_a]
-    for bits in far[:-1]:
-        downs = downs + [swap(v, "dp", n_dp, bits) for v in downs]
-    rest = lax.cond(jnp.sum(live) > room, rest_of, lambda v: v, after(rest, cots[1]))
-    early = 2 if kw % 128 == 0 and n_tensor > 2 else 0
-    base = base_call(z_one, live, weight, cots[:early], n_tensor) if early else jnp.zeros((8, 128), wide)
-
-    cots[2], rest, base, *both = together(cots[2], rest, base, *downs, *ups)
-    downs, ups = both[: len(downs)], both[len(downs) :]
+    downs = [after(v, cots[1]) for v in downs]
+    downs = downs + [swap(v, "dp", n_dp, far[-1]) for v in downs]
+    hs = list(hidden_call(d_one, z_one, live, tables, activations, downs, order, n_tensor))
+
+    cots[2], *both = together(cots[2], *hs, *ups)
+    hs, ups = both[: len(hs)], both[len(hs) :]
     while len(cots) < n_tensor:
         cots.append(onward(cots[-1]))
-    downs = downs + [swap(v, "dp", n_dp, far[-1]) for v in downs]
-    ups = [ordered_call(z_one, ups)]
+    ups = [ordered_call(z_one, live, tables, ups)]
     for bits in far[:-1]:
         ups = ups + [swap(v, "dp", n_dp, bits) for v in ups]
-    hs = list(hidden_call(d_one, z_one, live, tables, x, downs, order, n_tensor))
-
     hs = [hs[0]] + [swap(hs[k], "tensor", n_tensor, k) for k in range(1, n_tensor)]
-    cots[-1], *both = together(cots[-1], *hs, *ups)
+    early = 3 if kw % 128 == 0 and n_tensor > 3 else 0
+    base = jnp.zeros((8, 128), wide)
+    if early:
+        base = base_call(z_one, live, value_weight, cots[:early], n_tensor)
+    cots[-1], base, *both = together(cots[-1], base, *hs, *ups)
     hs, ups = both[: len(hs)], both[len(hs) :]
     ups = ups + [swap(v, "dp", n_dp, far[-1]) for v in ups]
     if kw % 128:
@@ -646,40 +652,34 @@
         in_order = lambda v: jnp.moveaxis(v[away], 0, 1).reshape(v.shape[1], n_tensor * kw)
         cots = [in_order(jnp.stack(cots))]
         rest = in_order(rest)[None]
-    u, packed_u = upward_call(d_one, z_one, live, tables, cots, rest, ups, order)
-
-    def other_sums(total, *others):
-        for bits in levels[1:]:
+    def other_sums(total, levels, *others):
+        for bits in levels:
             n = total.shape[0] // 2
             got = after(swap(total[n:].astype(half), "dp", n_dp, bits), *others)
             total = total[:n] + got.astype(wide)
         return total[0]
 
-    rows = width // 2
-    keep_0, send_0 = down_call(x, u, ranks, 0, rows)
-    got_0 = swap(send_0, "dp", n_dp, 1)
-    keep_1, send_1 = down_call(x, after(u, send_0), ranks, rows, rows)
-    got_1 = swap(send_1, "dp", n_dp, 1)
-    hs[0] = after(hs[0], send_1)
     if own_ranks % 16:
         keep_up, send_up = up_plain(d, z, live, tables, hs, cots, rest, order)
     else:
         keep_up, send_up = up_call(d_one, z_one, live, tables, hs, cots, rest, order)
     got_up = swap(send_up, "dp", n_dp, 1)
-    down_0 = keep_0.astype(wide) + after(got_0, send_up).astype(wide)
-    down_1 = keep_1.astype(wide) + after(got_1, down_0).astype(wide)
-    up_sum = keep_up.astype(wide) + after(got_up, down_1).astype(wide)
-    grad_acts = acts_call(
-        z_one, live, weight, after(packed_u, down_1, up_sum), base, cots[early:], rest, downs
-    )
-    up_sum = other_sums(up_sum, grad_acts)
-    denom = jnp.maximum(up_sum[own_ranks, 0] * 32.0 + up_sum[own_ranks + 1, 0], 1.0)
-
-    up_grad = up_sum[None, :own_ranks] / denom
+    u, packed_u, count = upward_call(d_one, z_one, live, tables, cots, after(rest, send_up), ups, order, ranks)
+    quarter = slots // 4
+    keep_far, send_far = down_call(activations, u, ranks, 2 * quarter, quarter)
+    got_far = swap(send_far, "dp", n_dp, 1)
+    keep_near, send_near = down_call(activations, after(u, send_far), ranks, 0, quarter)
+    sum_far = (keep_far.astype(wide) + after(got_far, send_near).astype(wide)).astype(half)
+    got_far = swap(sum_far, "dp", n_dp, levels[1])
+    got_near = swap(send_near, "dp", n_dp, 1)
+    up_sum = keep_up.astype(wide) + after(got_up, sum_far).astype(wide)
+    got_near = after(got_near, up_sum)
+    grad_acts = acts_call(z_one, live, value_weight, after(packed_u, got_near), base, cots[early:], rest, downs)
+    down_sum = keep_near.astype(wide) + got_near.astype(wide) + after(got_far, grad_acts).astype(wide)
+    down_grad = other_sums(down_sum, levels[2:])[None] / count[None, :1, :ranks]
+    new_down = moment_update_rule(adapter_down_factors, down_first_moment, down_second_moment, down_grad)
+    up_grad = other_sums(up_sum, levels[1:], new_down[0])[None] / count[None, :1, :]
     new_up = moment_update_rule(adapter_up_factors, up_first_moment, up_second_moment, up_grad)
-    down_sums = [other_sums(down_0, grad_acts), other_sums(down_1, grad_acts)]
-    down_grad = jnp.concatenate(down_sums, axis=0)[None] / denom
-    new_down = moment_update_rule(adapter_down_factors, down_first_moment, down_second_moment, down_grad)
     return (grad_acts, *new_down, *new_up)
 
 

time: 84.3 us -> 80.8 us (0.958)
  local copies, waits for them, and re-layouts: 16.5 us -> 1.07 us
  Pallas kernels: 24 us -> 30.6 us
  waiting for transfers between devices: 15.2 us -> 21 us
  between operations: 3.2 us -> 1.58 us
    unnamed x52 -> x44, local copies, waits for them, and re-layouts: 15.9 us -> 1.05 us
    ppermute x18 -> x17, waiting for transfers between devices: 15.2 us -> 21 us  [swap(): return lax.ppermute(v, axis, [(i, i ^ bits) for i in range(n)])]
    pallas_call x1, Pallas kernels: 4.81 us -> 7.28 us  [hidden_call(): pl.pallas_call(functools.partial(hidden_kernel, order, groups), grid=(tok...]
    pallas_call x1, Pallas kernels: 3.37 us -> 5.52 us  [base_call(): pl.pallas_call(functools.partial(base_kernel, parts), grid=(width // blk,...]
    ppermute x18 -> x17, starting transfers between devices: 17.8 us -> 19.5 us  [swap(): return lax.ppermute(v, axis, [(i, i ^ bits) for i in range(n)])]
    pallas_call x8 -> x5, Pallas kernels: 7.14 us -> 8.56 us  [the longest x2 4.2 us: down_call(): pl.pallas_call(functools.partial(down_kernel, ranks, first), grid=(width...]
    ppermute x3, starting transfers between devices: 3.25 us -> 2.34 us  [onward(): return lax.ppermute(v, 'tensor', ring_pairs)]
  transfers between devices with their start and end apart: 21 -> 20, of which waited for: 10 -> 7; matrix products, arithmetic and copies ran while one was open for 3% -> 5% of each run, Pallas kernels for 22% -> 30%
where the time goes in v3:
time: 80.8 us; the launch traced here: 80.6 us
  Pallas kernels  30.6 us (38%)
  starting transfers between devices  21.9 us (27%)
  waiting for transfers between devices  21 us (26%)
  other arithmetic  4.47 us (6%)
  between operations  1.58 us (2%)
  local copies, waits for them, and re-layouts  1.07 us (1%)
    ppermute x17, waiting for transfers between devices, swap(): return lax.ppermute(v, axis, [(i, i ^ bits) for i in range(n)])  21 us
    ppermute x17, starting transfers between devices, swap(): return lax.ppermute(v, axis, [(i, i ^ bits) for i in range(n)])  19.5 us
    pallas_call x1, Pallas kernels, hidden_call(): pl.pallas_call(functools.partial(hidden_kernel, order, groups), grid=(tok...  7.28 us
    pallas_call x1, Pallas kernels, acts_call(): pl.pallas_call(functools.partial(acts_kernel, parts, parts - len(cots)),...  7.15 us
    pallas_call x1, Pallas kernels, base_call(): pl.pallas_call(functools.partial(base_kernel, parts), grid=(width // blk,...  5.52 us
    pallas_call x2, Pallas kernels, down_call(): pl.pallas_call(functools.partial(down_kernel, ranks, first), grid=(width...  4.2 us
    sub x2, other arithmetic, moment_update_rule(): param - learn_rate * fixed_first / (jnp.sqrt(fixed_second) + adam_eps)  3.01 us
    pallas_call x1, Pallas kernels, pack_call(): pl.pallas_call(pack_kernel, grid=(1,), in_specs=[smem(), resident(a), res...  2.63 us
  transfers between devices with their start and end apart: 20, of which 7 were waited for; matrix products, arithmetic and copies ran while one was open for 5% of the time, Pallas kernels for 30%

profile of v3, /device:TPU:0, one launch (start us, length us, event | category | flops | bytes accessed | tf_op | source)
XLA Modules:
  0.0 80.6 jit_solution(15887942743938957151)
XLA Ops:
  0.6 2.6 %pack.1 = (bf16[128,2048]{1,0:T(8,128)(2,1)}, bf16[32,1024]{1,0:T(8,128)(2,1)}, bf16[768,256]{1,0:T(8,128)(2,1)}, bf16[4,256,256]{2,1,0:T(8,128)(2,1)S(1)}) custom-call(s32[16]{0:T(128)} %live_ref.13, f32[1,2048,128]{2,1,0:T(8,128)} %a_ref.1, f32[1,32,1024]{2,1,0:T(8,128)} %b_ref.1, bf16[1024,256]{1,0:T(8,128)(2,1)} %cot_ref.1), custom_call_target="tpu_custom_call" | custom-call | bytes 2818048 | tf_op jit(solution)/shard_map/pack/pallas_call | solution.py:158
  3.3 2.9 %collective-permute-start.6 = (bf16[128,2048]{1,0:T(8,128)(2,1)}, bf16[128,2048]{1,0:T(8,128)(2,1)S(1)}, u32[]{:S(2)}, u32[]{:S(2)}) collective-permute-start(bf16[128,2048]{1,0:T(8,128)(2,1)} %get-tuple-element.65.refs_4_.refs_1_), channel_id=1, source_target_pairs={{0,8},{4,12},{8,0},{12,4},{1,9},{5,13},{9,1},{13,5},{2,10},{6,14},... | collective-permute-start | bytes 1572872 | tf_op jit(solution)/shard_map/ppermute | solution.py:57
  6.2 1.6 %collective-permute-start.3 = (bf16[768,256]{1,0:T(8,128)(2,1)}, bf16[768,256]{1,0:T(8,128)(2,1)S(1)}, u32[]{:S(2)}, u32[]{:S(2)}) collective-permute-start(bf16[768,256]{1,0:T(8,128)(2,1)} %get-tuple-element.60.refs_0_.refs_7_.refs_3_), channel_id=1, source_target_pairs={{0,1},{1,3},{3,2},{2,0},{4,5},{5,7},{7,6},{6,4},{8,9},{9,11},{11,1... | collective-permute-start | bytes 1179656 | tf_op jit(solution)/shard_map/ppermute | solution.py:602
  7.8 2.6 %collective-permute-start.4 = (bf16[32,1024]{1,0:T(8,128)(2,1)}, bf16[32,1024]{1,0:T(8,128)(2,1)S(1)}, u32[]{:S(2)}, u32[]{:S(2)}) collective-permute-start(bf16[32,1024]{1,0:T(8,128)(2,1)} %get-tuple-element.78.refs_0_), channel_id=1, source_target_pairs={{0,1},{1,0},{2,3},{3,2},{4,5},{5,4},{6,7},{7,6},{8,9},{9,8},{10,11... | collective-permute-start | bytes 196616 | tf_op jit(solution)/shard_map/ppermute | solution.py:57
  10.4 1.3 %reduce_sum.9 = s32[]{:T(128)} reduce(s32[16]{0:T(128)} %live_ref.13, s32[]{:T(128)} %constant.13.clone.1), dimensions={0}, to_apply=%region_0.0 | reduce | flops 15 | bytes 72 | tf_op jit(solution)/shard_map/reduce_sum | solution.py:622
  12.4 6.9 %collective-permute-done.4.refs_1_ = bf16[32,1024]{1,0:T(8,128)(2,1)S(1)} collective-permute-done((bf16[32,1024]{1,0:T(8,128)(2,1)}, bf16[32,1024]{1,0:T(8,128)(2,1)S(1)}, u32[]{:S(2)}, u32[]{:S(2)}) %collective-permute-start.4) | collective-permute-done | bytes 65568 | tf_op jit(solution)/shard_map/ppermute | solution.py:57
  19.3 0.5 collective-permute-start.8
  19.8 0.7 collective-permute-start.5
  20.5 2.2 %collective-permute-start.9 = (bf16[32,1024]{1,0:T(8,128)(2,1)}, bf16[32,1024]{1,0:T(8,128)(2,1)S(1)}, u32[]{:S(2)}, u32[]{:S(2)}) collective-permute-start(bf16[32,1024]{1,0:T(8,128)(2,1)} %get-tuple-element.78.refs_0_), channel_id=1, source_target_pairs={{0,2},{1,3},{2,0},{3,1},{4,6},{5,7},{6,4},{7,5},{8,10},{9,11},{10,... | collective-permute-start | bytes 196616 | tf_op jit(solution)/shard_map/ppermute | solution.py:57
  22.7 0.7 collective-permute-start.10
  23.4 0.8 copy-done.6
  24.4 7.3 %hidden.1 = (bf16[32,1024]{1,0:T(8,128)(2,1)}, bf16[32,1024]{1,0:T(8,128)(2,1)}, bf16[32,1024]{1,0:T(8,128)(2,1)}, bf16[32,1024]{1,0:T(8,128)(2,1)}) custom-call(s32[1]{0:T(128)} %bitcast.5.d_ref, s32[1]{0:T(128)} %bitcast.4.z_ref, s32[16]{0:T(128)} %live_ref.13, s32[16]{0:T(128)} %refs_0_.5, s32[4]{0:T(128)} %refs_1_.5, s32[4]{0:T(128)} %refs_2_.5, ...), custom_call_target="tpu_custom_call" | custom-call | flops 2147483648 | bytes 6291456 | tf_op jit(solution)/shard_map/hidden/pallas_call | solution.py:259
  31.7 5.1 %collective-permute-done.9.refs_2_ = bf16[32,1024]{1,0:T(8,128)(2,1)S(1)} collective-permute-done((bf16[32,1024]{1,0:T(8,128)(2,1)}, bf16[32,1024]{1,0:T(8,128)(2,1)S(1)}, u32[]{:S(2)}, u32[]{:S(2)}) %collective-permute-start.9) | collective-permute-done | bytes 65568 | tf_op jit(solution)/shard_map/ppermute | solution.py:57
  36.7 0.7 collective-permute-done.10.refs_3_
  37.5 0.7 ordered.1.refs_8_
  38.3 1.5 %collective-permute-start.15 = (bf16[144,1024]{1,0:T(8,128)(2,1)S(1)}, bf16[144,1024]{1,0:T(8,128)(2,1)S(1)}, u32[]{:S(2)}, u32[]{:S(2)}) collective-permute-start(bf16[144,1024]{1,0:T(8,128)(2,1)S(1)} %ordered.1.refs_8_), channel_id=1, source_target_pairs={{0,8},{4,12},{8,0},{12,4},{1,9},{5,13},{9,1},{13,5},{2,10},{6,14},... | collective-permute-start | bytes 884744 | tf_op jit(solution)/shard_map/ppermute | solution.py:57
  39.7 3.4 %collective-permute-start.12 = (bf16[32,1024]{1,0:T(8,128)(2,1)}, bf16[32,1024]{1,0:T(8,128)(2,1)S(1)}, u32[]{:S(2)}, u32[]{:S(2)}) collective-permute-start(bf16[32,1024]{1,0:T(8,128)(2,1)} %get-tuple-element.75), channel_id=1, source_target_pairs={{0,1},{1,0},{2,3},{3,2},{4,5},{5,4},{6,7},{7,6},{8,9},{9,8},{10,11... | collective-permute-start | bytes 196616 | tf_op jit(solution)/shard_map/ppermute | solution.py:57
  43.1 2.3 %collective-permute-start.14 = (bf16[32,1024]{1,0:T(8,128)(2,1)}, bf16[32,1024]{1,0:T(8,128)(2,1)S(1)}, u32[]{:S(2)}, u32[]{:S(2)}) collective-permute-start(bf16[32,1024]{1,0:T(8,128)(2,1)} %get-tuple-element.77), channel_id=1, source_target_pairs={{0,3},{1,2},{2,1},{3,0},{4,7},{5,6},{6,5},{7,4},{8,11},{9,10},{10,... | collective-permute-start | bytes 196616 | tf_op jit(solution)/shard_map/ppermute | solution.py:57
  45.5 5.5 %base.1.base_ref = f32[768,2048]{1,0:T(8,128)S(1)} custom-call(s32[1]{0:T(128)} %bitcast.4.z_ref, s32[16]{0:T(128)S(1)} %copy-done.12, bf16[2048,1024]{1,0:T(8,128)(2,1)S(1)} %copy-done.1, bf16[768,256]{1,0:T(8,128)(2,1)S(1)} %copy-done.2, bf16[768,256]{1,0:T(8,128)(2,1)S(1)} %collective-permute-done.3.refs_1_.refs_8_.refs_4_, ...), custom_call_target="tpu_custom_call" | custom-call | flops 2415919104 | bytes 6291456 | tf_op jit(solution)/shard_map/base/pallas_call | solution.py:480
  51.0 2.5 %collective-permute-done.13.refs_5_ = bf16[32,1024]{1,0:T(8,128)(2,1)S(1)} collective-permute-done((bf16[32,1024]{1,0:T(8,128)(2,1)}, bf16[32,1024]{1,0:T(8,128)(2,1)S(1)}, u32[]{:S(2)}, u32[]{:S(2)}) %collective-permute-start.13) | collective-permute-done | bytes 65568 | tf_op jit(solution)/shard_map/ppermute | solution.py:57
  53.6 0.5 collective-permute-start.17
  54.1 1.0 %up_grad.1 = (bf16[2,32,1024]{2,1,0:T(8,128)(2,1)S(1)}, bf16[2,32,1024]{2,1,0:T(8,128)(2,1)S(1)}) custom-call(s32[1]{0:T(128)} %bitcast.5.d_ref, s32[1]{0:T(128)} %bitcast.4.z_ref, s32[16]{0:T(128)S(1)} %copy-done.12, s32[16]{0:T(128)S(1)} %copy-done.13, s32[4]{0:T(128)S(1)} %copy-done.14, s32[4]{0:T(128)S(1)} %copy-done.15, ...), custom_call_target="tpu_custom_call" | custom-call | flops 268435456 | bytes 4194304 | tf_op jit(solution)/shard_map/up_grad/pallas_call | solution.py:420
  55.6 2.1 %upward.1 = (bf16[1024,512]{1,0:T(8,128)(2,1)S(1)}, bf16[1024,512]{1,0:T(8,128)(2,1)S(1)}, f32[8,1024]{1,0:T(8,128)S(1)}) custom-call(s32[1]{0:T(128)} %bitcast.5.d_ref, s32[1]{0:T(128)} %bitcast.4.z_ref, s32[16]{0:T(128)S(1)} %copy-done.12, s32[16]{0:T(128)S(1)} %copy-done.13, s32[4]{0:T(128)S(1)} %copy-done.14, s32[4]{0:T(128)S(1)} %copy-done.15, ...), custom_call_target="tpu_custom_call" | custom-call | flops 1073741824 | bytes 4194304 | tf_op jit(solution)/shard_map/upward/pallas_call | solution.py:335
  57.8 2.1 %down_grad.2 = (bf16[1,2048,128]{2,1,0:T(8,128)(2,1)S(1)}, bf16[1,2048,128]{2,1,0:T(8,128)(2,1)S(1)}) custom-call(bf16[1024,2048]{1,0:T(8,128)(2,1)S(1)} %copy-done, bf16[1024,512]{1,0:T(8,128)(2,1)S(1)} %get-tuple-element.95.u_ref), custom_call_target="tpu_custom_call" | custom-call | bytes 4096 | tf_op jit(solution)/shard_map/down_grad/pallas_call | solution.py:364
  60.1 2.1 %down_grad.3 = (bf16[1,2048,128]{2,1,0:T(8,128)(2,1)S(1)}, bf16[1,2048,128]{2,1,0:T(8,128)(2,1)S(1)}) custom-call(bf16[1024,2048]{1,0:T(8,128)(2,1)S(1)} %copy-done, bf16[1024,512]{1,0:T(8,128)(2,1)S(1)} %get-tuple-element.95.u_ref), custom_call_target="tpu_custom_call" | custom-call | bytes 4096 | tf_op jit(solution)/shard_map/down_grad/pallas_call | solution.py:364
  62.8 1.5 %collective-permute-start.21 = (bf16[1,2048,128]{2,1,0:T(8,128)(2,1)S(1)}, bf16[1,2048,128]{2,1,0:T(8,128)(2,1)S(1)}, u32[]{:S(2)}, u32[]{:S(2)}) collective-permute-start(bf16[1,2048,128]{2,1,0:T(8,128)(2,1)S(1)} %add_convert_fusion), channel_id=1, source_target_pairs={{0,8},{4,12},{8,0},{12,4},{1,9},{5,13},{9,1},{13,5},{2,10},{6,14},... | collective-permute-start | bytes 1572872 | tf_op jit(solution)/shard_map/ppermute | solution.py:57
  64.3 1.3 %collective-permute-done.19 = bf16[2,32,1024]{2,1,0:T(8,128)(2,1)S(1)} collective-permute-done((bf16[2,32,1024]{2,1,0:T(8,128)(2,1)S(1)}, bf16[2,32,1024]{2,1,0:T(8,128)(2,1)S(1)}, u32[]{:S(2)}, u32[]{:S(2)}) %collective-permute-start.19) | collective-permute-done | bytes 131104 | tf_op jit(solution)/shard_map/ppermute | solution.py:57
  65.8 0.6 collective-permute-start.22
  66.4 7.2 %grad_acts.1 = bf16[1024,2048]{1,0:T(8,128)(2,1)} custom-call(s32[1]{0:T(128)} %bitcast.4.z_ref, s32[16]{0:T(128)S(1)} %copy-done.12, bf16[2048,1024]{1,0:T(8,128)(2,1)S(1)} %copy-done.1, bf16[1024,512]{1,0:T(8,128)(2,1)S(1)} %get-tuple-element.102.u_ref, f32[768,2048]{1,0:T(8,128)S(1)} %base.1.base_ref, ...), custom_call_target="tpu_custom_call" | custom-call | bytes 4096 | tf_op jit(solution)/shard_map/grad_acts/pallas_call | solution.py:542
  73.6 4.0 %collective-permute-done.21 = bf16[1,2048,128]{2,1,0:T(8,128)(2,1)S(1)} collective-permute-done((bf16[1,2048,128]{2,1,0:T(8,128)(2,1)S(1)}, bf16[1,2048,128]{2,1,0:T(8,128)(2,1)S(1)}, u32[]{:S(2)}, u32[]{:S(2)}) %collective-permute-start.21) | collective-permute-done | bytes 524320 | tf_op jit(solution)/shard_map/ppermute | solution.py:57
  77.6 2.2 %divide_subtract_fusion = (f32[1,2048,128]{2,1,0:T(8,128)}, f32[1,2048,128]{2,1,0:T(8,128)}, f32[1,2048,128]{2,1,0:T(8,128)}) fusion(f32[1,2048,128]{2,1,0:T(8,128)S(1)} %copy-done.16, f32[128]{0:T(128)S(1)} %slice_bitcast_fusion.1, bf16[1,2048,128]{2,1,0:T(8,128)(2,1)S(1)} %collective-permute-done.21, bf16[1,2048,128]{2,1,0:T(8,128)(2,1)S(1)} %collective-permute-done.18, ...), kind=kLoop, calls=%fused_computation.4 | loop fusion | flops 4718592 | bytes 7864832 | tf_op jit(solution)/shard_map/sub | solution.py:34
  79.8 0.8 %divide_subtract_fusion.1 = (f32[1,32,1024]{2,1,0:T(8,128)}, f32[1,32,1024]{2,1,0:T(8,128)}, f32[1,32,1024]{2,1,0:T(8,128)}) fusion(f32[1,32,1024]{2,1,0:T(8,128)S(1)} %copy-done.19, f32[1024]{0:T(1024)S(1)} %bitcast.13, bf16[1,32,1024]{2,1,0:T(8,128)(2,1)S(1)} %collective-permute-done.22, f32[2,32,1024]{2,1,0:T(8,128)S(1)} %convert_add_fusion, ...), kind=kLoop, calls=%fused_computation.14 | loop fusion | flops 491520 | bytes 987136 | tf_op jit(solution)/shard_map/sub | solution.py:34
  (70 shorter events, 1.8 us)
Async XLA Ops:
  3.3 16.1 %collective-permute-start.6 = (bf16[128,2048]{1,0:T(8,128)(2,1)}, bf16[128,2048]{1,0:T(8,128)(2,1)S(1)}, u32[]{:S(2)}, u32[]{:S(2)}) collective-permute-start(bf16[128,2048]{1,0:T(8,128)(2,1)} %get-tuple-element.65.refs_4_.refs_1_), channel_id=1, source_target_pairs={{0,8},{4,12},{8,0},{12,4},{1,9},{5,13},{9,1},{13,5},{2,10},{6,14},... | collective-permute-start | bytes 1572872 | tf_op jit(solution)/shard_map/ppermute | solution.py:57
  6.2 13.1 %collective-permute-start.3 = (bf16[768,256]{1,0:T(8,128)(2,1)}, bf16[768,256]{1,0:T(8,128)(2,1)S(1)}, u32[]{:S(2)}, u32[]{:S(2)}) collective-permute-start(bf16[768,256]{1,0:T(8,128)(2,1)} %get-tuple-element.60.refs_0_.refs_7_.refs_3_), channel_id=1, source_target_pairs={{0,1},{1,3},{3,2},{2,0},{4,5},{5,7},{7,6},{6,4},{8,9},{9,11},{11,1... | collective-permute-start | bytes 1179656 | tf_op jit(solution)/shard_map/ppermute | solution.py:602
  7.8 11.5 %collective-permute-start.4 = (bf16[32,1024]{1,0:T(8,128)(2,1)}, bf16[32,1024]{1,0:T(8,128)(2,1)S(1)}, u32[]{:S(2)}, u32[]{:S(2)}) collective-permute-start(bf16[32,1024]{1,0:T(8,128)(2,1)} %get-tuple-element.78.refs_0_), channel_id=1, source_target_pairs={{0,1},{1,0},{2,3},{3,2},{4,5},{5,4},{6,7},{7,6},{8,9},{9,8},{10,11... | collective-permute-start | bytes 196616 | tf_op jit(solution)/shard_map/ppermute | solution.py:57
  12.3 25.2 %copy-start.10 = (bf16[32,1024]{1,0:T(8,128)(2,1)S(1)}, bf16[32,1024]{1,0:T(8,128)(2,1)}, u32[]{:S(2)}) copy-start(bf16[32,1024]{1,0:T(8,128)(2,1)} %get-tuple-element.78.refs_0_) | copy-start | bytes 196612
  12.3 25.2 %copy-start.12 = (s32[16]{0:T(128)S(1)}, s32[16]{0:T(128)}, u32[]{:S(2)}) copy-start(s32[16]{0:T(128)} %live_ref.13) | copy-start | bytes 196
  12.4 25.2 %copy-start.13 = (s32[16]{0:T(128)S(1)}, s32[16]{0:T(128)}, u32[]{:S(2)}) copy-start(s32[16]{0:T(128)} %refs_0_.5) | copy-start | bytes 196
  12.4 25.2 %copy-start.14 = (s32[4]{0:T(128)S(1)}, s32[4]{0:T(128)}, u32[]{:S(2)}) copy-start(s32[4]{0:T(128)} %refs_1_.5) | copy-start | bytes 52
  19.3 4.1 %collective-permute-start.7 = (bf16[128,2048]{1,0:T(8,128)(2,1)}, bf16[128,2048]{1,0:T(8,128)(2,1)S(1)}, u32[]{:S(2)}, u32[]{:S(2)}) collective-permute-start(bf16[128,2048]{1,0:T(8,128)(2,1)} %get-tuple-element.65.refs_4_.refs_1_), channel_id=1, source_target_pairs={{0,4},{4,0},{8,12},{12,8},{1,5},{5,1},{9,13},{13,9},{2,6},{6,2},{1... | collective-permute-start | bytes 1572872 | tf_op jit(solution)/shard_map/ppermute | solution.py:57
  19.3 4.1 %collective-permute-start.8 = (bf16[128,2048]{1,0:T(8,128)(2,1)S(1)}, bf16[128,2048]{1,0:T(8,128)(2,1)S(1)}, u32[]{:S(2)}, u32[]{:S(2)}) collective-permute-start(bf16[128,2048]{1,0:T(8,128)(2,1)S(1)} %collective-permute-done.6.refs_5_.refs_2_), channel_id=1, source_target_pairs={{0,4},{4,0},{8,12},{12,8},{1,5},{5,1},{9,13},{13,9},{2,6},{6,2},{1... | collective-permute-start | bytes 1572872 | tf_op jit(solution)/shard_map/ppermute | solution.py:57
  19.8 17.6 %collective-permute-start.5 = (bf16[768,256]{1,0:T(8,128)(2,1)S(1)}, bf16[768,256]{1,0:T(8,128)(2,1)S(1)}, u32[]{:S(2)}, u32[]{:S(2)}) collective-permute-start(bf16[768,256]{1,0:T(8,128)(2,1)S(1)} %collective-permute-done.3.refs_1_.refs_8_.refs_4_), channel_id=1, source_target_pairs={{0,1},{1,3},{3,2},{2,0},{4,5},{5,7},{7,6},{6,4},{8,9},{9,11},{11,1... | collective-permute-start | bytes 1179656 | tf_op jit(solution)/shard_map/ppermute | solution.py:602
  20.5 16.2 %collective-permute-start.9 = (bf16[32,1024]{1,0:T(8,128)(2,1)}, bf16[32,1024]{1,0:T(8,128)(2,1)S(1)}, u32[]{:S(2)}, u32[]{:S(2)}) collective-permute-start(bf16[32,1024]{1,0:T(8,128)(2,1)} %get-tuple-element.78.refs_0_), channel_id=1, source_target_pairs={{0,2},{1,3},{2,0},{3,1},{4,6},{5,7},{6,4},{7,5},{8,10},{9,11},{10,... | collective-permute-start | bytes 196616 | tf_op jit(solution)/shard_map/ppermute | solution.py:57
  22.7 14.7 %collective-permute-start.10 = (bf16[32,1024]{1,0:T(8,128)(2,1)S(1)}, bf16[32,1024]{1,0:T(8,128)(2,1)S(1)}, u32[]{:S(2)}, u32[]{:S(2)}) collective-permute-start(bf16[32,1024]{1,0:T(8,128)(2,1)S(1)} %collective-permute-done.4.refs_1_), channel_id=1, source_target_pairs={{0,2},{1,3},{2,0},{3,1},{4,6},{5,7},{6,4},{7,5},{8,10},{9,11},{10,... | collective-permute-start | bytes 196616 | tf_op jit(solution)/shard_map/ppermute | solution.py:57
  24.4 21.1 %copy-start.1 = (bf16[2048,1024]{1,0:T(8,128)(2,1)S(1)}, bf16[2048,1024]{1,0:T(8,128)(2,1)}, u32[]{:S(2)}) copy-start(bf16[2048,1024]{1,0:T(8,128)(2,1)} %w_ref.3) | copy-start | bytes 12582916
  24.4 21.1 %copy-start.2 = (bf16[768,256]{1,0:T(8,128)(2,1)S(1)}, bf16[768,256]{1,0:T(8,128)(2,1)}, u32[]{:S(2)}) copy-start(bf16[768,256]{1,0:T(8,128)(2,1)} %get-tuple-element.60.refs_0_.refs_7_.refs_3_) | copy-start | bytes 1179652
  37.4 16.1 %collective-permute-start.11 = (bf16[768,256]{1,0:T(8,128)(2,1)S(1)}, bf16[768,256]{1,0:T(8,128)(2,1)S(1)}, u32[]{:S(2)}, u32[]{:S(2)}) collective-permute-start(bf16[768,256]{1,0:T(8,128)(2,1)S(1)} %collective-permute-done.5.refs_2_.refs_9_.refs_5_), channel_id=1, source_target_pairs={{0,1},{1,3},{3,2},{2,0},{4,5},{5,7},{7,6},{6,4},{8,9},{9,11},{11,1... | collective-permute-start | bytes 1179656 | tf_op jit(solution)/shard_map/ppermute | solution.py:602
  38.2 15.9 %copy-start.11 = (bf16[32,1024]{1,0:T(8,128)(2,1)S(1)}, bf16[32,1024]{1,0:T(8,128)(2,1)}, u32[]{:S(2)}) copy-start(bf16[32,1024]{1,0:T(8,128)(2,1)} %get-tuple-element.84.refs_3_) | copy-start | bytes 196612
  38.2 15.9 %copy-start.15 = (s32[4]{0:T(128)S(1)}, s32[4]{0:T(128)}, u32[]{:S(2)}) copy-start(s32[4]{0:T(128)} %refs_2_.5) | copy-start | bytes 52
  38.3 15.3 %collective-permute-start.15 = (bf16[144,1024]{1,0:T(8,128)(2,1)S(1)}, bf16[144,1024]{1,0:T(8,128)(2,1)S(1)}, u32[]{:S(2)}, u32[]{:S(2)}) collective-permute-start(bf16[144,1024]{1,0:T(8,128)(2,1)S(1)} %ordered.1.refs_8_), channel_id=1, source_target_pairs={{0,8},{4,12},{8,0},{12,4},{1,9},{5,13},{9,1},{13,5},{2,10},{6,14},... | collective-permute-start | bytes 884744 | tf_op jit(solution)/shard_map/ppermute | solution.py:57
  39.7 11.3 %collective-permute-start.12 = (bf16[32,1024]{1,0:T(8,128)(2,1)}, bf16[32,1024]{1,0:T(8,128)(2,1)S(1)}, u32[]{:S(2)}, u32[]{:S(2)}) collective-permute-start(bf16[32,1024]{1,0:T(8,128)(2,1)} %get-tuple-element.75), channel_id=1, source_target_pairs={{0,1},{1,0},{2,3},{3,2},{4,5},{5,4},{6,7},{7,6},{8,9},{9,8},{10,11... | collective-permute-start | bytes 196616 | tf_op jit(solution)/shard_map/ppermute | solution.py:57
  43.1 10.4 %collective-permute-start.13 = (bf16[32,1024]{1,0:T(8,128)(2,1)}, bf16[32,1024]{1,0:T(8,128)(2,1)S(1)}, u32[]{:S(2)}, u32[]{:S(2)}) collective-permute-start(bf16[32,1024]{1,0:T(8,128)(2,1)} %get-tuple-element.76), channel_id=1, source_target_pairs={{0,2},{1,3},{2,0},{3,1},{4,6},{5,7},{6,4},{7,5},{8,10},{9,11},{10,... | collective-permute-start | bytes 196616 | tf_op jit(solution)/shard_map/ppermute | solution.py:57
  43.1 10.4 %collective-permute-start.14 = (bf16[32,1024]{1,0:T(8,128)(2,1)}, bf16[32,1024]{1,0:T(8,128)(2,1)S(1)}, u32[]{:S(2)}, u32[]{:S(2)}) collective-permute-start(bf16[32,1024]{1,0:T(8,128)(2,1)} %get-tuple-element.77), channel_id=1, source_target_pairs={{0,3},{1,2},{2,1},{3,0},{4,7},{5,6},{6,5},{7,4},{8,11},{9,10},{10,... | collective-permute-start | bytes 196616 | tf_op jit(solution)/shard_map/ppermute | solution.py:57
  51.0 6.7 %copy-start = (bf16[1024,2048]{1,0:T(8,128)(2,1)S(1)}, bf16[1024,2048]{1,0:T(8,128)(2,1)}, u32[]{:S(2)}) copy-start(bf16[1024,2048]{1,0:T(8,128)(2,1)} %x_ref.3) | copy-start | bytes 12582916
  53.6 1.6 %collective-permute-start.16 = (bf16[144,1024]{1,0:T(8,128)(2,1)S(1)}, bf16[144,1024]{1,0:T(8,128)(2,1)S(1)}, u32[]{:S(2)}, u32[]{:S(2)}) collective-permute-start(bf16[144,1024]{1,0:T(8,128)(2,1)S(1)} %ordered.1.refs_8_), channel_id=1, source_target_pairs={{0,4},{4,0},{8,12},{12,8},{1,5},{5,1},{9,13},{13,9},{2,6},{6,2},{1... | collective-permute-start | bytes 884744 | tf_op jit(solution)/shard_map/ppermute | solution.py:57
  53.6 2.0 %collective-permute-start.17 = (bf16[144,1024]{1,0:T(8,128)(2,1)S(1)}, bf16[144,1024]{1,0:T(8,128)(2,1)S(1)}, u32[]{:S(2)}, u32[]{:S(2)}) collective-permute-start(bf16[144,1024]{1,0:T(8,128)(2,1)S(1)} %collective-permute-done.15.refs_9_), channel_id=1, source_target_pairs={{0,4},{4,0},{8,12},{12,8},{1,5},{5,1},{9,13},{13,9},{2,6},{6,2},{1... | collective-permute-start | bytes 884744 | tf_op jit(solution)/shard_map/ppermute | solution.py:57
  59.9 2.8 %collective-permute-start.20 = (bf16[1,2048,128]{2,1,0:T(8,128)(2,1)S(1)}, bf16[1,2048,128]{2,1,0:T(8,128)(2,1)S(1)}, u32[]{:S(2)}, u32[]{:S(2)}) collective-permute-start(bf16[1,2048,128]{2,1,0:T(8,128)(2,1)S(1)} %get-tuple-element.94), channel_id=1, source_target_pairs={{0,4},{4,0},{8,12},{12,8},{1,5},{5,1},{9,13},{13,9},{2,6},{6,2},{1... | collective-permute-start | bytes 1572872 | tf_op jit(solution)/shard_map/ppermute | solution.py:57
  62.2 3.5 %collective-permute-start.18 = (bf16[1,2048,128]{2,1,0:T(8,128)(2,1)S(1)}, bf16[1,2048,128]{2,1,0:T(8,128)(2,1)S(1)}, u32[]{:S(2)}, u32[]{:S(2)}) collective-permute-start(bf16[1,2048,128]{2,1,0:T(8,128)(2,1)S(1)} %get-tuple-element.96), channel_id=1, source_target_pairs={{0,4},{4,0},{8,12},{12,8},{1,5},{5,1},{9,13},{13,9},{2,6},{6,2},{1... | collective-permute-start | bytes 1572872 | tf_op jit(solution)/shard_map/ppermute | solution.py:57
  62.8 14.8 %collective-permute-start.21 = (bf16[1,2048,128]{2,1,0:T(8,128)(2,1)S(1)}, bf16[1,2048,128]{2,1,0:T(8,128)(2,1)S(1)}, u32[]{:S(2)}, u32[]{:S(2)}) collective-permute-start(bf16[1,2048,128]{2,1,0:T(8,128)(2,1)S(1)} %add_convert_fusion), channel_id=1, source_target_pairs={{0,8},{4,12},{8,0},{12,4},{1,9},{5,13},{9,1},{13,5},{2,10},{6,14},... | collective-permute-start | bytes 1572872 | tf_op jit(solution)/shard_map/ppermute | solution.py:57
  64.3 1.3 %collective-permute-start.19 = (bf16[2,32,1024]{2,1,0:T(8,128)(2,1)S(1)}, bf16[2,32,1024]{2,1,0:T(8,128)(2,1)S(1)}, u32[]{:S(2)}, u32[]{:S(2)}) collective-permute-start(bf16[2,32,1024]{2,1,0:T(8,128)(2,1)S(1)} %get-tuple-element.88), channel_id=1, source_target_pairs={{0,4},{4,0},{8,12},{12,8},{1,5},{5,1},{9,13},{13,9},{2,6},{6,2},{1... | collective-permute-start | bytes 393224 | tf_op jit(solution)/shard_map/ppermute | solution.py:57
  65.7 11.8 %copy-start.16 = (f32[1,2048,128]{2,1,0:T(8,128)S(1)}, f32[1,2048,128]{2,1,0:T(8,128)}, u32[]{:S(2)}) copy-start(f32[1,2048,128]{2,1,0:T(8,128)} %a_ref.1) | copy-start | bytes 3145732
  65.7 11.8 %copy-start.17 = (f32[1,2048,128]{2,1,0:T(8,128)S(1)}, f32[1,2048,128]{2,1,0:T(8,128)}, u32[]{:S(2)}) copy-start(f32[1,2048,128]{2,1,0:T(8,128)} %param.20) | copy-start | bytes 3145732
  65.8 11.8 %copy-start.18 = (f32[1,2048,128]{2,1,0:T(8,128)S(1)}, f32[1,2048,128]{2,1,0:T(8,128)}, u32[]{:S(2)}) copy-start(f32[1,2048,128]{2,1,0:T(8,128)} %param.21) | copy-start | bytes 3145732
  65.8 14.0 %collective-permute-start.22 = (bf16[1,32,1024]{2,1,0:T(8,128)(2,1)S(1)}, bf16[1,32,1024]{2,1,0:T(8,128)(2,1)S(1)}, u32[]{:S(2)}, u32[]{:S(2)}) collective-permute-start(bf16[1,32,1024]{2,1,0:T(8,128)(2,1)S(1)} %slice.32), channel_id=1, source_target_pairs={{0,8},{4,12},{8,0},{12,4},{1,9},{5,13},{9,1},{13,5},{2,10},{6,14},... | collective-permute-start | bytes 196616 | tf_op jit(solution)/shard_map/ppermute | solution.py:57
  (10 other events, 50.7 us)

commit v4 on v3

--- a/solution.py
+++ b/solution.py
@@ -126,7 +126,28 @@
     )(a)
 
 
-def pack_kernel(live_ref, a_ref, b_ref, cot_ref, down_ref, up_ref, first_ref, rest_ref, all_ref):
+def round_kernel(a_ref, low_ref, high_ref):
+    turned = a_ref[0].T.astype(half)
+    low_ref[...] = turned[: low_ref.shape[0]]
+    high_ref[...] = turned[low_ref.shape[0] :]
+
+
+def round_call(a):
+    _, width, ranks = a.shape
+    blk = width
+    return pl.pallas_call(
+        round_kernel,
+        grid=(width // blk,),
+        in_specs=[pl.BlockSpec((1, blk, ranks), lambda i: (0, i, 0))],
+        out_specs=[pl.BlockSpec((ranks // 2, blk), lambda i: (0, i))] * 2,
+        out_shape=[jax.ShapeDtypeStruct((ranks // 2, width), half)] * 2,
+        compiler_params=kernel_params(16),
+        cost_estimate=cost(0, 6 * a.size),
+        name="round_factors",
+    )(a)
+
+
+def pack_kernel(live_ref, b_ref, cot_ref, up_ref, first_ref, rest_ref, all_ref):
     blocks = live_ref.shape[0]
     blk_len = cot_ref.shape[0] // blocks
     starts, _ = starts_of(live_ref)
@@ -143,13 +164,11 @@
         first_ref[:, cols] = all_ref[p, :room, :].astype(half)
         rest_ref[0, :, cols] = all_ref[p, room:, :].astype(half)
     up_ref[...] = b_ref[0].astype(half)
-    down_ref[...] = a_ref[0].T.astype(half)
-
-
-def pack_call(live, a, b, cot, room, copies):
+
+
+def pack_call(live, b, cot, room, copies):
     tok, kw = cot.shape
     shapes = [
-        jax.ShapeDtypeStruct((a.shape[2], a.shape[1]), half),
         jax.ShapeDtypeStruct(b.shape[1:], half),
         jax.ShapeDtypeStruct((room, kw), half),
         jax.ShapeDtypeStruct((copies, tok - room, kw), half),
@@ -158,14 +177,14 @@
     return pl.pallas_call(
         pack_kernel,
         grid=(1,),
-        in_specs=[smem(), resident(a), resident(b), resident(cot)],
+        in_specs=[smem(), resident(b), resident(cot)],
         out_specs=specs,
         out_shape=shapes,
         scratch_shapes=[pltpu.VMEM((kw // min(kw, 128), tok, min(kw, 128)), wide)],
         compiler_params=kernel_params(56),
-        cost_estimate=cost(0, 4 * tok * kw + 6 * (a.size + b.size)),
+        cost_estimate=cost(0, 4 * tok * kw + 6 * b.size),
         name="pack",
-    )(live, a, b, cot)
+    )(live, b, cot)
 
 
 def ordered_kernel(z_ref, live_ref, tenant_ref, slot_ref, *refs):
@@ -260,8 +279,7 @@
         functools.partial(hidden_kernel, order, groups),
         grid=(tok // blk,),
         in_specs=[smem()] * 6
-        + [vmem()]
-        + [resident(a) for a in downs],
+        + [vmem()] * (1 + len(downs)),
         out_specs=[resident(shape)] * groups,
         out_shape=[shape] * groups,
         scratch_shapes=[
@@ -270,8 +288,8 @@
             pltpu.VMEM((tok, ranks), wide),
             pltpu.VMEM((ranks, tok), wide),
         ],
-        compiler_params=kernel_params(56),
-        cost_estimate=cost(2 * tok * width * ranks * len(order), 2 * (x.size + 4 * downs[0].size)),
+        compiler_params=kernel_params(24),
+        cost_estimate=cost(0, 4 * tok),
         name="hidden",
     )(d, z, live, *tables, x, *downs)
 
@@ -602,9 +620,7 @@
         return lax.ppermute(v, "tensor", ring_pairs)
 
     room = tok * 3 // 4
-    own_a, own_b, first, rest = pack_call(
-        live, adapter_down_factors, adapter_up_factors, output_gradient, room, n_tensor
-    )
+    own_b, first, rest = pack_call(live, adapter_up_factors, output_gradient, room, n_tensor)
 
     def rest_of(v):
         out = [v[0]]
@@ -615,9 +631,10 @@
     cots = [first, onward(first)]
     ups = [own_b, swap(own_b, "tensor", n_tensor, 1)]
     far = list(reversed(levels))
-    downs = [own_a]
+    downs = list(round_call(after(adapter_down_factors, first)))
     for bits in far[:-1]:
         downs = downs + [swap(v, "dp", n_dp, bits) for v in downs]
+
 
     rest = lax.cond(jnp.sum(live) > room, rest_of, lambda v: v, rest)
 

time: 80.8 us -> 78.7 us (0.974)
  waiting for transfers between devices: 21 us -> 15.7 us
  local copies, waits for them, and re-layouts: 1.07 us -> 6.13 us
  Pallas kernels: 30.6 us -> 27.2 us
  starting transfers between devices: 21.9 us -> 23.3 us
    ppermute x17 -> x20, waiting for transfers between devices: 21 us -> 15.7 us  [swap(): return lax.ppermute(v, axis, [(i, i ^ bits) for i in range(n)])]
    unnamed x44, local copies, waits for them, and re-layouts: 1.05 us -> 6.11 us
    pallas_call x1, Pallas kernels: 7.28 us -> 4.18 us  [hidden_call(): pl.pallas_call(functools.partial(hidden_kernel, order, groups), grid=(tok...]
    ppermute x3, starting transfers between devices: 2.34 us -> 4.59 us  [onward(): return lax.ppermute(v, 'tensor', ring_pairs)]
    ppermute x17 -> x20, starting transfers between devices: 19.5 us -> 18.7 us  [swap(): return lax.ppermute(v, axis, [(i, i ^ bits) for i in range(n)])]
    pallas_call x1 -> x2, Pallas kernels: 2.63 us -> 2.28 us  [the longest x1 2.08 us: pack_call(): pl.pallas_call(pack_kernel, grid=(1,), in_specs=[smem(), resident(b), res...]
  transfers between devices with their start and end apart: 20 -> 23, of which waited for: 7 -> 9; matrix products, arithmetic and copies ran while one was open for 5% -> 5% of each run, Pallas kernels for 30% -> 27%
where the time goes in v4:
time: 78.7 us; the launch traced here: 78.5 us
  Pallas kernels  27.2 us (35%)
  starting transfers between devices  23.3 us (30%)
  waiting for transfers between devices  15.7 us (20%)
  local copies, waits for them, and re-layouts  6.13 us (8%)
  other arithmetic  4.54 us (6%)
  between operations  1.53 us (2%)
    ppermute x20, starting transfers between devices, swap(): return lax.ppermute(v, axis, [(i, i ^ bits) for i in range(n)])  18.7 us
    ppermute x20, waiting for transfers between devices, swap(): return lax.ppermute(v, axis, [(i, i ^ bits) for i in range(n)])  15.7 us
    pallas_call x1, Pallas kernels, acts_call(): pl.pallas_call(functools.partial(acts_kernel, parts, parts - len(cots)),...  7.18 us
    unnamed x44, local copies, waits for them, and re-layouts  6.11 us
    pallas_call x1, Pallas kernels, base_call(): pl.pallas_call(functools.partial(base_kernel, parts), grid=(width // blk,...  5.52 us
    ppermute x3, starting transfers between devices, onward(): return lax.ppermute(v, 'tensor', ring_pairs)  4.59 us
    pallas_call x2, Pallas kernels, down_call(): pl.pallas_call(functools.partial(down_kernel, ranks, first), grid=(width...  4.19 us
    pallas_call x1, Pallas kernels, hidden_call(): pl.pallas_call(functools.partial(hidden_kernel, order, groups), grid=(tok...  4.18 us
  transfers between devices with their start and end apart: 23, of which 9 were waited for; matrix products, arithmetic and copies ran while one was open for 5% of the time, Pallas kernels for 27%

profile of v4, /device:TPU:0, one launch (start us, length us, event | category | flops | bytes accessed | tf_op | source)
XLA Modules:
  0.0 78.5 jit_solution(2795233521472244910)
XLA Ops:
  0.6 2.1 %pack.1 = (bf16[32,1024]{1,0:T(8,128)(2,1)}, bf16[768,256]{1,0:T(8,128)(2,1)}, bf16[4,256,256]{2,1,0:T(8,128)(2,1)S(1)}) custom-call(s32[16]{0:T(128)} %live_ref.13, f32[1,32,1024]{2,1,0:T(8,128)} %b_ref.1, bf16[1024,256]{1,0:T(8,128)(2,1)} %cot_ref.1), custom_call_target="tpu_custom_call" | custom-call | bytes 1245184 | tf_op jit(solution)/shard_map/pack/pallas_call | solution.py:177
  2.7 3.0 %collective-permute-start.3 = (bf16[768,256]{1,0:T(8,128)(2,1)}, bf16[768,256]{1,0:T(8,128)(2,1)S(1)}, u32[]{:S(2)}, u32[]{:S(2)}) collective-permute-start(bf16[768,256]{1,0:T(8,128)(2,1)} %get-tuple-element.64.refs_0_.refs_7_.refs_3_), channel_id=1, source_target_pairs={{0,1},{1,3},{3,2},{2,0},{4,5},{5,7},{7,6},{6,4},{8,9},{9,11},{11,1... | collective-permute-start | bytes 1179656 | tf_op jit(solution)/shard_map/ppermute | solution.py:620
  5.7 1.2 %copy-done.3 = f32[1,2048,128]{2,1,0:T(8,128)S(1)} copy-done((f32[1,2048,128]{2,1,0:T(8,128)S(1)}, f32[1,2048,128]{2,1,0:T(8,128)}, u32[]{:S(2)}) %copy-start.3) | copy-done | bytes 1048600
  7.2 1.6 %collective-permute-start.6 = (bf16[64,2048]{1,0:T(8,128)(2,1)S(1)}, bf16[64,2048]{1,0:T(8,128)(2,1)S(1)}, u32[]{:S(2)}, u32[]{:S(2)}) collective-permute-start(bf16[64,2048]{1,0:T(8,128)(2,1)S(1)} %get-tuple-element.70.refs_4_.refs_1_), channel_id=1, source_target_pairs={{0,8},{4,12},{8,0},{12,4},{1,9},{5,13},{9,1},{13,5},{2,10},{6,14},... | collective-permute-start | bytes 786440 | tf_op jit(solution)/shard_map/ppermute | solution.py:57
  9.3 2.6 %collective-permute-start.4 = (bf16[32,1024]{1,0:T(8,128)(2,1)}, bf16[32,1024]{1,0:T(8,128)(2,1)S(1)}, u32[]{:S(2)}, u32[]{:S(2)}) collective-permute-start(bf16[32,1024]{1,0:T(8,128)(2,1)} %get-tuple-element.86.refs_0_), channel_id=1, source_target_pairs={{0,1},{1,0},{2,3},{3,2},{4,5},{5,4},{6,7},{7,6},{8,9},{9,8},{10,11... | collective-permute-start | bytes 196616 | tf_op jit(solution)/shard_map/ppermute | solution.py:57
  11.9 1.3 %reduce_sum.9 = s32[]{:T(128)} reduce(s32[16]{0:T(128)} %live_ref.13, s32[]{:T(128)} %constant.13.clone.1), dimensions={0}, to_apply=%region_0.0 | reduce | flops 15 | bytes 72 | tf_op jit(solution)/shard_map/reduce_sum | solution.py:639
  13.8 3.6 %collective-permute-done.4.refs_1_ = bf16[32,1024]{1,0:T(8,128)(2,1)S(1)} collective-permute-done((bf16[32,1024]{1,0:T(8,128)(2,1)}, bf16[32,1024]{1,0:T(8,128)(2,1)S(1)}, u32[]{:S(2)}, u32[]{:S(2)}) %collective-permute-start.4) | collective-permute-done | bytes 65568 | tf_op jit(solution)/shard_map/ppermute | solution.py:57
  17.5 0.7 collective-permute-start.5
  18.7 1.9 %collective-permute-done.7.refs_7_.refs_4_ = bf16[64,2048]{1,0:T(8,128)(2,1)S(1)} collective-permute-done((bf16[64,2048]{1,0:T(8,128)(2,1)S(1)}, bf16[64,2048]{1,0:T(8,128)(2,1)S(1)}, u32[]{:S(2)}, u32[]{:S(2)}) %collective-permute-start.7) | collective-permute-done | bytes 262176 | tf_op jit(solution)/shard_map/ppermute | solution.py:57
  20.6 1.3 %collective-permute-start.12 = (bf16[32,1024]{1,0:T(8,128)(2,1)}, bf16[32,1024]{1,0:T(8,128)(2,1)S(1)}, u32[]{:S(2)}, u32[]{:S(2)}) collective-permute-start(bf16[32,1024]{1,0:T(8,128)(2,1)} %get-tuple-element.86.refs_0_), channel_id=1, source_target_pairs={{0,2},{1,3},{2,0},{3,1},{4,6},{5,7},{6,4},{7,5},{8,10},{9,11},{10,... | collective-permute-start | bytes 196616 | tf_op jit(solution)/shard_map/ppermute | solution.py:57
  21.9 1.6 %collective-permute-start.13 = (bf16[32,1024]{1,0:T(8,128)(2,1)S(1)}, bf16[32,1024]{1,0:T(8,128)(2,1)S(1)}, u32[]{:S(2)}, u32[]{:S(2)}) collective-permute-start(bf16[32,1024]{1,0:T(8,128)(2,1)S(1)} %collective-permute-done.4.refs_1_), channel_id=1, source_target_pairs={{0,2},{1,3},{2,0},{3,1},{4,6},{5,7},{6,4},{7,5},{8,10},{9,11},{10,... | collective-permute-start | bytes 196616 | tf_op jit(solution)/shard_map/ppermute | solution.py:57
  23.6 2.2 %copy-done = bf16[1024,2048]{1,0:T(8,128)(2,1)S(1)} copy-done((bf16[1024,2048]{1,0:T(8,128)(2,1)S(1)}, bf16[1024,2048]{1,0:T(8,128)(2,1)}, u32[]{:S(2)}) %copy-start) | copy-done | bytes 4194328
  28.4 4.2 %hidden.1 = (bf16[32,1024]{1,0:T(8,128)(2,1)S(1)}, bf16[32,1024]{1,0:T(8,128)(2,1)S(1)}, bf16[32,1024]{1,0:T(8,128)(2,1)S(1)}, bf16[32,1024]{1,0:T(8,128)(2,1)S(1)}) custom-call(s32[1]{0:T(128)} %bitcast.5.d_ref, s32[1]{0:T(128)} %bitcast.4.z_ref, s32[16]{0:T(128)S(1)} %copy-done.7, s32[16]{0:T(128)S(1)} %copy-done.9, s32[4]{0:T(128)S(1)} %copy-done.11, ...), custom_call_target="tpu_custom_call" | custom-call | bytes 4096 | tf_op jit(solution)/shard_map/hidden/pallas_call | solution.py:278
  32.6 1.7 %collective-permute-done.12.refs_2_ = bf16[32,1024]{1,0:T(8,128)(2,1)S(1)} collective-permute-done((bf16[32,1024]{1,0:T(8,128)(2,1)}, bf16[32,1024]{1,0:T(8,128)(2,1)S(1)}, u32[]{:S(2)}, u32[]{:S(2)}) %collective-permute-start.12) | collective-permute-done | bytes 65568 | tf_op jit(solution)/shard_map/ppermute | solution.py:57
  34.3 0.7 collective-permute-done.13.refs_3_
  35.0 0.8 %collective-permute-start.14 = (bf16[768,256]{1,0:T(8,128)(2,1)S(1)}, bf16[768,256]{1,0:T(8,128)(2,1)S(1)}, u32[]{:S(2)}, u32[]{:S(2)}) collective-permute-start(bf16[768,256]{1,0:T(8,128)(2,1)S(1)} %collective-permute-done.5.refs_2_.refs_9_.refs_5_), channel_id=1, source_target_pairs={{0,1},{1,3},{3,2},{2,0},{4,5},{5,7},{7,6},{6,4},{8,9},{9,11},{11,1... | collective-permute-start | bytes 1179656 | tf_op jit(solution)/shard_map/ppermute | solution.py:620
  35.9 0.7 ordered.1.refs_8_
  36.6 1.6 %collective-permute-start.18 = (bf16[144,1024]{1,0:T(8,128)(2,1)S(1)}, bf16[144,1024]{1,0:T(8,128)(2,1)S(1)}, u32[]{:S(2)}, u32[]{:S(2)}) collective-permute-start(bf16[144,1024]{1,0:T(8,128)(2,1)S(1)} %ordered.1.refs_8_), channel_id=1, source_target_pairs={{0,8},{4,12},{8,0},{12,4},{1,9},{5,13},{9,1},{13,5},{2,10},{6,14},... | collective-permute-start | bytes 884744 | tf_op jit(solution)/shard_map/ppermute | solution.py:57
  38.2 3.4 %collective-permute-start.15 = (bf16[32,1024]{1,0:T(8,128)(2,1)S(1)}, bf16[32,1024]{1,0:T(8,128)(2,1)S(1)}, u32[]{:S(2)}, u32[]{:S(2)}) collective-permute-start(bf16[32,1024]{1,0:T(8,128)(2,1)S(1)} %get-tuple-element.83), channel_id=1, source_target_pairs={{0,1},{1,0},{2,3},{3,2},{4,5},{5,4},{6,7},{7,6},{8,9},{9,8},{10,11... | collective-permute-start | bytes 196616 | tf_op jit(solution)/shard_map/ppermute | solution.py:57
  41.6 2.3 %collective-permute-start.17 = (bf16[32,1024]{1,0:T(8,128)(2,1)S(1)}, bf16[32,1024]{1,0:T(8,128)(2,1)S(1)}, u32[]{:S(2)}, u32[]{:S(2)}) collective-permute-start(bf16[32,1024]{1,0:T(8,128)(2,1)S(1)} %get-tuple-element.85), channel_id=1, source_target_pairs={{0,3},{1,2},{2,1},{3,0},{4,7},{5,6},{6,5},{7,4},{8,11},{9,10},{10,... | collective-permute-start | bytes 196616 | tf_op jit(solution)/shard_map/ppermute | solution.py:57
  43.9 5.5 %base.1.base_ref = f32[768,2048]{1,0:T(8,128)S(1)} custom-call(s32[1]{0:T(128)} %bitcast.4.z_ref, s32[16]{0:T(128)S(1)} %copy-done.7, bf16[2048,1024]{1,0:T(8,128)(2,1)S(1)} %copy-done.2, bf16[768,256]{1,0:T(8,128)(2,1)S(1)} %copy-done.5, bf16[768,256]{1,0:T(8,128)(2,1)S(1)} %collective-permute-done.3.refs_1_.refs_8_.refs_4_, ...), custom_call_target="tpu_custom_call" | custom-call | flops 2415919104 | bytes 6291456 | tf_op jit(solution)/shard_map/base/pallas_call | solution.py:498
  49.6 1.9 %collective-permute-done.17.refs_6_ = bf16[32,1024]{1,0:T(8,128)(2,1)S(1)} collective-permute-done((bf16[32,1024]{1,0:T(8,128)(2,1)S(1)}, bf16[32,1024]{1,0:T(8,128)(2,1)S(1)}, u32[]{:S(2)}, u32[]{:S(2)}) %collective-permute-start.17) | collective-permute-done | bytes 65568 | tf_op jit(solution)/shard_map/ppermute | solution.py:57
  52.0 1.0 %up_grad.1 = (bf16[2,32,1024]{2,1,0:T(8,128)(2,1)S(1)}, bf16[2,32,1024]{2,1,0:T(8,128)(2,1)S(1)}) custom-call(s32[1]{0:T(128)} %bitcast.5.d_ref, s32[1]{0:T(128)} %bitcast.4.z_ref, s32[16]{0:T(128)S(1)} %copy-done.7, s32[16]{0:T(128)S(1)} %copy-done.10, s32[4]{0:T(128)S(1)} %copy-done.12, s32[4]{0:T(128)S(1)} %copy-done.14, ...), custom_call_target="tpu_custom_call" | custom-call | flops 268435456 | bytes 4194304 | tf_op jit(solution)/shard_map/up_grad/pallas_call | solution.py:438
  53.5 2.1 %upward.1 = (bf16[1024,512]{1,0:T(8,128)(2,1)S(1)}, bf16[1024,512]{1,0:T(8,128)(2,1)S(1)}, f32[8,1024]{1,0:T(8,128)S(1)}) custom-call(s32[1]{0:T(128)} %bitcast.5.d_ref, s32[1]{0:T(128)} %bitcast.4.z_ref, s32[16]{0:T(128)S(1)} %copy-done.7, s32[16]{0:T(128)S(1)} %copy-done.10, s32[4]{0:T(128)S(1)} %copy-done.12, s32[4]{0:T(128)S(1)} %copy-done.14, ...), custom_call_target="tpu_custom_call" | custom-call | flops 1073741824 | bytes 4194304 | tf_op jit(solution)/shard_map/upward/pallas_call | solution.py:353
  55.6 2.1 %down_grad.2 = (bf16[1,2048,128]{2,1,0:T(8,128)(2,1)S(1)}, bf16[1,2048,128]{2,1,0:T(8,128)(2,1)S(1)}) custom-call(bf16[1024,2048]{1,0:T(8,128)(2,1)S(1)} %copy-done.1, bf16[1024,512]{1,0:T(8,128)(2,1)S(1)} %get-tuple-element.103.u_ref), custom_call_target="tpu_custom_call" | custom-call | bytes 4096 | tf_op jit(solution)/shard_map/down_grad/pallas_call | solution.py:382
  57.9 2.1 %down_grad.3 = (bf16[1,2048,128]{2,1,0:T(8,128)(2,1)S(1)}, bf16[1,2048,128]{2,1,0:T(8,128)(2,1)S(1)}) custom-call(bf16[1024,2048]{1,0:T(8,128)(2,1)S(1)} %copy-done.1, bf16[1024,512]{1,0:T(8,128)(2,1)S(1)} %get-tuple-element.103.u_ref), custom_call_target="tpu_custom_call" | custom-call | bytes 4096 | tf_op jit(solution)/shard_map/down_grad/pallas_call | solution.py:382
  60.6 1.6 %collective-permute-start.24 = (bf16[1,2048,128]{2,1,0:T(8,128)(2,1)S(1)}, bf16[1,2048,128]{2,1,0:T(8,128)(2,1)S(1)}, u32[]{:S(2)}, u32[]{:S(2)}) collective-permute-start(bf16[1,2048,128]{2,1,0:T(8,128)(2,1)S(1)} %add_convert_fusion), channel_id=1, source_target_pairs={{0,8},{4,12},{8,0},{12,4},{1,9},{5,13},{9,1},{13,5},{2,10},{6,14},... | collective-permute-start | bytes 1572872 | tf_op jit(solution)/shard_map/ppermute | solution.py:57
  62.2 1.3 %collective-permute-done.22 = bf16[2,32,1024]{2,1,0:T(8,128)(2,1)S(1)} collective-permute-done((bf16[2,32,1024]{2,1,0:T(8,128)(2,1)S(1)}, bf16[2,32,1024]{2,1,0:T(8,128)(2,1)S(1)}, u32[]{:S(2)}, u32[]{:S(2)}) %collective-permute-start.22) | collective-permute-done | bytes 131104 | tf_op jit(solution)/shard_map/ppermute | solution.py:57
  64.2 7.2 %grad_acts.1 = bf16[1024,2048]{1,0:T(8,128)(2,1)} custom-call(s32[1]{0:T(128)} %bitcast.4.z_ref, s32[16]{0:T(128)S(1)} %copy-done.8, bf16[2048,1024]{1,0:T(8,128)(2,1)S(1)} %copy-done.2, bf16[1024,512]{1,0:T(8,128)(2,1)S(1)} %get-tuple-element.110.u_ref, f32[768,2048]{1,0:T(8,128)S(1)} %base.1.base_ref, bf16[4,256,256]{2,1,0:T(8,128)(2,1)S(1)} %copy-done.16, ...), custom_call_target="tpu_custom_call" | custom-call | bytes 4096 | tf_op jit(solution)/shard_map/grad_acts/pallas_call | solution.py:560
  71.4 4.0 %collective-permute-done.24 = bf16[1,2048,128]{2,1,0:T(8,128)(2,1)S(1)} collective-permute-done((bf16[1,2048,128]{2,1,0:T(8,128)(2,1)S(1)}, bf16[1,2048,128]{2,1,0:T(8,128)(2,1)S(1)}, u32[]{:S(2)}, u32[]{:S(2)}) %collective-permute-start.24) | collective-permute-done | bytes 524320 | tf_op jit(solution)/shard_map/ppermute | solution.py:57
  75.4 2.3 %divide_subtract_fusion = (f32[1,2048,128]{2,1,0:T(8,128)}, f32[1,2048,128]{2,1,0:T(8,128)}, f32[1,2048,128]{2,1,0:T(8,128)}) fusion(f32[1,2048,128]{2,1,0:T(8,128)S(1)} %copy-done.4, f32[128]{0:T(128)S(1)} %slice_bitcast_fusion.1, bf16[1,2048,128]{2,1,0:T(8,128)(2,1)S(1)} %collective-permute-done.24, bf16[1,2048,128]{2,1,0:T(8,128)(2,1)S(1)} %collective-permute-done.21, ...), kind=kLoop, calls=%fused_computation.4 | loop fusion | flops 4718592 | bytes 7864832 | tf_op jit(solution)/shard_map/sub | solution.py:34
  77.7 0.8 %divide_subtract_fusion.1 = (f32[1,32,1024]{2,1,0:T(8,128)}, f32[1,32,1024]{2,1,0:T(8,128)}, f32[1,32,1024]{2,1,0:T(8,128)}) fusion(f32[1,32,1024]{2,1,0:T(8,128)S(1)} %copy-done.19, f32[1024]{0:T(1024)S(1)} %bitcast.13, bf16[1,32,1024]{2,1,0:T(8,128)(2,1)S(1)} %collective-permute-done.25, f32[2,32,1024]{2,1,0:T(8,128)S(1)} %convert_add_fusion, ...), kind=kLoop, calls=%fused_computation.14 | loop fusion | flops 491520 | bytes 987136 | tf_op jit(solution)/shard_map/sub | solution.py:34
  (77 shorter events, 6.5 us)
Async XLA Ops:
  2.7 14.8 %collective-permute-start.3 = (bf16[768,256]{1,0:T(8,128)(2,1)}, bf16[768,256]{1,0:T(8,128)(2,1)S(1)}, u32[]{:S(2)}, u32[]{:S(2)}) collective-permute-start(bf16[768,256]{1,0:T(8,128)(2,1)} %get-tuple-element.64.refs_0_.refs_7_.refs_3_), channel_id=1, source_target_pairs={{0,1},{1,3},{3,2},{2,0},{4,5},{5,7},{7,6},{6,4},{8,9},{9,11},{11,1... | collective-permute-start | bytes 1179656 | tf_op jit(solution)/shard_map/ppermute | solution.py:620
  7.0 28.9 %copy-start.6 = (bf16[32,1024]{1,0:T(8,128)(2,1)S(1)}, bf16[32,1024]{1,0:T(8,128)(2,1)}, u32[]{:S(2)}) copy-start(bf16[32,1024]{1,0:T(8,128)(2,1)} %get-tuple-element.86.refs_0_) | copy-start | bytes 196612
  7.0 28.9 %copy-start.10 = (s32[16]{0:T(128)S(1)}, s32[16]{0:T(128)}, u32[]{:S(2)}) copy-start(s32[16]{0:T(128)} %refs_0_.5) | copy-start | bytes 196
  7.0 28.9 %copy-start.12 = (s32[4]{0:T(128)S(1)}, s32[4]{0:T(128)}, u32[]{:S(2)}) copy-start(s32[4]{0:T(128)} %refs_1_.5) | copy-start | bytes 52
  7.2 36.7 %copy-start.5 = (bf16[768,256]{1,0:T(8,128)(2,1)S(1)}, bf16[768,256]{1,0:T(8,128)(2,1)}, u32[]{:S(2)}) copy-start(bf16[768,256]{1,0:T(8,128)(2,1)} %get-tuple-element.64.refs_0_.refs_7_.refs_3_) | copy-start | bytes 1179652
  7.2 11.5 %collective-permute-start.6 = (bf16[64,2048]{1,0:T(8,128)(2,1)S(1)}, bf16[64,2048]{1,0:T(8,128)(2,1)S(1)}, u32[]{:S(2)}, u32[]{:S(2)}) collective-permute-start(bf16[64,2048]{1,0:T(8,128)(2,1)S(1)} %get-tuple-element.70.refs_4_.refs_1_), channel_id=1, source_target_pairs={{0,8},{4,12},{8,0},{12,4},{1,9},{5,13},{9,1},{13,5},{2,10},{6,14},... | collective-permute-start | bytes 786440 | tf_op jit(solution)/shard_map/ppermute | solution.py:57
  8.7 11.9 %collective-permute-start.7 = (bf16[64,2048]{1,0:T(8,128)(2,1)S(1)}, bf16[64,2048]{1,0:T(8,128)(2,1)S(1)}, u32[]{:S(2)}, u32[]{:S(2)}) collective-permute-start(bf16[64,2048]{1,0:T(8,128)(2,1)S(1)} %get-tuple-element.72.refs_5_.refs_2_), channel_id=1, source_target_pairs={{0,8},{4,12},{8,0},{12,4},{1,9},{5,13},{9,1},{13,5},{2,10},{6,14},... | collective-permute-start | bytes 786440 | tf_op jit(solution)/shard_map/ppermute | solution.py:57
  9.3 8.2 %collective-permute-start.4 = (bf16[32,1024]{1,0:T(8,128)(2,1)}, bf16[32,1024]{1,0:T(8,128)(2,1)S(1)}, u32[]{:S(2)}, u32[]{:S(2)}) collective-permute-start(bf16[32,1024]{1,0:T(8,128)(2,1)} %get-tuple-element.86.refs_0_), channel_id=1, source_target_pairs={{0,1},{1,0},{2,3},{3,2},{4,5},{5,4},{6,7},{7,6},{8,9},{9,8},{10,11... | collective-permute-start | bytes 196616 | tf_op jit(solution)/shard_map/ppermute | solution.py:57
  17.5 17.6 %collective-permute-start.5 = (bf16[768,256]{1,0:T(8,128)(2,1)S(1)}, bf16[768,256]{1,0:T(8,128)(2,1)S(1)}, u32[]{:S(2)}, u32[]{:S(2)}) collective-permute-start(bf16[768,256]{1,0:T(8,128)(2,1)S(1)} %collective-permute-done.3.refs_1_.refs_8_.refs_4_), channel_id=1, source_target_pairs={{0,1},{1,3},{3,2},{2,0},{4,5},{5,7},{7,6},{6,4},{8,9},{9,11},{11,1... | collective-permute-start | bytes 1179656 | tf_op jit(solution)/shard_map/ppermute | solution.py:620
  18.2 2.4 %collective-permute-start.9 = (bf16[64,2048]{1,0:T(8,128)(2,1)S(1)}, bf16[64,2048]{1,0:T(8,128)(2,1)S(1)}, u32[]{:S(2)}, u32[]{:S(2)}) collective-permute-start(bf16[64,2048]{1,0:T(8,128)(2,1)S(1)} %get-tuple-element.72.refs_5_.refs_2_), channel_id=1, source_target_pairs={{0,4},{4,0},{8,12},{12,8},{1,5},{5,1},{9,13},{13,9},{2,6},{6,2},{1... | collective-permute-start | bytes 786440 | tf_op jit(solution)/shard_map/ppermute | solution.py:57
  18.2 3.7 %collective-permute-start.8 = (bf16[64,2048]{1,0:T(8,128)(2,1)S(1)}, bf16[64,2048]{1,0:T(8,128)(2,1)S(1)}, u32[]{:S(2)}, u32[]{:S(2)}) collective-permute-start(bf16[64,2048]{1,0:T(8,128)(2,1)S(1)} %get-tuple-element.70.refs_4_.refs_1_), channel_id=1, source_target_pairs={{0,4},{4,0},{8,12},{12,8},{1,5},{5,1},{9,13},{13,9},{2,6},{6,2},{1... | collective-permute-start | bytes 786440 | tf_op jit(solution)/shard_map/ppermute | solution.py:57
  18.7 4.9 %collective-permute-start.10 = (bf16[64,2048]{1,0:T(8,128)(2,1)S(1)}, bf16[64,2048]{1,0:T(8,128)(2,1)S(1)}, u32[]{:S(2)}, u32[]{:S(2)}) collective-permute-start(bf16[64,2048]{1,0:T(8,128)(2,1)S(1)} %collective-permute-done.6.refs_6_.refs_3_), channel_id=1, source_target_pairs={{0,4},{4,0},{8,12},{12,8},{1,5},{5,1},{9,13},{13,9},{2,6},{6,2},{1... | collective-permute-start | bytes 786440 | tf_op jit(solution)/shard_map/ppermute | solution.py:57
  20.6 2.9 %collective-permute-start.11 = (bf16[64,2048]{1,0:T(8,128)(2,1)S(1)}, bf16[64,2048]{1,0:T(8,128)(2,1)S(1)}, u32[]{:S(2)}, u32[]{:S(2)}) collective-permute-start(bf16[64,2048]{1,0:T(8,128)(2,1)S(1)} %collective-permute-done.7.refs_7_.refs_4_), channel_id=1, source_target_pairs={{0,4},{4,0},{8,12},{12,8},{1,5},{5,1},{9,13},{13,9},{2,6},{6,2},{1... | collective-permute-start | bytes 786440 | tf_op jit(solution)/shard_map/ppermute | solution.py:57
  20.6 13.7 %collective-permute-start.12 = (bf16[32,1024]{1,0:T(8,128)(2,1)}, bf16[32,1024]{1,0:T(8,128)(2,1)S(1)}, u32[]{:S(2)}, u32[]{:S(2)}) collective-permute-start(bf16[32,1024]{1,0:T(8,128)(2,1)} %get-tuple-element.86.refs_0_), channel_id=1, source_target_pairs={{0,2},{1,3},{2,0},{3,1},{4,6},{5,7},{6,4},{7,5},{8,10},{9,11},{10,... | collective-permute-start | bytes 196616 | tf_op jit(solution)/shard_map/ppermute | solution.py:57
  21.9 13.1 %collective-permute-start.13 = (bf16[32,1024]{1,0:T(8,128)(2,1)S(1)}, bf16[32,1024]{1,0:T(8,128)(2,1)S(1)}, u32[]{:S(2)}, u32[]{:S(2)}) collective-permute-start(bf16[32,1024]{1,0:T(8,128)(2,1)S(1)} %collective-permute-done.4.refs_1_), channel_id=1, source_target_pairs={{0,2},{1,3},{2,0},{3,1},{4,6},{5,7},{6,4},{7,5},{8,10},{9,11},{10,... | collective-permute-start | bytes 196616 | tf_op jit(solution)/shard_map/ppermute | solution.py:57
  28.4 15.5 %copy-start.2 = (bf16[2048,1024]{1,0:T(8,128)(2,1)S(1)}, bf16[2048,1024]{1,0:T(8,128)(2,1)}, u32[]{:S(2)}) copy-start(bf16[2048,1024]{1,0:T(8,128)(2,1)} %w_ref.3) | copy-start | bytes 12582916
  35.0 16.4 %collective-permute-start.14 = (bf16[768,256]{1,0:T(8,128)(2,1)S(1)}, bf16[768,256]{1,0:T(8,128)(2,1)S(1)}, u32[]{:S(2)}, u32[]{:S(2)}) collective-permute-start(bf16[768,256]{1,0:T(8,128)(2,1)S(1)} %collective-permute-done.5.refs_2_.refs_9_.refs_5_), channel_id=1, source_target_pairs={{0,1},{1,3},{3,2},{2,0},{4,5},{5,7},{7,6},{6,4},{8,9},{9,11},{11,1... | collective-permute-start | bytes 1179656 | tf_op jit(solution)/shard_map/ppermute | solution.py:620
  36.6 15.4 %copy-start.14 = (s32[4]{0:T(128)S(1)}, s32[4]{0:T(128)}, u32[]{:S(2)}) copy-start(s32[4]{0:T(128)} %refs_2_.5) | copy-start | bytes 52
  36.6 15.4 %copy-start.16 = (bf16[4,256,256]{2,1,0:T(8,128)(2,1)S(1)}, bf16[4,256,256]{2,1,0:T(8,128)(2,1)}, u32[]{:S(2)}) copy-start(bf16[4,256,256]{2,1,0:T(8,128)(2,1)} %copy-done.15) | copy-start | bytes 1572868
  36.6 14.9 %collective-permute-start.18 = (bf16[144,1024]{1,0:T(8,128)(2,1)S(1)}, bf16[144,1024]{1,0:T(8,128)(2,1)S(1)}, u32[]{:S(2)}, u32[]{:S(2)}) collective-permute-start(bf16[144,1024]{1,0:T(8,128)(2,1)S(1)} %ordered.1.refs_8_), channel_id=1, source_target_pairs={{0,8},{4,12},{8,0},{12,4},{1,9},{5,13},{9,1},{13,5},{2,10},{6,14},... | collective-permute-start | bytes 884744 | tf_op jit(solution)/shard_map/ppermute | solution.py:57
  38.2 11.3 %collective-permute-start.15 = (bf16[32,1024]{1,0:T(8,128)(2,1)S(1)}, bf16[32,1024]{1,0:T(8,128)(2,1)S(1)}, u32[]{:S(2)}, u32[]{:S(2)}) collective-permute-start(bf16[32,1024]{1,0:T(8,128)(2,1)S(1)} %get-tuple-element.83), channel_id=1, source_target_pairs={{0,1},{1,0},{2,3},{3,2},{4,5},{5,4},{6,7},{7,6},{8,9},{9,8},{10,11... | collective-permute-start | bytes 196616 | tf_op jit(solution)/shard_map/ppermute | solution.py:57
  41.5 8.0 %collective-permute-start.16 = (bf16[32,1024]{1,0:T(8,128)(2,1)S(1)}, bf16[32,1024]{1,0:T(8,128)(2,1)S(1)}, u32[]{:S(2)}, u32[]{:S(2)}) collective-permute-start(bf16[32,1024]{1,0:T(8,128)(2,1)S(1)} %get-tuple-element.84), channel_id=1, source_target_pairs={{0,2},{1,3},{2,0},{3,1},{4,6},{5,7},{6,4},{7,5},{8,10},{9,11},{10,... | collective-permute-start | bytes 196616 | tf_op jit(solution)/shard_map/ppermute | solution.py:57
  41.6 9.9 %collective-permute-start.17 = (bf16[32,1024]{1,0:T(8,128)(2,1)S(1)}, bf16[32,1024]{1,0:T(8,128)(2,1)S(1)}, u32[]{:S(2)}, u32[]{:S(2)}) collective-permute-start(bf16[32,1024]{1,0:T(8,128)(2,1)S(1)} %get-tuple-element.85), channel_id=1, source_target_pairs={{0,3},{1,2},{2,1},{3,0},{4,7},{5,6},{6,5},{7,4},{8,11},{9,10},{10,... | collective-permute-start | bytes 196616 | tf_op jit(solution)/shard_map/ppermute | solution.py:57
  51.5 1.6 %collective-permute-start.19 = (bf16[144,1024]{1,0:T(8,128)(2,1)S(1)}, bf16[144,1024]{1,0:T(8,128)(2,1)S(1)}, u32[]{:S(2)}, u32[]{:S(2)}) collective-permute-start(bf16[144,1024]{1,0:T(8,128)(2,1)S(1)} %ordered.1.refs_8_), channel_id=1, source_target_pairs={{0,4},{4,0},{8,12},{12,8},{1,5},{5,1},{9,13},{13,9},{2,6},{6,2},{1... | collective-permute-start | bytes 884744 | tf_op jit(solution)/shard_map/ppermute | solution.py:57
  51.5 2.0 %collective-permute-start.20 = (bf16[144,1024]{1,0:T(8,128)(2,1)S(1)}, bf16[144,1024]{1,0:T(8,128)(2,1)S(1)}, u32[]{:S(2)}, u32[]{:S(2)}) collective-permute-start(bf16[144,1024]{1,0:T(8,128)(2,1)S(1)} %collective-permute-done.18.refs_9_), channel_id=1, source_target_pairs={{0,4},{4,0},{8,12},{12,8},{1,5},{5,1},{9,13},{13,9},{2,6},{6,2},{1... | collective-permute-start | bytes 884744 | tf_op jit(solution)/shard_map/ppermute | solution.py:57
  57.7 2.8 %collective-permute-start.23 = (bf16[1,2048,128]{2,1,0:T(8,128)(2,1)S(1)}, bf16[1,2048,128]{2,1,0:T(8,128)(2,1)S(1)}, u32[]{:S(2)}, u32[]{:S(2)}) collective-permute-start(bf16[1,2048,128]{2,1,0:T(8,128)(2,1)S(1)} %get-tuple-element.102), channel_id=1, source_target_pairs={{0,4},{4,0},{8,12},{12,8},{1,5},{5,1},{9,13},{13,9},{2,6},{6,2},{1... | collective-permute-start | bytes 1572872 | tf_op jit(solution)/shard_map/ppermute | solution.py:57
  60.0 3.5 %collective-permute-start.21 = (bf16[1,2048,128]{2,1,0:T(8,128)(2,1)S(1)}, bf16[1,2048,128]{2,1,0:T(8,128)(2,1)S(1)}, u32[]{:S(2)}, u32[]{:S(2)}) collective-permute-start(bf16[1,2048,128]{2,1,0:T(8,128)(2,1)S(1)} %get-tuple-element.104), channel_id=1, source_target_pairs={{0,4},{4,0},{8,12},{12,8},{1,5},{5,1},{9,13},{13,9},{2,6},{6,2},{1... | collective-permute-start | bytes 1572872 | tf_op jit(solution)/shard_map/ppermute | solution.py:57
  60.6 14.7 %collective-permute-start.24 = (bf16[1,2048,128]{2,1,0:T(8,128)(2,1)S(1)}, bf16[1,2048,128]{2,1,0:T(8,128)(2,1)S(1)}, u32[]{:S(2)}, u32[]{:S(2)}) collective-permute-start(bf16[1,2048,128]{2,1,0:T(8,128)(2,1)S(1)} %add_convert_fusion), channel_id=1, source_target_pairs={{0,8},{4,12},{8,0},{12,4},{1,9},{5,13},{9,1},{13,5},{2,10},{6,14},... | collective-permute-start | bytes 1572872 | tf_op jit(solution)/shard_map/ppermute | solution.py:57
  62.2 1.3 %collective-permute-start.22 = (bf16[2,32,1024]{2,1,0:T(8,128)(2,1)S(1)}, bf16[2,32,1024]{2,1,0:T(8,128)(2,1)S(1)}, u32[]{:S(2)}, u32[]{:S(2)}) collective-permute-start(bf16[2,32,1024]{2,1,0:T(8,128)(2,1)S(1)} %get-tuple-element.96), channel_id=1, source_target_pairs={{0,4},{4,0},{8,12},{12,8},{1,5},{5,1},{9,13},{13,9},{2,6},{6,2},{1... | collective-permute-start | bytes 393224 | tf_op jit(solution)/shard_map/ppermute | solution.py:57
  63.6 11.8 %copy-start.4 = (f32[1,2048,128]{2,1,0:T(8,128)S(1)}, f32[1,2048,128]{2,1,0:T(8,128)}, u32[]{:S(2)}) copy-start(f32[1,2048,128]{2,1,0:T(8,128)} %a_ref) | copy-start | bytes 3145732
  63.6 11.8 %copy-start.17 = (f32[1,2048,128]{2,1,0:T(8,128)S(1)}, f32[1,2048,128]{2,1,0:T(8,128)}, u32[]{:S(2)}) copy-start(f32[1,2048,128]{2,1,0:T(8,128)} %param.20) | copy-start | bytes 3145732
  63.6 14.0 %collective-permute-start.25 = (bf16[1,32,1024]{2,1,0:T(8,128)(2,1)S(1)}, bf16[1,32,1024]{2,1,0:T(8,128)(2,1)S(1)}, u32[]{:S(2)}, u32[]{:S(2)}) collective-permute-start(bf16[1,32,1024]{2,1,0:T(8,128)(2,1)S(1)} %slice.32), channel_id=1, source_target_pairs={{0,8},{4,12},{8,0},{12,4},{1,9},{5,13},{9,1},{13,5},{2,10},{6,14},... | collective-permute-start | bytes 196616 | tf_op jit(solution)/shard_map/ppermute | solution.py:57
  (13 other events, 52.9 us)
